TPU v7x, 32 devices: a whole 2x2x4 slice. The times are simulated.
32 devices in a mesh: src: 4 (over y, x), tgt: 8 (over z, core).
Axes of the slice: x: 2, y: 2, z: 4, core: 2. Of those that a mesh axis runs over, the one named last changes fastest.
Arguments:
- source_points: float32 [32, 4096], P(None, 'src'), may hold values from -12 to 12
- target_points: float32 [32, 32768], P('src', 'tgt'), may hold values from -12 to 12
- g_init: float32 [32768], P('tgt'), may hold values from -6 to 6
Outputs:
- source_potential: float32 [4096], P('src')
- target_potential: float32 [32768], P('tgt')
- row_marginal: float32 [4096], P('src')
All inputs are finite; a program needn't handle non-finite values.
Results may differ from a plain program's by a relative error of at most 0.0003.
Values sent between devices are 32-bit elements; how exact they have to be, the bound alone decides.
No kernel may reach another device: no remote copies, remote signals or barrier semaphores. Data moves between devices by JAX's collectives and lax.ppermute only.
A program may use at most 64 MiB of HBM per device.

v0:
```python
import math

import jax
import jax.numpy as jnp
from jax import lax
from jax.sharding import PartitionSpec as P

ITERS = 2


epsilon = 0.05


def body(source_points, target_points, g_init):
    target_block = lax.all_gather(target_points, "src", axis=0, tiled=True)
    rows = source_points.shape[1]
    width = min(rows, 64)
    count = rows // width
    dims = source_points.shape[0]
    n_tgt = lax.axis_size("tgt")
    log_nt = math.log(target_block.shape[1] * n_tgt)
    log_ns = math.log(rows * lax.axis_size("src"))
    blocks = source_points.T.reshape(count, width, dims)
    target_sq = jnp.sum(target_block * target_block, axis=0)

    def cost_block(rows_block):
        rows_sq = jnp.sum(rows_block * rows_block, axis=1)
        cross = jnp.dot(
            rows_block,
            target_block,
            precision=lax.Precision.HIGHEST,
            preferred_element_type=jnp.float32,
        )
        return rows_sq[:, None] + target_sq[None, :] - 2.0 * cross

    g_pot = g_init
    f_pot = jnp.zeros((rows,), jnp.float32)
    for step in range(ITERS):

        def row_pass(carry, rows_block):
            scores = (g_pot[None, :] - cost_block(rows_block)) / epsilon
            top = jnp.max(scores, axis=1)
            return (carry, (top, jnp.sum(jnp.exp(scores - top[:, None]), axis=1)))

        _, (row_top, row_sum) = lax.scan(row_pass, 0.0, blocks)
        row_top = row_top.reshape(rows)
        row_sum = row_sum.reshape(rows)
        whole_top = lax.pmax(row_top, "tgt")
        whole_sum = lax.psum(row_sum * jnp.exp(row_top - whole_top), "tgt")
        f_pot = -epsilon * (whole_top + jnp.log(whole_sum) - log_nt)

        def column_pass(carry, packed):
            rows_block, f_block = packed
            scores = (f_block[:, None] - cost_block(rows_block)) / epsilon
            top = jnp.maximum(carry[0], jnp.max(scores, axis=0))
            total = carry[1] * jnp.exp(carry[0] - top) + jnp.sum(
                jnp.exp(scores - top[None, :]), axis=0
            )
            return ((top, total), None)

        columns = target_block.shape[1]
        start = (jnp.full((columns,), -jnp.inf, jnp.float32), jnp.zeros((columns,), jnp.float32))
        (col_top, col_sum), _ = lax.scan(column_pass, start, (blocks, f_pot.reshape(count, width)))
        whole_top = lax.pmax(col_top, "src")
        whole_sum = lax.psum(col_sum * jnp.exp(col_top - whole_top), "src")
        g_pot = -epsilon * (whole_top + jnp.log(whole_sum) - log_ns)

    def marginal_pass(carry, packed):
        rows_block, f_block = packed
        scores = (f_block[:, None] + g_pot[None, :] - cost_block(rows_block)) / epsilon
        return (carry, jnp.sum(jnp.exp(scores), axis=1))

    _, partial_rows = lax.scan(marginal_pass, 0.0, (blocks, f_pot.reshape(count, width)))
    marginal = lax.psum(partial_rows.reshape(rows), "tgt")
    return (f_pot, g_pot, marginal / (target_block.shape[1] * n_tgt))


def solution(mesh):
    in_specs = (P(None, "src"), P("src", "tgt"), P("tgt"))
    out_specs = (P("src"), P("tgt"), P("src"))
    return jax.shard_map(body, mesh=mesh, in_specs=in_specs, out_specs=out_specs, check_vma=False)
```

profile of v0, /device:TPU:0, one launch (start us, length us, event | category | flops | bytes accessed | tf_op | source)
XLA Modules:
  0.0 273.4 jit_solution(14333866755377849148)
XLA Ops:
  0.6 11.8 %all_gather.3 = f32[32,4096]{1,0:T(8,128)S(1)} all-gather(f32[8,4096]{1,0:T(8,128)} %param.14), channel_id=1, replica_groups=mesh['src'=4,'tgt'=8] {'src'}, dimensions={0}, use_global_device_ids=true | all-gather | bytes 655360 | tf_op jit(solution)/shard_map/all_gather | solution.py:15
  14.3 28.0 %while.60 = (s32[]{:T(128)}, f32[16,64]{1,0:T(8,128)S(1)}, f32[16,64]{1,0:T(8,128)S(1)}, f32[4096]{0:T(1024)S(1)}, f32[16,64,32]{2,1,0:T(8,128)S(1)}, /*index=5*...) while((s32[]{:T(128)}, f32[16,64]{1,0:T(8,128)S(1)}, f32[16,64]{1,0:T(8,128)S(1)}, ...), condition=%wide.region_5.6_spmd, body=%wide.region_1.5_spmd.sunk | while | flops 102764352 | bytes 2697837 | solution.py:45
  14.4 1.2 fusion.68
  16.2 1.2 fusion.68
  17.9 1.2 fusion.68
  19.7 1.2 fusion.68
  21.4 1.2 fusion.68
  23.2 1.2 fusion.68
  24.9 1.2 fusion.68
  26.7 1.2 fusion.68
  28.4 1.2 fusion.68
  30.2 1.2 fusion.68
  31.9 1.2 fusion.68
  33.7 1.2 fusion.68
  35.4 1.2 fusion.68
  37.2 1.2 fusion.68
  38.9 1.2 fusion.68
  40.7 1.2 fusion.68
  42.4 15.2 %pmax.28 = f32[1024]{0:T(1024)S(1)} all-reduce(f32[1024]{0:T(1024)S(1)} %reshape.55), channel_id=1, replica_groups=mesh['src'=4,'tgt'=8] {'tgt'}, use_global_device_ids=true, to_apply=%region_6.7 | all-reduce | flops 1024 | bytes 8192 | tf_op jit(solution)/shard_map/pmax | solution.py:48
  57.6 13.6 %psum.35 = f32[1024]{0:T(1024)S(1)} all-reduce(f32[1024]{0:T(1024)S(1)} %exponential_multiply_fusion.3), channel_id=1, replica_groups=mesh['src'=4,'tgt'=8] {'tgt'}, use_global_device_ids=true, to_apply=%region_7.8 | all-reduce | flops 1024 | bytes 8192 | tf_op jit(solution)/shard_map/psum | solution.py:49
  71.3 24.4 %while.63 = (s32[]{:T(128)}, f32[4096]{0:T(1024)S(1)}, f32[4096]{0:T(1024)S(1)}, f32[16,64]{1,0:T(8,128)S(1)}, f32[16,64,32]{2,1,0:T(8,128)S(1)}, /*index=5*/f32...) while((s32[]{:T(128)}, f32[4096]{0:T(1024)S(1)}, f32[4096]{0:T(1024)S(1)}, ...), condition=%wide.region_12.13_spmd.clone, body=%wide.region_8.12_spmd.clone.sunk | while | flops 102784960 | bytes 2893684 | solution.py:63
  95.7 15.1 %pmax.29 = f32[4096]{0:T(1024)S(1)} all-reduce(f32[4096]{0:T(1024)S(1)} %get-tuple-element.194), channel_id=1, replica_groups=mesh['src'=4,'tgt'=8] {'src'}, use_global_device_ids=true, to_apply=%region_13.14 | all-reduce | flops 4096 | bytes 32768 | tf_op jit(solution)/shard_map/pmax | solution.py:64
  110.8 14.1 %psum.36 = f32[4096]{0:T(1024)S(1)} all-reduce(f32[4096]{0:T(1024)S(1)} %exponential_multiply_fusion.1), channel_id=1, replica_groups=mesh['src'=4,'tgt'=8] {'src'}, use_global_device_ids=true, to_apply=%region_14.15 | all-reduce | flops 4096 | bytes 32768 | tf_op jit(solution)/shard_map/psum | solution.py:65
  124.9 28.0 %while.61 = (s32[]{:T(128)}, f32[16,64]{1,0:T(8,128)S(1)}, f32[16,64]{1,0:T(8,128)S(1)}, f32[4096]{0:T(1024)S(1)}, f32[16,64,32]{2,1,0:T(8,128)S(1)}, /*index=5*...) while((s32[]{:T(128)}, f32[16,64]{1,0:T(8,128)S(1)}, f32[16,64]{1,0:T(8,128)S(1)}, ...), condition=%wide.region_19.20_spmd, body=%wide.region_15.19_spmd.sunk | while | flops 102764352 | bytes 2697837 | solution.py:45
  125.0 1.2 fusion.71
  126.8 1.2 fusion.71
  128.5 1.2 fusion.71
  130.3 1.2 fusion.71
  132.0 1.2 fusion.71
  133.8 1.2 fusion.71
  135.5 1.2 fusion.71
  137.3 1.2 fusion.71
  139.1 1.2 fusion.71
  140.8 1.2 fusion.71
  142.6 1.2 fusion.71
  144.3 1.2 fusion.71
  146.1 1.2 fusion.71
  147.8 1.2 fusion.71
  149.6 1.2 fusion.71
  151.3 1.2 fusion.71
  153.0 13.6 %pmax.30 = f32[1024]{0:T(1024)S(1)} all-reduce(f32[1024]{0:T(1024)S(1)} %reshape.58), channel_id=1, replica_groups=mesh['src'=4,'tgt'=8] {'tgt'}, use_global_device_ids=true, to_apply=%region_20.21 | all-reduce | flops 1024 | bytes 8192 | tf_op jit(solution)/shard_map/pmax | solution.py:48
  166.7 13.6 %psum.37 = f32[1024]{0:T(1024)S(1)} all-reduce(f32[1024]{0:T(1024)S(1)} %exponential_multiply_fusion.2), channel_id=1, replica_groups=mesh['src'=4,'tgt'=8] {'tgt'}, use_global_device_ids=true, to_apply=%region_21.22 | all-reduce | flops 1024 | bytes 8192 | tf_op jit(solution)/shard_map/psum | solution.py:49
  180.9 24.4 %while.64 = (s32[]{:T(128)}, f32[4096]{0:T(1024)S(1)}, f32[4096]{0:T(1024)S(1)}, f32[16,64]{1,0:T(8,128)S(1)}, f32[16,64,32]{2,1,0:T(8,128)S(1)}, /*index=5*/f32...) while((s32[]{:T(128)}, f32[4096]{0:T(1024)S(1)}, f32[4096]{0:T(1024)S(1)}, ...), condition=%wide.region_26.27_spmd.clone, body=%wide.region_22.26_spmd.clone.sunk | while | flops 102784960 | bytes 2893684 | solution.py:63
  187.1 1.2 fusion.82
  205.3 15.1 %pmax.31 = f32[4096]{0:T(1024)S(1)} all-reduce(f32[4096]{0:T(1024)S(1)} %get-tuple-element.198), channel_id=1, replica_groups=mesh['src'=4,'tgt'=8] {'src'}, use_global_device_ids=true, to_apply=%region_27.28 | all-reduce | flops 4096 | bytes 32768 | tf_op jit(solution)/shard_map/pmax | solution.py:64
  220.4 14.1 %psum.38 = f32[4096]{0:T(1024)S(1)} all-reduce(f32[4096]{0:T(1024)S(1)} %exponential_multiply_fusion), channel_id=1, replica_groups=mesh['src'=4,'tgt'=8] {'src'}, use_global_device_ids=true, to_apply=%region_28.29 | all-reduce | flops 4096 | bytes 32768 | tf_op jit(solution)/shard_map/psum | solution.py:65
  234.5 24.6 %while.62 = (s32[]{:T(128)}, f32[16,64]{1,0:T(8,128)S(1)}, f32[16,64]{1,0:T(8,128)S(1)}, f32[4096]{0:T(1024)S(1)}, f32[16,64,32]{2,1,0:T(8,128)S(1)}, /*index=5*...) while((s32[]{:T(128)}, f32[16,64]{1,0:T(8,128)S(1)}, f32[16,64]{1,0:T(8,128)S(1)}, ...), condition=%wide.region_32.33_spmd, body=%wide.region_29.32_spmd.sunk | while | flops 102502272 | bytes 600685 | solution.py:73
  234.6 1.4 fusion.75
  236.1 1.3 fusion.75
  237.7 1.3 fusion.75
  239.2 1.4 fusion.75
  240.8 1.4 fusion.75
  242.3 1.4 fusion.75
  243.8 1.4 fusion.75
  245.4 1.4 fusion.75
  246.9 1.4 fusion.75
  248.5 1.4 fusion.75
  250.0 1.4 fusion.75
  251.6 1.4 fusion.75
  253.1 1.4 fusion.75
  254.6 1.4 fusion.75
  256.2 1.4 fusion.75
  257.7 1.4 fusion.75
  259.2 13.6 %psum.39 = f32[1024]{0:T(1024)S(1)} all-reduce(f32[1024]{0:T(1024)S(1)} %reshape.61), channel_id=1, replica_groups=mesh['src'=4,'tgt'=8] {'tgt'}, use_global_device_ids=true, to_apply=%region_33.34 | all-reduce | flops 1024 | bytes 8192 | tf_op jit(solution)/shard_map/psum | solution.py:74
  (434 shorter events, 68.2 us)
Async XLA Ops:
  12.5 0.9 copy-start.1
  13.6 0.7 copy-start
  180.3 0.6 copy-start.3
  259.1 14.3 %copy-start.2 = (f32[4096]{0:T(1024)}, f32[4096]{0:T(1024)S(1)}, u32[]{:S(2)}) copy-start(f32[4096]{0:T(1024)S(1)} %get-tuple-element.705) | copy-start | bytes 49156
where the time goes:
time: 274 us; the launch traced here: 273 us
  blocking collectives  140 us (51%)
  matrix products  97.5 us (36%)
  other arithmetic  26.2 us (10%)
  local copies, waits for them, and re-layouts  6.34 us (2%)
  loops' own time  3.02 us (1%)
    dot_general x80, matrix products, cost_block(): jnp.dot(rows_block, target_block, precision=lax.Precision.HIGHEST, prefer...  97.5 us
    pmax x2, blocking collectives, body(): whole_top = lax.pmax(col_top, 'src')  30.1 us
    pmax x2, blocking collectives, body(): whole_top = lax.pmax(row_top, 'tgt')  28.7 us
    psum x2, blocking collectives, body(): whole_sum = lax.psum(col_sum * jnp.exp(col_top - whole_top), 'src')  28.1 us
    psum x2, blocking collectives, body(): whole_sum = lax.psum(row_sum * jnp.exp(row_top - whole_top), 'tgt')  27.2 us
    psum x1, blocking collectives, body(): marginal = lax.psum(partial_rows.reshape(rows), 'tgt')  13.6 us
    all_gather x1, blocking collectives, body(): target_block = lax.all_gather(target_points, 'src', axis=0, tiled=True)  11.8 us
    reduce_sum x32, other arithmetic, row_pass(): return (carry, (top, jnp.sum(jnp.exp(scores - top[:, None]), axis=1)))  10.6 us

commit v1 on v0

v1 whole, which is shorter than its diff:
```python
import functools
import math

import jax
import jax.numpy as jnp
from jax import lax
from jax.experimental import pallas as pl
from jax.experimental.pallas import tpu as pltpu
from jax.sharding import PartitionSpec as P

epsilon = 0.05
KAPPA = math.log2(math.e) / epsilon
LANES = 128
ROW_BLOCK = 256
COL_BLOCK = 512

f32 = jnp.float32
bf16 = jnp.bfloat16
VMEM = pl.BlockSpec(memory_space=pltpu.VMEM)
PARAMS = pltpu.CompilerParams(vmem_limit_bytes=40 * 2**20)


def vmem(shape, dtype=f32):
    return pltpu.VMEM(shape, dtype)


def pin(x):
    return pltpu.with_memory_space_constraint(x, pltpu.VMEM)


def split(x):
    first = x.astype(bf16)
    rest = x - first.astype(f32)
    second = rest.astype(bf16)
    third = (rest - second.astype(f32)).astype(bf16)
    return first, second, third


def to_lanes(x, reduce):
    parts = [
        reduce(x[r : r + LANES].T, axis=0, keepdims=True) for r in range(0, x.shape[0], LANES)
    ]
    return jnp.concatenate(parts, axis=1)


def to_rows(x):
    parts = [
        jnp.broadcast_to(x[:, r : r + LANES], (LANES, LANES)).T
        for r in range(0, x.shape[1], LANES)
    ]
    return jnp.concatenate(parts, axis=0)


def lse2(parts):
    top = functools.reduce(jnp.maximum, parts)
    return top + jnp.log2(sum(jnp.exp2(p - top) for p in parts))


def scores(a_ref, b_ref, row, rows, col, cols):
    return jnp.dot(
        a_ref[pl.ds(row, rows), :], b_ref[:, pl.ds(col, cols)], preferred_element_type=f32
    )


def tiles(width):
    return range(0, width, LANES)


def prepare_rows(n_src, src_ref, a_ref):
    dims, rows = src_ref.shape
    if n_src == 4:
        me, each = lax.axis_index("src"), dims // n_src
        points = jnp.concatenate(
            [src_ref[pl.ds(pl.multiple_of((me ^ k) * each, each), each), :] for k in range(n_src)],
            axis=0,
        )
    else:
        points = src_ref[...]
    s1, s2, s3 = (x.astype(f32) for x in split(points * (2.0 * KAPPA)))
    last = (lax.broadcasted_iota(jnp.int32, (16, rows), 0) < 3).astype(f32)
    a_ref[...] = jnp.concatenate([s1, s1, s2, s1, s3, s2, last], axis=0).T.astype(bf16)


def build(n_blocks, *refs):
    a_ref, g_ref = refs[:2]
    blocks = refs[2 : 2 + n_blocks]
    e_ref, b_ref, rho_ref, m_ref, acc_ref, shift_ref = refs[2 + n_blocks :]
    rows, cols = e_ref.shape
    dims = sum(ref.shape[0] for ref in blocks)
    points = jnp.concatenate([ref[...] for ref in blocks], axis=0)
    t1, t2, t3 = split(points)
    for k, part in enumerate((t1, t2, t1, t3, t1, t2)):
        b_ref[k * dims : (k + 1) * dims, :] = part
    offset = KAPPA * (g_ref[...] - jnp.sum(points * points, axis=0, keepdims=True))
    o1, o2, o3 = (x.astype(f32) for x in split(offset))
    fill = jnp.zeros((13, cols), f32)
    b_ref[6 * dims :, :] = jnp.concatenate([o1, o2, o3, fill], axis=0).astype(bf16)

    def run(columns):
        for row in range(0, rows, ROW_BLOCK):

            def top(i, best):
                s = scores(a_ref, b_ref, row, ROW_BLOCK, pl.multiple_of(i * COL_BLOCK, COL_BLOCK), COL_BLOCK)
                for t in tiles(COL_BLOCK):
                    best = jnp.maximum(best, s[:, t : t + LANES])
                return best

            best = lax.fori_loop(0, columns // COL_BLOCK, top, jnp.full((ROW_BLOCK, LANES), -jnp.inf, f32))
            shift_ref[row : row + ROW_BLOCK, :] = jnp.broadcast_to(
                jnp.max(best, axis=1, keepdims=True), (ROW_BLOCK, LANES)
            )
        acc_ref[...] = jnp.zeros_like(acc_ref)

        def block(i, _):
            col = pl.multiple_of(i * COL_BLOCK, COL_BLOCK)
            for row in range(0, rows, ROW_BLOCK):
                s = scores(a_ref, b_ref, row, ROW_BLOCK, col, COL_BLOCK)
                shift = shift_ref[row : row + ROW_BLOCK, :]
                acc = acc_ref[row : row + ROW_BLOCK, :]
                for t in tiles(COL_BLOCK):
                    e = jnp.exp2(s[:, t : t + LANES] - shift)
                    e_ref[row : row + ROW_BLOCK, pl.ds(pl.multiple_of(col + t, LANES), LANES)] = e
                    acc = acc + e
                acc_ref[row : row + ROW_BLOCK, :] = acc
            return 0

        lax.fori_loop(0, cols // COL_BLOCK, block, 0)
        total = to_lanes(acc_ref[...], jnp.sum)
        shift = to_lanes(shift_ref[...], jnp.max)
        m_ref[...] = shift
        rho_ref[...] = shift + jnp.log2(total)
        return total

    total = run(COL_BLOCK)
    fine = jnp.max(total) < 2.0**100

    @pl.when(jnp.logical_not(fine))
    def _():
        run(cols)


def column_sums(e_ref, u_ref, q_ref):
    rows, cols = e_ref.shape
    width, height = 1024, 64

    for col in range(0, cols, width):

        def body(i, acc):
            row = pl.multiple_of(i * height, height)
            u = u_ref[pl.ds(row, height), :]
            out = []
            for k, t in enumerate(tiles(width)):
                x = e_ref[pl.ds(row, height), col + t : col + t + LANES] * u
                out.append(acc[k] + jnp.sum(x.reshape(height // 8, 8, LANES), axis=0))
            return tuple(out)

        start = tuple(jnp.zeros((8, LANES), f32) for _ in tiles(width))
        acc = lax.fori_loop(0, rows // height, body, start, unroll=4)
        for k, t in enumerate(tiles(width)):
            q_ref[:, col + t : col + t + LANES] = jnp.sum(acc[k], axis=0, keepdims=True)


def row_sums(e_ref, v, v_ref, acc_ref):
    rows, cols = e_ref.shape
    height = 64
    v_ref[...] = v

    def body(i, _):
        row = pl.multiple_of(i * height, height)
        acc = jnp.zeros((height, LANES), f32)
        for t in tiles(cols):
            acc = acc + e_ref[pl.ds(row, height), t : t + LANES] * v_ref[:, t : t + LANES]
        acc_ref[pl.ds(row, height), :] = acc
        return 0

    lax.fori_loop(0, rows // height, body, 0, unroll=4)
    return to_lanes(acc_ref[...], jnp.sum)


def column_pass(n_parts, log_nt, *refs):
    parts = refs[:n_parts]
    m_ref, e_ref, a_ref, b_ref, lam_ref, f_ref, u_ref, q_ref = refs[n_parts:]
    rows, cols = e_ref.shape
    pot = log_nt - lse2([ref[...] for ref in parts])
    f_ref[...] = pot
    power = pot + m_ref[...]
    u = jnp.exp2(power)
    u_ref[...] = to_rows(u)
    column_sums(e_ref, u_ref, q_ref)
    q = q_ref[...]
    lam_ref[...] = jnp.log2(q)
    least = jnp.maximum(jnp.sum(u) * 2.0**-106, 2.0**-96)
    fine = (jnp.min(power) > -100.0) & (jnp.min(q) >= least) & (jnp.max(q) < 2.0**120)

    @pl.when(jnp.logical_not(fine))
    def _():
        u_ref[...] = to_rows(pot)

        def block(c, _):
            col = pl.multiple_of(c * COL_BLOCK, COL_BLOCK)

            def shifted(i):
                row = pl.multiple_of(i * LANES, LANES)
                s = scores(a_ref, b_ref, row, LANES, col, COL_BLOCK)
                return s + jnp.concatenate([u_ref[pl.ds(row, LANES), :]] * (COL_BLOCK // LANES), axis=1)

            top = lax.fori_loop(
                0,
                rows // LANES,
                lambda i, best: jnp.maximum(best, jnp.max(shifted(i), axis=0, keepdims=True)),
                jnp.full((1, COL_BLOCK), -jnp.inf, f32),
            )
            total = lax.fori_loop(
                0,
                rows // LANES,
                lambda i, acc: acc + jnp.sum(jnp.exp2(shifted(i) - top), axis=0, keepdims=True),
                jnp.zeros((1, COL_BLOCK), f32),
            )
            lam_ref[:, pl.ds(col, COL_BLOCK)] = top + jnp.log2(total)
            return 0

        lax.fori_loop(0, cols // COL_BLOCK, block, 0)


def row_log_sums(parts, log_ns, m_ref, e_ref, a_ref, b_ref, rho_ref, v_ref, acc_ref):
    rows, cols = e_ref.shape
    change = log_ns - lse2([ref[...] for ref in parts])
    v = jnp.exp2(change)
    r = row_sums(e_ref, v, v_ref, acc_ref)
    rho_ref[...] = m_ref[...] + jnp.log2(r)
    least = jnp.maximum(jnp.sum(v) * 2.0**-106, 2.0**-94)
    fine = (jnp.min(change) > -100.0) & (jnp.min(r) >= least) & (jnp.max(r) < 2.0**120)

    @pl.when(jnp.logical_not(fine))
    def _():
        v_ref[...] = change

        def block(i, _):
            row = pl.multiple_of(i * LANES, LANES)

            def shifted(c):
                col = pl.multiple_of(c * COL_BLOCK, COL_BLOCK)
                return scores(a_ref, b_ref, row, LANES, col, COL_BLOCK) + v_ref[:, pl.ds(col, COL_BLOCK)]

            top = lax.fori_loop(
                0,
                cols // COL_BLOCK,
                lambda c, best: jnp.maximum(best, jnp.max(shifted(c), axis=1, keepdims=True)),
                jnp.full((LANES, 1), -jnp.inf, f32),
            )
            total = lax.fori_loop(
                0,
                cols // COL_BLOCK,
                lambda c, acc: acc + jnp.sum(jnp.exp2(shifted(c) - top), axis=1, keepdims=True),
                jnp.zeros((LANES, 1), f32),
            )
            value = jnp.broadcast_to(top + jnp.log2(total), (LANES, LANES))
            rho_ref[:, pl.ds(row, LANES)] = jnp.max(value.T, axis=0, keepdims=True)
            return 0

        lax.fori_loop(0, rows // LANES, block, 0)

    return change


def row_pass(n_parts, log_ns, *refs):
    parts = refs[:n_parts]
    m_ref, e_ref, a_ref, b_ref, rho_ref, v_ref, acc_ref = refs[n_parts:]
    row_log_sums(parts, log_ns, m_ref, e_ref, a_ref, b_ref, rho_ref, v_ref, acc_ref)


def marginal_pass(n_parts, log_ns, *refs):
    parts = refs[:n_parts]
    m_ref, e_ref, a_ref, b_ref, f_ref, g_ref, sum_ref, new_g_ref, rho_ref, v_ref, acc_ref = refs[n_parts:]
    change = row_log_sums(parts, log_ns, m_ref, e_ref, a_ref, b_ref, rho_ref, v_ref, acc_ref)
    new_g_ref[...] = g_ref[...] + change * (1.0 / KAPPA)
    sum_ref[...] = jnp.exp2(f_ref[...] + rho_ref[...])


def others(x, axis, size, steps):
    return [lax.ppermute(x, axis, [(i, i ^ k) for i in range(size)]) for k in steps]


def pool_src(x):
    size = lax.axis_size("src")
    if size == 4:
        return [x] + others(x, "src", size, (1, 2, 3))
    every = lax.all_gather(x, "src", axis=0)
    return [every[k] for k in range(size)]


def pool_tgt(x, join):
    size = lax.axis_size("tgt")
    if size == 8:
        x = join([x] + others(x, "tgt", size, (1,)))
        return [x] + others(x, "tgt", size, (2, 4, 6))
    every = lax.all_gather(x, "tgt", axis=0)
    return [every[k] for k in range(size)]


def body(source_points, target_points, g_init):
    dims, rows = source_points.shape
    cols = target_points.shape[1]
    n_src, n_tgt = lax.axis_size("src"), lax.axis_size("tgt")
    log_nt, log_ns = math.log2(cols * n_tgt), math.log2(rows * n_src)
    depth = 6 * dims + 16
    row, col, square = vmem((1, rows)), vmem((1, cols)), vmem((rows, LANES))

    if n_src == 4:
        blocks = pool_src(target_points)
    else:
        blocks = [lax.all_gather(target_points, "src", axis=0, tiled=True)]
    a = pl.pallas_call(
        functools.partial(prepare_rows, n_src),
        out_shape=vmem((rows, depth), bf16),
        in_specs=[VMEM],
        out_specs=VMEM,
        compiler_params=PARAMS,
    )(source_points)
    g = g_init.reshape(1, cols)
    e, b, rho, m = pl.pallas_call(
        functools.partial(build, len(blocks)),
        out_shape=(vmem((rows, cols)), vmem((depth, cols), bf16), row, row),
        in_specs=[VMEM] * (2 + len(blocks)),
        out_specs=(VMEM,) * 4,
        scratch_shapes=[square, square],
        compiler_params=PARAMS,
    )(pin(a), g, *blocks)
    a, e, b, m = pin(a), pin(e), pin(b), pin(m)

    def columns(rho):
        parts = pool_tgt(rho, lse2)
        return pl.pallas_call(
            functools.partial(column_pass, len(parts), log_nt),
            out_shape=(col, row),
            in_specs=[VMEM] * (len(parts) + 4),
            out_specs=(VMEM, VMEM),
            scratch_shapes=[square, col],
            compiler_params=PARAMS,
        )(*parts, m, e, a, b)

    lam, _ = columns(rho)
    parts = pool_src(lam)
    rho = pl.pallas_call(
        functools.partial(row_pass, len(parts), log_ns),
        out_shape=row,
        in_specs=[VMEM] * (len(parts) + 4),
        out_specs=VMEM,
        scratch_shapes=[col, square],
        compiler_params=PARAMS,
    )(*parts, m, e, a, b)
    lam, f = columns(rho)
    parts = pool_src(lam)
    total, g_pot = pl.pallas_call(
        functools.partial(marginal_pass, len(parts), log_ns),
        out_shape=(row, jax.ShapeDtypeStruct((1, cols), f32)),
        in_specs=[VMEM] * (len(parts) + 6),
        out_specs=(VMEM, VMEM),
        scratch_shapes=[row, col, square],
        compiler_params=PARAMS,
    )(*parts, m, e, a, b, f, g)
    marginal = sum(pool_tgt(total, sum)) * (1.0 / (cols * n_tgt))
    f_pot = jnp.sum(source_points * source_points, axis=0) + f.reshape(rows) * (1.0 / KAPPA)
    return f_pot, g_pot.reshape(cols), marginal.reshape(rows)


def solution(mesh):
    in_specs = (P(None, "src"), P("src", "tgt"), P("tgt"))
    out_specs = (P("src"), P("tgt"), P("src"))
    return jax.shard_map(body, mesh=mesh, in_specs=in_specs, out_specs=out_specs, check_vma=False)
```

time: 274 us -> 213 us (0.78)
  Pallas kernels: 0 us -> 154 us
  blocking collectives: 140 us -> 0 us
  matrix products: 97.5 us -> 0 us
  waiting for transfers between devices: 0 us -> 26.7 us
  starting transfers between devices: 0 us -> 25 us
  other arithmetic: 26.2 us -> 1.29 us
  loops' own time: 3.02 us -> 0 us
    pallas_call x0 -> x6, Pallas kernels: none -> 154 us  [the longest x2 57.3 us: columns(): pl.pallas_call(functools.partial(column_pass, len(parts), log_nt), out_sh...]
    dot_general x80 -> x0, matrix products: 97.5 us -> none  [cost_block(): jnp.dot(rows_block, target_block, precision=lax.Precision.HIGHEST, prefer...]
    psum x5 -> x0, blocking collectives: 68.9 us -> none  [the longest x2 28.1 us: body(): whole_sum = lax.psum(col_sum * jnp.exp(col_top - whole_top), 'src')]
    pmax x4 -> x0, blocking collectives: 58.9 us -> none  [the longest x2 30.1 us: body(): whole_top = lax.pmax(col_top, 'src')]
    ppermute x0 -> x21, waiting for transfers between devices: none -> 26.7 us  [others(): lax.ppermute(x, axis, [(i, i ^ k) for i in range(size)])]
    ppermute x0 -> x21, starting transfers between devices: none -> 25 us  [others(): lax.ppermute(x, axis, [(i, i ^ k) for i in range(size)])]
    reduce_sum x145 -> x1, other arithmetic: 24.8 us -> 0.02 us  [body(): jnp.sum(source_points * source_points, axis=0)]
    all_gather x1 -> x0, blocking collectives: 11.8 us -> none  [body(): target_block = lax.all_gather(target_points, 'src', axis=0, tiled=True)]
  transfers between devices with their start and end apart: 0 -> 21, of which waited for: 0 -> 17; matrix products, arithmetic and copies ran while one was open for 0% -> 0% of each run, Pallas kernels for 0% -> 0%
where the time goes in v1:
time: 213 us; the launch traced here: 212 us
  Pallas kernels  154 us (72%)
  waiting for transfers between devices  26.7 us (13%)
  starting transfers between devices  25 us (12%)
  local copies, waits for them, and re-layouts  4.59 us (2%)
    pallas_call x2, Pallas kernels, columns(): pl.pallas_call(functools.partial(column_pass, len(parts), log_nt), out_sh...  57.3 us
    pallas_call x1, Pallas kernels, body(): pl.pallas_call(functools.partial(marginal_pass, len(parts), log_ns), out_...  38.3 us
    pallas_call x1, Pallas kernels, body(): pl.pallas_call(functools.partial(row_pass, len(parts), log_ns), out_shape...  37.6 us
    ppermute x21, waiting for transfers between devices, others(): lax.ppermute(x, axis, [(i, i ^ k) for i in range(size)])  26.7 us
    ppermute x21, starting transfers between devices, others(): lax.ppermute(x, axis, [(i, i ^ k) for i in range(size)])  25 us
    pallas_call x1, Pallas kernels, body(): pl.pallas_call(functools.partial(build, len(blocks)), out_shape=(vmem((ro...  20.7 us
    unnamed x44, local copies, waits for them, and re-layouts  4.59 us
  transfers between devices with their start and end apart: 21, of which 17 were waited for; matrix products, arithmetic and copies ran while one was open for 0% of the time, Pallas kernels for 0%

profile of v1, /device:TPU:0, one launch (start us, length us, event | category | flops | bytes accessed | tf_op | source)
XLA Modules:
  0.0 212.3 jit_solution(12984086114244322766)
XLA Ops:
  0.6 3.0 %collective-permute-start = (f32[8,4096]{1,0:T(8,128)}, f32[8,4096]{1,0:T(8,128)S(1)}, u32[]{:S(2)}, u32[]{:S(2)}) collective-permute-start(f32[8,4096]{1,0:T(8,128)} %refs_2_.1), channel_id=1, source_target_pairs={{0,8},{8,0},{16,24},{24,16},{1,9},{9,1},{17,25},{25,17},{2,10},{10... | collective-permute-start | bytes 393224 | tf_op jit(solution)/shard_map/ppermute | solution.py:281
  3.6 1.5 collective-permute-start.1
  5.2 0.0 collective-permute-start.2
  5.2 0.9 copy-done
  6.1 0.2 shard_map.58.refs_0_.refs_6_
  6.3 1.6 collective-permute-done.refs_3_
  7.9 3.8 %collective-permute-done.1.refs_4_ = f32[8,4096]{1,0:T(8,128)S(1)} collective-permute-done((f32[8,4096]{1,0:T(8,128)}, f32[8,4096]{1,0:T(8,128)S(1)}, u32[]{:S(2)}, u32[]{:S(2)}) %collective-permute-start.1) | collective-permute-done | bytes 131104 | tf_op jit(solution)/shard_map/ppermute | solution.py:281
  11.6 0.0 collective-permute-done.2.refs_5_
  11.6 0.0 copy-done.5
  11.6 0.6 copy-done.6
  12.3 0.1 copy-done.7
  12.3 20.7 %shard_map.59 = (f32[1024,4096]{1,0:T(8,128)S(1)}, bf16[208,4096]{1,0:T(8,128)(2,1)S(1)}, f32[1,1024]{1,0:T(1,128)S(1)}, f32[1,1024]{1,0:T(1,128)S(1)}) custom-call(bf16[1024,208]{1,0:T(8,128)(2,1)S(1)} %shard_map.58.refs_0_.refs_6_, f32[1,4096]{1,0:T(1,128)} %bitcast.4, f32[8,4096]{1,0:T(8,128)} %refs_2_.1, f32[8,4096]{1,0:T(8,128)} %copy-done.5, ...), custom_call_target="tpu_custom_call" | custom-call | tf_op jit(solution)/shard_map/pallas_call | solution.py:321
  33.0 0.1 collective-permute-start.3
  33.1 1.2 collective-permute-done.3
  34.3 0.0 copy-start.11
  34.3 1.6 collective-permute-start.4
  35.9 2.6 %collective-permute-start.5 = (f32[1,1024]{1,0:T(1,128)S(1)}, f32[1,1024]{1,0:T(1,128)S(1)}, u32[]{:S(2)}, u32[]{:S(2)}) collective-permute-start(f32[1,1024]{1,0:T(1,128)S(1)} %multiply_add_fusion.1.refs_0_), channel_id=1, source_target_pairs={{0,4},{1,5},{2,6},{3,7},{4,0},{5,1},{6,2},{7,3},{8,12},{9,13},{10,... | collective-permute-start | bytes 12296 | tf_op jit(solution)/shard_map/ppermute | solution.py:281
  38.5 0.2 collective-permute-start.6
  38.7 0.0 collective-permute-done.4.refs_1_
  38.7 1.7 collective-permute-done.5.refs_2_
  40.4 3.5 %collective-permute-done.6.refs_3_ = f32[1,1024]{1,0:T(1,128)S(1)} collective-permute-done((f32[1,1024]{1,0:T(1,128)S(1)}, f32[1,1024]{1,0:T(1,128)S(1)}, u32[]{:S(2)}, u32[]{:S(2)}) %collective-permute-start.6) | collective-permute-done | bytes 4128 | tf_op jit(solution)/shard_map/ppermute | solution.py:281
  43.9 0.0 copy-done.16
  43.9 0.6 copy-done.20
  44.5 28.9 %shard_map.60 = (f32[1,4096]{1,0:T(1,128)S(1)}, f32[1,1024]{1,0:T(1,128)}) custom-call(f32[1,1024]{1,0:T(1,128)} %copy-done.11, f32[1,1024]{1,0:T(1,128)} %copy-done.16, f32[1,1024]{1,0:T(1,128)} %copy-done.18, f32[1,1024]{1,0:T(1,128)} %copy-done.20, f32[1,1024]{1,0:T(1,128)S(1)} %get-tuple-element.13.refs_4_, f32[1024,4096]{1,0:T(8,128)S(1)} %get-tuple-element.14.refs_5_, ...), custom_call_target="tpu_custom_call" | custom-call | tf_op jit(solution)/shard_map/pallas_call | solution.py:333
  73.4 1.2 collective-permute-start.7
  74.6 0.9 collective-permute-start.8
  75.5 1.4 collective-permute-start.9
  76.9 0.2 collective-permute-done.7.refs_1_
  77.2 1.2 collective-permute-done.8.refs_2_
  78.4 1.8 collective-permute-done.9.refs_3_
  80.1 0.0 copy-done.4
  80.1 0.6 copy-done.15
  80.7 37.6 %shard_map.61 = f32[1,1024]{1,0:T(1,128)S(1)} custom-call(f32[1,4096]{1,0:T(1,128)} %copy-done.4, f32[1,4096]{1,0:T(1,128)} %copy-done.13, f32[1,4096]{1,0:T(1,128)} %copy-done.14, f32[1,4096]{1,0:T(1,128)} %copy-done.15, f32[1,1024]{1,0:T(1,128)S(1)} %get-tuple-element.13.refs_4_, f32[1024,4096]{1,0:T(8,128)S(1)} %get-tuple-element.14.refs_5_, ...), custom_call_target="tpu_custom_call" | custom-call | tf_op jit(solution)/shard_map/pallas_call | solution.py:344
  118.3 0.1 collective-permute-start.10
  118.4 1.2 collective-permute-done.10
  119.6 0.0 copy-start.12
  119.6 0.1 collective-permute-start.11
  119.7 0.8 collective-permute-start.12
  120.4 3.6 %collective-permute-start.13 = (f32[1,1024]{1,0:T(1,128)S(1)}, f32[1,1024]{1,0:T(1,128)S(1)}, u32[]{:S(2)}, u32[]{:S(2)}) collective-permute-start(f32[1,1024]{1,0:T(1,128)S(1)} %multiply_add_fusion.refs_0_), channel_id=1, source_target_pairs={{0,6},{1,7},{2,4},{3,5},{4,2},{5,3},{6,0},{7,1},{8,14},{9,15},{10,... | collective-permute-start | bytes 12296 | tf_op jit(solution)/shard_map/ppermute | solution.py:281
  124.0 0.0 collective-permute-done.11.refs_1_
  124.0 0.2 collective-permute-done.12.refs_2_
  124.2 1.6 collective-permute-done.13.refs_3_
  125.9 0.6 copy-done.21
  126.4 28.4 %shard_map.62 = (f32[1,4096]{1,0:T(1,128)S(1)}, f32[1,1024]{1,0:T(1,128)S(1)}) custom-call(f32[1,1024]{1,0:T(1,128)} %copy-done.12, f32[1,1024]{1,0:T(1,128)} %copy-done.17, f32[1,1024]{1,0:T(1,128)} %copy-done.19, f32[1,1024]{1,0:T(1,128)} %copy-done.21, f32[1,1024]{1,0:T(1,128)S(1)} %get-tuple-element.13.refs_4_, ...), custom_call_target="tpu_custom_call" | custom-call | tf_op jit(solution)/shard_map/pallas_call | solution.py:333
  154.8 0.0 copy-start.2
  154.8 0.6 copy-done.2
  155.4 1.5 collective-permute-start.14
  156.9 0.5 collective-permute-start.15
  157.4 1.5 collective-permute-start.16
  158.9 0.4 collective-permute-done.14.refs_1_
  159.3 1.3 collective-permute-done.15.refs_2_
  160.7 1.4 collective-permute-done.16.refs_3_
  162.1 0.6 copy-done.10
  162.7 38.3 %shard_map.63 = (f32[1,1024]{1,0:T(1,128)S(1)}, f32[1,4096]{1,0:T(1,128)}) custom-call(f32[1,4096]{1,0:T(1,128)} %copy-done.1, f32[1,4096]{1,0:T(1,128)} %copy-done.8, f32[1,4096]{1,0:T(1,128)} %copy-done.9, f32[1,4096]{1,0:T(1,128)} %copy-done.10, f32[1,1024]{1,0:T(1,128)S(1)} %get-tuple-element.13.refs_4_, f32[1024,4096]{1,0:T(8,128)S(1)} %get-tuple-element.14.refs_5_, ...), custom_call_target="tpu_custom_call" | custom-call | tf_op jit(solution)/shard_map/pallas_call | solution.py:354
  200.9 0.0 collective-permute-start.17
  201.0 1.1 collective-permute-done.17
  202.1 0.9 collective-permute-start.18
  203.0 3.3 %collective-permute-start.19 = (f32[1,1024]{1,0:T(1,128)S(1)}, f32[1,1024]{1,0:T(1,128)S(1)}, u32[]{:S(2)}, u32[]{:S(2)}) collective-permute-start(f32[1,1024]{1,0:T(1,128)S(1)} %add.32), channel_id=1, source_target_pairs={{0,4},{1,5},{2,6},{3,7},{4,0},{5,1},{6,2},{7,3},{8,12},{9,13},{10,... | collective-permute-start | bytes 12296 | tf_op jit(solution)/shard_map/ppermute | solution.py:281
  206.3 0.2 collective-permute-start.20
  206.5 0.6 add.31
  207.1 0.0 collective-permute-done.18
  207.1 0.8 collective-permute-done.19
  207.9 3.8 %collective-permute-done.20 = f32[1,1024]{1,0:T(1,128)S(1)} collective-permute-done((f32[1,1024]{1,0:T(1,128)S(1)}, f32[1,1024]{1,0:T(1,128)S(1)}, u32[]{:S(2)}, u32[]{:S(2)}) %collective-permute-start.20) | collective-permute-done | bytes 4128 | tf_op jit(solution)/shard_map/ppermute | solution.py:281
  211.7 0.6 add_multiply_fusion
  (35 shorter events, 0.1 us)
Async XLA Ops:
  0.6 7.2 %collective-permute-start = (f32[8,4096]{1,0:T(8,128)}, f32[8,4096]{1,0:T(8,128)S(1)}, u32[]{:S(2)}, u32[]{:S(2)}) collective-permute-start(f32[8,4096]{1,0:T(8,128)} %refs_2_.1), channel_id=1, source_target_pairs={{0,8},{8,0},{16,24},{24,16},{1,9},{9,1},{17,25},{25,17},{2,10},{10... | collective-permute-start | bytes 393224 | tf_op jit(solution)/shard_map/ppermute | solution.py:281
  3.6 8.0 %collective-permute-start.1 = (f32[8,4096]{1,0:T(8,128)}, f32[8,4096]{1,0:T(8,128)S(1)}, u32[]{:S(2)}, u32[]{:S(2)}) collective-permute-start(f32[8,4096]{1,0:T(8,128)} %refs_2_.1), channel_id=1, source_target_pairs={{0,16},{8,24},{16,0},{24,8},{1,17},{9,25},{17,1},{25,9},{2,18},{10... | collective-permute-start | bytes 393224 | tf_op jit(solution)/shard_map/ppermute | solution.py:281
  5.2 6.5 %collective-permute-start.2 = (f32[8,4096]{1,0:T(8,128)}, f32[8,4096]{1,0:T(8,128)S(1)}, u32[]{:S(2)}, u32[]{:S(2)}) collective-permute-start(f32[8,4096]{1,0:T(8,128)} %refs_2_.1), channel_id=1, source_target_pairs={{0,24},{8,16},{16,8},{24,0},{1,25},{9,17},{17,9},{25,1},{2,26},{10... | collective-permute-start | bytes 393224 | tf_op jit(solution)/shard_map/ppermute | solution.py:281
  5.2 0.9 copy-start
  7.9 3.8 %copy-start.5 = (f32[8,4096]{1,0:T(8,128)}, f32[8,4096]{1,0:T(8,128)S(1)}, u32[]{:S(2)}) copy-start(f32[8,4096]{1,0:T(8,128)S(1)} %collective-permute-done.refs_3_) | copy-start | bytes 393220
  11.6 0.7 copy-start.6
  11.6 0.7 copy-start.7
  33.0 1.2 collective-permute-start.3
  34.3 9.6 %copy-start.11 = (f32[1,1024]{1,0:T(1,128)}, f32[1,1024]{1,0:T(1,128)S(1)}, u32[]{:S(2)}) copy-start(f32[1,1024]{1,0:T(1,128)S(1)} %multiply_add_fusion.1.refs_0_) | copy-start | bytes 12292
  34.3 4.5 %collective-permute-start.4 = (f32[1,1024]{1,0:T(1,128)S(1)}, f32[1,1024]{1,0:T(1,128)S(1)}, u32[]{:S(2)}, u32[]{:S(2)}) collective-permute-start(f32[1,1024]{1,0:T(1,128)S(1)} %multiply_add_fusion.1.refs_0_), channel_id=1, source_target_pairs={{0,2},{1,3},{2,0},{3,1},{4,6},{5,7},{6,4},{7,5},{8,10},{9,11},{10,... | collective-permute-start | bytes 12296 | tf_op jit(solution)/shard_map/ppermute | solution.py:281
  35.9 4.5 %collective-permute-start.5 = (f32[1,1024]{1,0:T(1,128)S(1)}, f32[1,1024]{1,0:T(1,128)S(1)}, u32[]{:S(2)}, u32[]{:S(2)}) collective-permute-start(f32[1,1024]{1,0:T(1,128)S(1)} %multiply_add_fusion.1.refs_0_), channel_id=1, source_target_pairs={{0,4},{1,5},{2,6},{3,7},{4,0},{5,1},{6,2},{7,3},{8,12},{9,13},{10,... | collective-permute-start | bytes 12296 | tf_op jit(solution)/shard_map/ppermute | solution.py:281
  38.5 5.4 %collective-permute-start.6 = (f32[1,1024]{1,0:T(1,128)S(1)}, f32[1,1024]{1,0:T(1,128)S(1)}, u32[]{:S(2)}, u32[]{:S(2)}) collective-permute-start(f32[1,1024]{1,0:T(1,128)S(1)} %multiply_add_fusion.1.refs_0_), channel_id=1, source_target_pairs={{0,6},{1,7},{2,4},{3,5},{4,2},{5,3},{6,0},{7,1},{8,14},{9,15},{10,... | collective-permute-start | bytes 12296 | tf_op jit(solution)/shard_map/ppermute | solution.py:281
  38.7 5.2 %copy-start.16 = (f32[1,1024]{1,0:T(1,128)}, f32[1,1024]{1,0:T(1,128)S(1)}, u32[]{:S(2)}) copy-start(f32[1,1024]{1,0:T(1,128)S(1)} %collective-permute-done.4.refs_1_) | copy-start | bytes 12292
  40.4 3.5 %copy-start.18 = (f32[1,1024]{1,0:T(1,128)}, f32[1,1024]{1,0:T(1,128)S(1)}, u32[]{:S(2)}) copy-start(f32[1,1024]{1,0:T(1,128)S(1)} %collective-permute-done.5.refs_2_) | copy-start | bytes 12292
  43.9 0.6 copy-start.20
  73.4 6.7 %copy-start.4 = (f32[1,4096]{1,0:T(1,128)}, f32[1,4096]{1,0:T(1,128)S(1)}, u32[]{:S(2)}) copy-start(f32[1,4096]{1,0:T(1,128)S(1)} %get-tuple-element.16.refs_0_) | copy-start | bytes 49156
  73.4 3.7 %collective-permute-start.7 = (f32[1,4096]{1,0:T(1,128)S(1)}, f32[1,4096]{1,0:T(1,128)S(1)}, u32[]{:S(2)}, u32[]{:S(2)}) collective-permute-start(f32[1,4096]{1,0:T(1,128)S(1)} %get-tuple-element.16.refs_0_), channel_id=1, source_target_pairs={{0,8},{8,0},{16,24},{24,16},{1,9},{9,1},{17,25},{25,17},{2,10},{10... | collective-permute-start | bytes 49160 | tf_op jit(solution)/shard_map/ppermute | solution.py:281
  74.6 3.7 %collective-permute-start.8 = (f32[1,4096]{1,0:T(1,128)S(1)}, f32[1,4096]{1,0:T(1,128)S(1)}, u32[]{:S(2)}, u32[]{:S(2)}) collective-permute-start(f32[1,4096]{1,0:T(1,128)S(1)} %get-tuple-element.16.refs_0_), channel_id=1, source_target_pairs={{0,16},{8,24},{16,0},{24,8},{1,17},{9,25},{17,1},{25,9},{2,18},{10... | collective-permute-start | bytes 49160 | tf_op jit(solution)/shard_map/ppermute | solution.py:281
  75.5 4.6 %collective-permute-start.9 = (f32[1,4096]{1,0:T(1,128)S(1)}, f32[1,4096]{1,0:T(1,128)S(1)}, u32[]{:S(2)}, u32[]{:S(2)}) collective-permute-start(f32[1,4096]{1,0:T(1,128)S(1)} %get-tuple-element.16.refs_0_), channel_id=1, source_target_pairs={{0,24},{8,16},{16,8},{24,0},{1,25},{9,17},{17,9},{25,1},{2,26},{10... | collective-permute-start | bytes 49160 | tf_op jit(solution)/shard_map/ppermute | solution.py:281
  77.2 3.0 %copy-start.13 = (f32[1,4096]{1,0:T(1,128)}, f32[1,4096]{1,0:T(1,128)S(1)}, u32[]{:S(2)}) copy-start(f32[1,4096]{1,0:T(1,128)S(1)} %collective-permute-done.7.refs_1_) | copy-start | bytes 49156
  78.4 1.8 copy-start.14
  80.1 0.6 copy-start.15
  118.3 1.2 collective-permute-start.10
  119.6 6.3 %copy-start.12 = (f32[1,1024]{1,0:T(1,128)}, f32[1,1024]{1,0:T(1,128)S(1)}, u32[]{:S(2)}) copy-start(f32[1,1024]{1,0:T(1,128)S(1)} %multiply_add_fusion.refs_0_) | copy-start | bytes 12292
  119.6 4.5 %collective-permute-start.11 = (f32[1,1024]{1,0:T(1,128)S(1)}, f32[1,1024]{1,0:T(1,128)S(1)}, u32[]{:S(2)}, u32[]{:S(2)}) collective-permute-start(f32[1,1024]{1,0:T(1,128)S(1)} %multiply_add_fusion.refs_0_), channel_id=1, source_target_pairs={{0,2},{1,3},{2,0},{3,1},{4,6},{5,7},{6,4},{7,5},{8,10},{9,11},{10,... | collective-permute-start | bytes 12296 | tf_op jit(solution)/shard_map/ppermute | solution.py:281
  119.7 4.6 %collective-permute-start.12 = (f32[1,1024]{1,0:T(1,128)S(1)}, f32[1,1024]{1,0:T(1,128)S(1)}, u32[]{:S(2)}, u32[]{:S(2)}) collective-permute-start(f32[1,1024]{1,0:T(1,128)S(1)} %multiply_add_fusion.refs_0_), channel_id=1, source_target_pairs={{0,4},{1,5},{2,6},{3,7},{4,0},{5,1},{6,2},{7,3},{8,12},{9,13},{10,... | collective-permute-start | bytes 12296 | tf_op jit(solution)/shard_map/ppermute | solution.py:281
  120.4 5.4 %collective-permute-start.13 = (f32[1,1024]{1,0:T(1,128)S(1)}, f32[1,1024]{1,0:T(1,128)S(1)}, u32[]{:S(2)}, u32[]{:S(2)}) collective-permute-start(f32[1,1024]{1,0:T(1,128)S(1)} %multiply_add_fusion.refs_0_), channel_id=1, source_target_pairs={{0,6},{1,7},{2,4},{3,5},{4,2},{5,3},{6,0},{7,1},{8,14},{9,15},{10,... | collective-permute-start | bytes 12296 | tf_op jit(solution)/shard_map/ppermute | solution.py:281
  124.0 1.8 copy-start.17
  124.2 1.6 copy-start.19
  125.8 0.6 copy-start.21
  154.8 0.6 copy-start.2
  155.4 6.7 %copy-start.1 = (f32[1,4096]{1,0:T(1,128)}, f32[1,4096]{1,0:T(1,128)S(1)}, u32[]{:S(2)}) copy-start(f32[1,4096]{1,0:T(1,128)S(1)} %get-tuple-element.18.refs_0_) | copy-start | bytes 49156
  155.4 51.1 %copy-start.3 = (f32[1,1024]{1,0:T(1,128)S(1)}, f32[1,1024]{1,0:T(1,128)}, u32[]{:S(2)}) copy-start(f32[1,1024]{1,0:T(1,128)} %copy-done.2) | copy-start | bytes 12292
  155.4 3.9 %collective-permute-start.14 = (f32[1,4096]{1,0:T(1,128)S(1)}, f32[1,4096]{1,0:T(1,128)S(1)}, u32[]{:S(2)}, u32[]{:S(2)}) collective-permute-start(f32[1,4096]{1,0:T(1,128)S(1)} %get-tuple-element.18.refs_0_), channel_id=1, source_target_pairs={{0,8},{8,0},{16,24},{24,16},{1,9},{9,1},{17,25},{25,17},{2,10},{10... | collective-permute-start | bytes 49160 | tf_op jit(solution)/shard_map/ppermute | solution.py:281
  156.9 3.7 %collective-permute-start.15 = (f32[1,4096]{1,0:T(1,128)S(1)}, f32[1,4096]{1,0:T(1,128)S(1)}, u32[]{:S(2)}, u32[]{:S(2)}) collective-permute-start(f32[1,4096]{1,0:T(1,128)S(1)} %get-tuple-element.18.refs_0_), channel_id=1, source_target_pairs={{0,16},{8,24},{16,0},{24,8},{1,17},{9,25},{17,1},{25,9},{2,18},{10... | collective-permute-start | bytes 49160 | tf_op jit(solution)/shard_map/ppermute | solution.py:281
  157.4 4.6 %collective-permute-start.16 = (f32[1,4096]{1,0:T(1,128)S(1)}, f32[1,4096]{1,0:T(1,128)S(1)}, u32[]{:S(2)}, u32[]{:S(2)}) collective-permute-start(f32[1,4096]{1,0:T(1,128)S(1)} %get-tuple-element.18.refs_0_), channel_id=1, source_target_pairs={{0,24},{8,16},{16,8},{24,0},{1,25},{9,17},{17,9},{25,1},{2,26},{10... | collective-permute-start | bytes 49160 | tf_op jit(solution)/shard_map/ppermute | solution.py:281
  159.3 2.8 %copy-start.8 = (f32[1,4096]{1,0:T(1,128)}, f32[1,4096]{1,0:T(1,128)S(1)}, u32[]{:S(2)}) copy-start(f32[1,4096]{1,0:T(1,128)S(1)} %collective-permute-done.14.refs_1_) | copy-start | bytes 49156
  160.6 1.4 copy-start.9
  162.1 0.6 copy-start.10
  200.9 1.2 collective-permute-start.17
  202.1 5.0 %collective-permute-start.18 = (f32[1,1024]{1,0:T(1,128)S(1)}, f32[1,1024]{1,0:T(1,128)S(1)}, u32[]{:S(2)}, u32[]{:S(2)}) collective-permute-start(f32[1,1024]{1,0:T(1,128)S(1)} %add.32), channel_id=1, source_target_pairs={{0,2},{1,3},{2,0},{3,1},{4,6},{5,7},{6,4},{7,5},{8,10},{9,11},{10,... | collective-permute-start | bytes 12296 | tf_op jit(solution)/shard_map/ppermute | solution.py:281
  203.0 4.9 %collective-permute-start.19 = (f32[1,1024]{1,0:T(1,128)S(1)}, f32[1,1024]{1,0:T(1,128)S(1)}, u32[]{:S(2)}, u32[]{:S(2)}) collective-permute-start(f32[1,1024]{1,0:T(1,128)S(1)} %add.32), channel_id=1, source_target_pairs={{0,4},{1,5},{2,6},{3,7},{4,0},{5,1},{6,2},{7,3},{8,12},{9,13},{10,... | collective-permute-start | bytes 12296 | tf_op jit(solution)/shard_map/ppermute | solution.py:281
  206.3 5.4 %collective-permute-start.20 = (f32[1,1024]{1,0:T(1,128)S(1)}, f32[1,1024]{1,0:T(1,128)S(1)}, u32[]{:S(2)}, u32[]{:S(2)}) collective-permute-start(f32[1,1024]{1,0:T(1,128)S(1)} %add.32), channel_id=1, source_target_pairs={{0,6},{1,7},{2,4},{3,5},{4,2},{5,3},{6,0},{7,1},{8,14},{9,15},{10,... | collective-permute-start | bytes 12296 | tf_op jit(solution)/shard_map/ppermute | solution.py:281

commit v2 on v1

--- a/solution.py
+++ b/solution.py
@@ -17,7 +17,7 @@
 f32 = jnp.float32
 bf16 = jnp.bfloat16
 VMEM = pl.BlockSpec(memory_space=pltpu.VMEM)
-PARAMS = pltpu.CompilerParams(vmem_limit_bytes=40 * 2**20)
+PARAMS = pltpu.CompilerParams(vmem_limit_bytes=16 * 2**20)
 
 
 def vmem(shape, dtype=f32):
@@ -325,7 +325,7 @@
         out_specs=(VMEM,) * 4,
         scratch_shapes=[square, square],
         compiler_params=PARAMS,
-    )(pin(a), g, *blocks)
+    )(pin(a), g, *map(pin, blocks))
     a, e, b, m = pin(a), pin(e), pin(b), pin(m)
 
     def columns(rho):
@@ -337,7 +337,7 @@
             out_specs=(VMEM, VMEM),
             scratch_shapes=[square, col],
             compiler_params=PARAMS,
-        )(*parts, m, e, a, b)
+        )(*map(pin, parts), m, e, a, b)
 
     lam, _ = columns(rho)
     parts = pool_src(lam)
@@ -348,7 +348,7 @@
         out_specs=VMEM,
         scratch_shapes=[col, square],
         compiler_params=PARAMS,
-    )(*parts, m, e, a, b)
+    )(*map(pin, parts), m, e, a, b)
     lam, f = columns(rho)
     parts = pool_src(lam)
     total, g_pot = pl.pallas_call(
@@ -358,7 +358,7 @@
         out_specs=(VMEM, VMEM),
         scratch_shapes=[row, col, square],
         compiler_params=PARAMS,
-    )(*parts, m, e, a, b, f, g)
+    )(*map(pin, parts), m, e, a, b, pin(f), g)
     marginal = sum(pool_tgt(total, sum)) * (1.0 / (cols * n_tgt))
     f_pot = jnp.sum(source_points * source_points, axis=0) + f.reshape(rows) * (1.0 / KAPPA)
     return f_pot, g_pot.reshape(cols), marginal.reshape(rows)

time: 213 us -> 207 us (0.972)
  Pallas kernels: 154 us -> 151 us
    unnamed x44 -> x6, local copies, waits for them, and re-layouts: 4.59 us -> 2.53 us
where the time goes in v2:
time: 207 us
  Pallas kernels  151 us (73%)
  waiting for transfers between devices  26.6 us (13%)
  starting transfers between devices  25 us (12%)
  local copies, waits for them, and re-layouts  2.53 us (1%)
    pallas_call x2, Pallas kernels, columns(): pl.pallas_call(functools.partial(column_pass, len(parts), log_nt), out_sh...  56 us
    pallas_call x1, Pallas kernels, body(): pl.pallas_call(functools.partial(marginal_pass, len(parts), log_ns), out_...  37.9 us
    pallas_call x1, Pallas kernels, body(): pl.pallas_call(functools.partial(row_pass, len(parts), log_ns), out_shape...  37.2 us
    ppermute x21, waiting for transfers between devices, others(): lax.ppermute(x, axis, [(i, i ^ k) for i in range(size)])  26.6 us
    ppermute x21, starting transfers between devices, others(): lax.ppermute(x, axis, [(i, i ^ k) for i in range(size)])  25 us
    pallas_call x1, Pallas kernels, body(): pl.pallas_call(functools.partial(build, len(blocks)), out_shape=(vmem((ro...  19.5 us
  transfers between devices with their start and end apart: 21, of which 17 were waited for; matrix products, arithmetic and copies ran while one was open for 0% of the time, Pallas kernels for 0%

profile of v2, /device:TPU:0, one launch (start us, length us, event | category | flops | bytes accessed | tf_op | source)
XLA Modules:
  0.0 207.0 jit_solution(11310076000866899213)
XLA Ops:
  0.6 3.0 %collective-permute-start = (f32[8,4096]{1,0:T(8,128)}, f32[8,4096]{1,0:T(8,128)S(1)}, u32[]{:S(2)}, u32[]{:S(2)}) collective-permute-start(f32[8,4096]{1,0:T(8,128)} %refs_2_.1), channel_id=1, source_target_pairs={{0,8},{8,0},{16,24},{24,16},{1,9},{9,1},{17,25},{25,17},{2,10},{10... | collective-permute-start | bytes 393224 | tf_op jit(solution)/shard_map/ppermute | solution.py:281
  3.6 1.5 collective-permute-start.1
  5.2 0.0 collective-permute-start.2
  5.2 0.0 copy-start
  5.2 0.9 copy-done
  6.1 0.2 shard_map.58.refs_0_.refs_6_
  6.3 1.6 collective-permute-done.refs_3_
  7.9 3.8 %collective-permute-done.1.refs_4_ = f32[8,4096]{1,0:T(8,128)S(1)} collective-permute-done((f32[8,4096]{1,0:T(8,128)}, f32[8,4096]{1,0:T(8,128)S(1)}, u32[]{:S(2)}, u32[]{:S(2)}) %collective-permute-start.1) | collective-permute-done | bytes 131104 | tf_op jit(solution)/shard_map/ppermute | solution.py:281
  11.6 0.0 collective-permute-done.2.refs_5_
  11.6 0.0 copy-start.1
  11.6 0.9 copy-done.1
  12.5 0.0 copy-start.2
  12.5 0.7 copy-done.2
  13.2 19.5 %shard_map.59 = (f32[1024,4096]{1,0:T(8,128)S(1)}, bf16[208,4096]{1,0:T(8,128)(2,1)S(1)}, f32[1,1024]{1,0:T(1,128)S(1)}, f32[1,1024]{1,0:T(1,128)S(1)}) custom-call(bf16[1024,208]{1,0:T(8,128)(2,1)S(1)} %shard_map.58.refs_0_.refs_6_, f32[1,4096]{1,0:T(1,128)S(1)} %bitcast.4, f32[8,4096]{1,0:T(8,128)S(1)} %copy-done.1, ...), custom_call_target="tpu_custom_call" | custom-call | tf_op jit(solution)/shard_map/pallas_call | solution.py:321
  32.8 0.1 collective-permute-start.3
  32.9 1.2 collective-permute-done.3
  34.0 1.6 collective-permute-start.4
  35.7 2.6 %collective-permute-start.5 = (f32[1,1024]{1,0:T(1,128)S(1)}, f32[1,1024]{1,0:T(1,128)S(1)}, u32[]{:S(2)}, u32[]{:S(2)}) collective-permute-start(f32[1,1024]{1,0:T(1,128)S(1)} %multiply_add_fusion.1.refs_0_), channel_id=1, source_target_pairs={{0,4},{1,5},{2,6},{3,7},{4,0},{5,1},{6,2},{7,3},{8,12},{9,13},{10,... | collective-permute-start | bytes 12296 | tf_op jit(solution)/shard_map/ppermute | solution.py:281
  38.3 0.2 collective-permute-start.6
  38.5 0.0 collective-permute-done.4.refs_1_
  38.5 1.7 collective-permute-done.5.refs_2_
  40.2 3.5 %collective-permute-done.6.refs_3_ = f32[1,1024]{1,0:T(1,128)S(1)} collective-permute-done((f32[1,1024]{1,0:T(1,128)S(1)}, f32[1,1024]{1,0:T(1,128)S(1)}, u32[]{:S(2)}, u32[]{:S(2)}) %collective-permute-start.6) | collective-permute-done | bytes 4128 | tf_op jit(solution)/shard_map/ppermute | solution.py:281
  43.7 28.3 %shard_map.60 = (f32[1,4096]{1,0:T(1,128)S(1)}, f32[1,1024]{1,0:T(1,128)}) custom-call(f32[1,1024]{1,0:T(1,128)S(1)} %multiply_add_fusion.1.refs_0_, f32[1,1024]{1,0:T(1,128)S(1)} %collective-permute-done.4.refs_1_, f32[1,1024]{1,0:T(1,128)S(1)} %collective-permute-done.5.refs_2_, f32[1,1024]{1,0:T(1,128)S(1)} %collective-permute-done.6.refs_3_, ...), custom_call_target="tpu_custom_call" | custom-call | tf_op jit(solution)/shard_map/pallas_call | solution.py:333
  72.0 1.2 collective-permute-start.7
  73.2 0.8 collective-permute-start.8
  74.0 1.4 collective-permute-start.9
  75.5 0.2 collective-permute-done.7.refs_1_
  75.7 1.2 collective-permute-done.8.refs_2_
  76.9 1.7 collective-permute-done.9.refs_3_
  78.7 37.2 %shard_map.61 = f32[1,1024]{1,0:T(1,128)S(1)} custom-call(f32[1,4096]{1,0:T(1,128)S(1)} %get-tuple-element.16.refs_0_, f32[1,4096]{1,0:T(1,128)S(1)} %collective-permute-done.7.refs_1_, f32[1,4096]{1,0:T(1,128)S(1)} %collective-permute-done.8.refs_2_, f32[1,4096]{1,0:T(1,128)S(1)} %collective-permute-done.9.refs_3_, ...), custom_call_target="tpu_custom_call" | custom-call | tf_op jit(solution)/shard_map/pallas_call | solution.py:344
  115.9 0.1 collective-permute-start.10
  115.9 1.2 collective-permute-done.10
  117.1 0.1 collective-permute-start.11
  117.2 0.7 collective-permute-start.12
  117.9 3.6 %collective-permute-start.13 = (f32[1,1024]{1,0:T(1,128)S(1)}, f32[1,1024]{1,0:T(1,128)S(1)}, u32[]{:S(2)}, u32[]{:S(2)}) collective-permute-start(f32[1,1024]{1,0:T(1,128)S(1)} %multiply_add_fusion.refs_0_), channel_id=1, source_target_pairs={{0,6},{1,7},{2,4},{3,5},{4,2},{5,3},{6,0},{7,1},{8,14},{9,15},{10,... | collective-permute-start | bytes 12296 | tf_op jit(solution)/shard_map/ppermute | solution.py:281
  121.6 0.0 collective-permute-done.11.refs_1_
  121.6 0.2 collective-permute-done.12.refs_2_
  121.8 1.6 collective-permute-done.13.refs_3_
  123.4 27.7 %shard_map.62 = (f32[1,4096]{1,0:T(1,128)S(1)}, f32[1,1024]{1,0:T(1,128)S(1)}) custom-call(f32[1,1024]{1,0:T(1,128)S(1)} %multiply_add_fusion.refs_0_, f32[1,1024]{1,0:T(1,128)S(1)} %collective-permute-done.11.refs_1_, f32[1,1024]{1,0:T(1,128)S(1)} %collective-permute-done.12.refs_2_, f32[1,1024]{1,0:T(1,128)S(1)} %collective-permute-done.13.refs_3_, ...), custom_call_target="tpu_custom_call" | custom-call | tf_op jit(solution)/shard_map/pallas_call | solution.py:333
  151.0 1.6 collective-permute-start.14
  152.6 0.5 collective-permute-start.15
  153.1 1.5 collective-permute-start.16
  154.6 0.4 collective-permute-done.14.refs_1_
  155.0 1.3 collective-permute-done.15.refs_2_
  156.3 1.4 collective-permute-done.16.refs_3_
  157.8 37.9 %shard_map.63 = (f32[1,1024]{1,0:T(1,128)S(1)}, f32[1,4096]{1,0:T(1,128)}) custom-call(f32[1,4096]{1,0:T(1,128)S(1)} %get-tuple-element.18.refs_0_, f32[1,4096]{1,0:T(1,128)S(1)} %collective-permute-done.14.refs_1_, f32[1,4096]{1,0:T(1,128)S(1)} %collective-permute-done.15.refs_2_, f32[1,4096]{1,0:T(1,128)S(1)} %collective-permute-done.16.refs_3_, ...), custom_call_target="tpu_custom_call" | custom-call | tf_op jit(solution)/shard_map/pallas_call | solution.py:354
  195.7 0.0 collective-permute-start.17
  195.7 1.1 collective-permute-done.17
  196.9 0.4 collective-permute-start.18
  197.2 3.8 %collective-permute-start.19 = (f32[1,1024]{1,0:T(1,128)S(1)}, f32[1,1024]{1,0:T(1,128)S(1)}, u32[]{:S(2)}, u32[]{:S(2)}) collective-permute-start(f32[1,1024]{1,0:T(1,128)S(1)} %add.32), channel_id=1, source_target_pairs={{0,4},{1,5},{2,6},{3,7},{4,0},{5,1},{6,2},{7,3},{8,12},{9,13},{10,... | collective-permute-start | bytes 12296 | tf_op jit(solution)/shard_map/ppermute | solution.py:281
  201.0 0.3 collective-permute-start.20
  201.3 0.6 add.31
  201.9 0.0 collective-permute-done.18
  201.9 0.7 collective-permute-done.19
  202.6 3.8 %collective-permute-done.20 = f32[1,1024]{1,0:T(1,128)S(1)} collective-permute-done((f32[1,1024]{1,0:T(1,128)S(1)}, f32[1,1024]{1,0:T(1,128)S(1)}, u32[]{:S(2)}, u32[]{:S(2)}) %collective-permute-start.20) | collective-permute-done | bytes 4128 | tf_op jit(solution)/shard_map/ppermute | solution.py:281
  206.4 0.6 add_multiply_fusion
  (5 shorter events, 0.1 us)
Async XLA Ops:
  0.6 7.2 %collective-permute-start = (f32[8,4096]{1,0:T(8,128)}, f32[8,4096]{1,0:T(8,128)S(1)}, u32[]{:S(2)}, u32[]{:S(2)}) collective-permute-start(f32[8,4096]{1,0:T(8,128)} %refs_2_.1), channel_id=1, source_target_pairs={{0,8},{8,0},{16,24},{24,16},{1,9},{9,1},{17,25},{25,17},{2,10},{10... | collective-permute-start | bytes 393224 | tf_op jit(solution)/shard_map/ppermute | solution.py:281
  3.6 8.0 %collective-permute-start.1 = (f32[8,4096]{1,0:T(8,128)}, f32[8,4096]{1,0:T(8,128)S(1)}, u32[]{:S(2)}, u32[]{:S(2)}) collective-permute-start(f32[8,4096]{1,0:T(8,128)} %refs_2_.1), channel_id=1, source_target_pairs={{0,16},{8,24},{16,0},{24,8},{1,17},{9,25},{17,1},{25,9},{2,18},{10... | collective-permute-start | bytes 393224 | tf_op jit(solution)/shard_map/ppermute | solution.py:281
  5.2 6.5 %collective-permute-start.2 = (f32[8,4096]{1,0:T(8,128)}, f32[8,4096]{1,0:T(8,128)S(1)}, u32[]{:S(2)}, u32[]{:S(2)}) collective-permute-start(f32[8,4096]{1,0:T(8,128)} %refs_2_.1), channel_id=1, source_target_pairs={{0,24},{8,16},{16,8},{24,0},{1,25},{9,17},{17,9},{25,1},{2,26},{10... | collective-permute-start | bytes 393224 | tf_op jit(solution)/shard_map/ppermute | solution.py:281
  5.2 0.9 copy-start
  11.6 0.9 copy-start.1
  12.5 0.7 copy-start.2
  32.8 1.2 collective-permute-start.3
  34.0 4.5 %collective-permute-start.4 = (f32[1,1024]{1,0:T(1,128)S(1)}, f32[1,1024]{1,0:T(1,128)S(1)}, u32[]{:S(2)}, u32[]{:S(2)}) collective-permute-start(f32[1,1024]{1,0:T(1,128)S(1)} %multiply_add_fusion.1.refs_0_), channel_id=1, source_target_pairs={{0,2},{1,3},{2,0},{3,1},{4,6},{5,7},{6,4},{7,5},{8,10},{9,11},{10,... | collective-permute-start | bytes 12296 | tf_op jit(solution)/shard_map/ppermute | solution.py:281
  35.7 4.5 %collective-permute-start.5 = (f32[1,1024]{1,0:T(1,128)S(1)}, f32[1,1024]{1,0:T(1,128)S(1)}, u32[]{:S(2)}, u32[]{:S(2)}) collective-permute-start(f32[1,1024]{1,0:T(1,128)S(1)} %multiply_add_fusion.1.refs_0_), channel_id=1, source_target_pairs={{0,4},{1,5},{2,6},{3,7},{4,0},{5,1},{6,2},{7,3},{8,12},{9,13},{10,... | collective-permute-start | bytes 12296 | tf_op jit(solution)/shard_map/ppermute | solution.py:281
  38.3 5.4 %collective-permute-start.6 = (f32[1,1024]{1,0:T(1,128)S(1)}, f32[1,1024]{1,0:T(1,128)S(1)}, u32[]{:S(2)}, u32[]{:S(2)}) collective-permute-start(f32[1,1024]{1,0:T(1,128)S(1)} %multiply_add_fusion.1.refs_0_), channel_id=1, source_target_pairs={{0,6},{1,7},{2,4},{3,5},{4,2},{5,3},{6,0},{7,1},{8,14},{9,15},{10,... | collective-permute-start | bytes 12296 | tf_op jit(solution)/shard_map/ppermute | solution.py:281
  72.0 3.7 %collective-permute-start.7 = (f32[1,4096]{1,0:T(1,128)S(1)}, f32[1,4096]{1,0:T(1,128)S(1)}, u32[]{:S(2)}, u32[]{:S(2)}) collective-permute-start(f32[1,4096]{1,0:T(1,128)S(1)} %get-tuple-element.16.refs_0_), channel_id=1, source_target_pairs={{0,8},{8,0},{16,24},{24,16},{1,9},{9,1},{17,25},{25,17},{2,10},{10... | collective-permute-start | bytes 49160 | tf_op jit(solution)/shard_map/ppermute | solution.py:281
  73.2 3.7 %collective-permute-start.8 = (f32[1,4096]{1,0:T(1,128)S(1)}, f32[1,4096]{1,0:T(1,128)S(1)}, u32[]{:S(2)}, u32[]{:S(2)}) collective-permute-start(f32[1,4096]{1,0:T(1,128)S(1)} %get-tuple-element.16.refs_0_), channel_id=1, source_target_pairs={{0,16},{8,24},{16,0},{24,8},{1,17},{9,25},{17,1},{25,9},{2,18},{10... | collective-permute-start | bytes 49160 | tf_op jit(solution)/shard_map/ppermute | solution.py:281
  74.0 4.6 %collective-permute-start.9 = (f32[1,4096]{1,0:T(1,128)S(1)}, f32[1,4096]{1,0:T(1,128)S(1)}, u32[]{:S(2)}, u32[]{:S(2)}) collective-permute-start(f32[1,4096]{1,0:T(1,128)S(1)} %get-tuple-element.16.refs_0_), channel_id=1, source_target_pairs={{0,24},{8,16},{16,8},{24,0},{1,25},{9,17},{17,9},{25,1},{2,26},{10... | collective-permute-start | bytes 49160 | tf_op jit(solution)/shard_map/ppermute | solution.py:281
  115.9 1.2 collective-permute-start.10
  117.1 4.5 %collective-permute-start.11 = (f32[1,1024]{1,0:T(1,128)S(1)}, f32[1,1024]{1,0:T(1,128)S(1)}, u32[]{:S(2)}, u32[]{:S(2)}) collective-permute-start(f32[1,1024]{1,0:T(1,128)S(1)} %multiply_add_fusion.refs_0_), channel_id=1, source_target_pairs={{0,2},{1,3},{2,0},{3,1},{4,6},{5,7},{6,4},{7,5},{8,10},{9,11},{10,... | collective-permute-start | bytes 12296 | tf_op jit(solution)/shard_map/ppermute | solution.py:281
  117.2 4.6 %collective-permute-start.12 = (f32[1,1024]{1,0:T(1,128)S(1)}, f32[1,1024]{1,0:T(1,128)S(1)}, u32[]{:S(2)}, u32[]{:S(2)}) collective-permute-start(f32[1,1024]{1,0:T(1,128)S(1)} %multiply_add_fusion.refs_0_), channel_id=1, source_target_pairs={{0,4},{1,5},{2,6},{3,7},{4,0},{5,1},{6,2},{7,3},{8,12},{9,13},{10,... | collective-permute-start | bytes 12296 | tf_op jit(solution)/shard_map/ppermute | solution.py:281
  117.9 5.4 %collective-permute-start.13 = (f32[1,1024]{1,0:T(1,128)S(1)}, f32[1,1024]{1,0:T(1,128)S(1)}, u32[]{:S(2)}, u32[]{:S(2)}) collective-permute-start(f32[1,1024]{1,0:T(1,128)S(1)} %multiply_add_fusion.refs_0_), channel_id=1, source_target_pairs={{0,6},{1,7},{2,4},{3,5},{4,2},{5,3},{6,0},{7,1},{8,14},{9,15},{10,... | collective-permute-start | bytes 12296 | tf_op jit(solution)/shard_map/ppermute | solution.py:281
  151.0 4.0 %collective-permute-start.14 = (f32[1,4096]{1,0:T(1,128)S(1)}, f32[1,4096]{1,0:T(1,128)S(1)}, u32[]{:S(2)}, u32[]{:S(2)}) collective-permute-start(f32[1,4096]{1,0:T(1,128)S(1)} %get-tuple-element.18.refs_0_), channel_id=1, source_target_pairs={{0,8},{8,0},{16,24},{24,16},{1,9},{9,1},{17,25},{25,17},{2,10},{10... | collective-permute-start | bytes 49160 | tf_op jit(solution)/shard_map/ppermute | solution.py:281
  152.6 3.7 %collective-permute-start.15 = (f32[1,4096]{1,0:T(1,128)S(1)}, f32[1,4096]{1,0:T(1,128)S(1)}, u32[]{:S(2)}, u32[]{:S(2)}) collective-permute-start(f32[1,4096]{1,0:T(1,128)S(1)} %get-tuple-element.18.refs_0_), channel_id=1, source_target_pairs={{0,16},{8,24},{16,0},{24,8},{1,17},{9,25},{17,1},{25,9},{2,18},{10... | collective-permute-start | bytes 49160 | tf_op jit(solution)/shard_map/ppermute | solution.py:281
  153.1 4.6 %collective-permute-start.16 = (f32[1,4096]{1,0:T(1,128)S(1)}, f32[1,4096]{1,0:T(1,128)S(1)}, u32[]{:S(2)}, u32[]{:S(2)}) collective-permute-start(f32[1,4096]{1,0:T(1,128)S(1)} %get-tuple-element.18.refs_0_), channel_id=1, source_target_pairs={{0,24},{8,16},{16,8},{24,0},{1,25},{9,17},{17,9},{25,1},{2,26},{10... | collective-permute-start | bytes 49160 | tf_op jit(solution)/shard_map/ppermute | solution.py:281
  195.7 1.2 collective-permute-start.17
  196.9 5.0 %collective-permute-start.18 = (f32[1,1024]{1,0:T(1,128)S(1)}, f32[1,1024]{1,0:T(1,128)S(1)}, u32[]{:S(2)}, u32[]{:S(2)}) collective-permute-start(f32[1,1024]{1,0:T(1,128)S(1)} %add.32), channel_id=1, source_target_pairs={{0,2},{1,3},{2,0},{3,1},{4,6},{5,7},{6,4},{7,5},{8,10},{9,11},{10,... | collective-permute-start | bytes 12296 | tf_op jit(solution)/shard_map/ppermute | solution.py:281
  197.2 5.3 %collective-permute-start.19 = (f32[1,1024]{1,0:T(1,128)S(1)}, f32[1,1024]{1,0:T(1,128)S(1)}, u32[]{:S(2)}, u32[]{:S(2)}) collective-permute-start(f32[1,1024]{1,0:T(1,128)S(1)} %add.32), channel_id=1, source_target_pairs={{0,4},{1,5},{2,6},{3,7},{4,0},{5,1},{6,2},{7,3},{8,12},{9,13},{10,... | collective-permute-start | bytes 12296 | tf_op jit(solution)/shard_map/ppermute | solution.py:281
  201.0 5.4 %collective-permute-start.20 = (f32[1,1024]{1,0:T(1,128)S(1)}, f32[1,1024]{1,0:T(1,128)S(1)}, u32[]{:S(2)}, u32[]{:S(2)}) collective-permute-start(f32[1,1024]{1,0:T(1,128)S(1)} %add.32), channel_id=1, source_target_pairs={{0,6},{1,7},{2,4},{3,5},{4,2},{5,3},{6,0},{7,1},{8,14},{9,15},{10,... | collective-permute-start | bytes 12296 | tf_op jit(solution)/shard_map/ppermute | solution.py:281

commit v3 on v2

--- a/solution.py
+++ b/solution.py
@@ -11,8 +11,8 @@
 epsilon = 0.05
 KAPPA = math.log2(math.e) / epsilon
 LANES = 128
-ROW_BLOCK = 256
-COL_BLOCK = 512
+ROW_BLOCK = 512
+COL_BLOCK = 256
 
 f32 = jnp.float32
 bf16 = jnp.bfloat16
@@ -66,7 +66,9 @@
     return range(0, width, LANES)
 
 
-def prepare_rows(n_src, src_ref, a_ref):
+def prepare(n_src, src_ref, t_ref, g_ref, a_ref, own_ref, start_ref):
+    own_ref[...] = t_ref[...]
+    start_ref[...] = g_ref[...]
     dims, rows = src_ref.shape
     if n_src == 4:
         me, each = lax.axis_index("src"), dims // n_src
@@ -96,47 +98,54 @@
     fill = jnp.zeros((13, cols), f32)
     b_ref[6 * dims :, :] = jnp.concatenate([o1, o2, o3, fill], axis=0).astype(bf16)
 
-    def run(columns):
-        for row in range(0, rows, ROW_BLOCK):
-
-            def top(i, best):
-                s = scores(a_ref, b_ref, row, ROW_BLOCK, pl.multiple_of(i * COL_BLOCK, COL_BLOCK), COL_BLOCK)
-                for t in tiles(COL_BLOCK):
-                    best = jnp.maximum(best, s[:, t : t + LANES])
-                return best
-
-            best = lax.fori_loop(0, columns // COL_BLOCK, top, jnp.full((ROW_BLOCK, LANES), -jnp.inf, f32))
-            shift_ref[row : row + ROW_BLOCK, :] = jnp.broadcast_to(
-                jnp.max(best, axis=1, keepdims=True), (ROW_BLOCK, LANES)
-            )
-        acc_ref[...] = jnp.zeros_like(acc_ref)
-
-        def block(i, _):
-            col = pl.multiple_of(i * COL_BLOCK, COL_BLOCK)
-            for row in range(0, rows, ROW_BLOCK):
+    def block(i, wide):
+        row = pl.multiple_of(i * ROW_BLOCK, ROW_BLOCK)
+        here = pl.ds(row, ROW_BLOCK)
+
+        def top(col):
+            s = scores(a_ref, b_ref, row, ROW_BLOCK, col, COL_BLOCK)
+            return s, functools.reduce(jnp.maximum, [s[:, t : t + LANES] for t in tiles(COL_BLOCK)])
+
+        def spread(best):
+            return jnp.broadcast_to(jnp.max(best, axis=1, keepdims=True), best.shape)
+
+        if wide:
+            best = lax.fori_loop(
+                1,
+                cols // COL_BLOCK,
+                lambda c, best: jnp.maximum(best, top(pl.multiple_of(c * COL_BLOCK, COL_BLOCK))[1]),
+                top(0)[1],
+            )
+            shift_ref[here, :] = spread(best)
+        for col in range(0, cols, COL_BLOCK):
+            if col == 0 and not wide:
+                s, best = top(0)
+                shift = spread(best)
+                shift_ref[here, :] = shift
+            else:
                 s = scores(a_ref, b_ref, row, ROW_BLOCK, col, COL_BLOCK)
-                shift = shift_ref[row : row + ROW_BLOCK, :]
-                acc = acc_ref[row : row + ROW_BLOCK, :]
-                for t in tiles(COL_BLOCK):
-                    e = jnp.exp2(s[:, t : t + LANES] - shift)
-                    e_ref[row : row + ROW_BLOCK, pl.ds(pl.multiple_of(col + t, LANES), LANES)] = e
-                    acc = acc + e
-                acc_ref[row : row + ROW_BLOCK, :] = acc
-            return 0
-
-        lax.fori_loop(0, cols // COL_BLOCK, block, 0)
+                shift = shift_ref[here, :]
+            acc = acc_ref[here, :] if col else 0.0
+            for t in tiles(COL_BLOCK):
+                e = jnp.exp2(s[:, t : t + LANES] - shift)
+                e_ref[here, col + t : col + t + LANES] = e
+                acc = acc + e
+            acc_ref[here, :] = acc
+
+    def run(wide):
+        lax.fori_loop(0, rows // ROW_BLOCK, lambda i, _: block(i, wide), None)
         total = to_lanes(acc_ref[...], jnp.sum)
         shift = to_lanes(shift_ref[...], jnp.max)
         m_ref[...] = shift
         rho_ref[...] = shift + jnp.log2(total)
         return total
 
-    total = run(COL_BLOCK)
+    total = run(False)
     fine = jnp.max(total) < 2.0**100
 
     @pl.when(jnp.logical_not(fine))
     def _():
-        run(cols)
+        run(True)
 
 
 def column_sums(e_ref, u_ref, q_ref):
@@ -179,10 +188,11 @@
 
 def column_pass(n_parts, log_nt, *refs):
     parts = refs[:n_parts]
-    m_ref, e_ref, a_ref, b_ref, lam_ref, f_ref, u_ref, q_ref = refs[n_parts:]
+    m_ref, e_ref, a_ref, b_ref, lam_ref, *f_ref, u_ref, q_ref = refs[n_parts:]
     rows, cols = e_ref.shape
     pot = log_nt - lse2([ref[...] for ref in parts])
-    f_ref[...] = pot
+    for ref in f_ref:
+        ref[...] = pot
     power = pot + m_ref[...]
     u = jnp.exp2(power)
     u_ref[...] = to_rows(u)
@@ -306,18 +316,18 @@
     depth = 6 * dims + 16
     row, col, square = vmem((1, rows)), vmem((1, cols)), vmem((rows, LANES))
 
+    g = g_init.reshape(1, cols)
+    a, own, g = pl.pallas_call(
+        functools.partial(prepare, n_src),
+        out_shape=(vmem((rows, depth), bf16), vmem(target_points.shape), col),
+        in_specs=[VMEM] * 3,
+        out_specs=(VMEM,) * 3,
+        compiler_params=PARAMS,
+    )(source_points, target_points, g)
     if n_src == 4:
-        blocks = pool_src(target_points)
+        blocks = [own] + others(target_points, "src", n_src, (1, 2, 3))
     else:
         blocks = [lax.all_gather(target_points, "src", axis=0, tiled=True)]
-    a = pl.pallas_call(
-        functools.partial(prepare_rows, n_src),
-        out_shape=vmem((rows, depth), bf16),
-        in_specs=[VMEM],
-        out_specs=VMEM,
-        compiler_params=PARAMS,
-    )(source_points)
-    g = g_init.reshape(1, cols)
     e, b, rho, m = pl.pallas_call(
         functools.partial(build, len(blocks)),
         out_shape=(vmem((rows, cols)), vmem((depth, cols), bf16), row, row),
@@ -325,21 +335,21 @@
         out_specs=(VMEM,) * 4,
         scratch_shapes=[square, square],
         compiler_params=PARAMS,
-    )(pin(a), g, *map(pin, blocks))
-    a, e, b, m = pin(a), pin(e), pin(b), pin(m)
-
-    def columns(rho):
+    )(pin(a), pin(g), *map(pin, blocks))
+    a, e, b, m, g = pin(a), pin(e), pin(b), pin(m), pin(g)
+
+    def columns(rho, outs):
         parts = pool_tgt(rho, lse2)
         return pl.pallas_call(
             functools.partial(column_pass, len(parts), log_nt),
-            out_shape=(col, row),
+            out_shape=outs,
             in_specs=[VMEM] * (len(parts) + 4),
-            out_specs=(VMEM, VMEM),
+            out_specs=(VMEM,) * len(outs),
             scratch_shapes=[square, col],
             compiler_params=PARAMS,
         )(*map(pin, parts), m, e, a, b)
 
-    lam, _ = columns(rho)
+    (lam,) = columns(rho, (col,))
     parts = pool_src(lam)
     rho = pl.pallas_call(
         functools.partial(row_pass, len(parts), log_ns),
@@ -349,11 +359,11 @@
         scratch_shapes=[col, square],
         compiler_params=PARAMS,
     )(*map(pin, parts), m, e, a, b)
-    lam, f = columns(rho)
+    lam, f = columns(rho, (col, row))
     parts = pool_src(lam)
     total, g_pot = pl.pallas_call(
         functools.partial(marginal_pass, len(parts), log_ns),
-        out_shape=(row, jax.ShapeDtypeStruct((1, cols), f32)),
+        out_shape=(row, col),
         in_specs=[VMEM] * (len(parts) + 6),
         out_specs=(VMEM, VMEM),
         scratch_shapes=[row, col, square],

time: 207 us -> 300 us (1.45)
  Pallas kernels: 151 us -> 245 us
    pallas_call x2, Pallas kernels: 56 us -> 97.6 us  [columns(): pl.pallas_call(functools.partial(column_pass, len(parts), log_nt), out_sh...]
    pallas_call x1, Pallas kernels: 37.2 us -> 66.4 us  [body(): pl.pallas_call(functools.partial(row_pass, len(parts), log_ns), out_shape...]
    pallas_call x1, Pallas kernels: 37.9 us -> 66.4 us  [body(): pl.pallas_call(functools.partial(marginal_pass, len(parts), log_ns), out_...]
    pallas_call x1, Pallas kernels: 19.5 us -> 13.9 us  [body(): pl.pallas_call(functools.partial(build, len(blocks)), out_shape=(vmem((ro...]
  transfers between devices with their start and end apart: 21 -> 21, of which waited for: 17 -> 16; matrix products, arithmetic and copies ran while one was open for 0% -> 0% of each run, Pallas kernels for 0% -> 0%
where the time goes in v3:
time: 300 us; the launch traced here: 299 us
  Pallas kernels  245 us (82%)
  starting transfers between devices  25.1 us (8%)
  waiting for transfers between devices  24.4 us (8%)
  local copies, waits for them, and re-layouts  3.13 us (1%)
    pallas_call x2, Pallas kernels, columns(): pl.pallas_call(functools.partial(column_pass, len(parts), log_nt), out_sh...  97.6 us
    pallas_call x1, Pallas kernels, body(): pl.pallas_call(functools.partial(marginal_pass, len(parts), log_ns), out_...  66.4 us
    pallas_call x1, Pallas kernels, body(): pl.pallas_call(functools.partial(row_pass, len(parts), log_ns), out_shape...  66.4 us
    ppermute x21, starting transfers between devices, others(): lax.ppermute(x, axis, [(i, i ^ k) for i in range(size)])  25.1 us
    ppermute x21, waiting for transfers between devices, others(): lax.ppermute(x, axis, [(i, i ^ k) for i in range(size)])  24.4 us
    pallas_call x1, Pallas kernels, body(): pl.pallas_call(functools.partial(build, len(blocks)), out_shape=(vmem((ro...  13.9 us
  transfers between devices with their start and end apart: 21, of which 16 were waited for; matrix products, arithmetic and copies ran while one was open for 0% of the time, Pallas kernels for 0%

profile of v3, /device:TPU:0, one launch (start us, length us, event | category | flops | bytes accessed | tf_op | source)
XLA Modules:
  0.0 299.3 jit_solution(15592043163265763020)
XLA Ops:
  0.6 3.0 %collective-permute-start = (f32[8,4096]{1,0:T(8,128)}, f32[8,4096]{1,0:T(8,128)S(1)}, u32[]{:S(2)}, u32[]{:S(2)}) collective-permute-start(f32[8,4096]{1,0:T(8,128)} %t_ref.1), channel_id=1, source_target_pairs={{0,8},{8,0},{16,24},{24,16},{1,9},{9,1},{17,25},{25,17},{2,10},{10... | collective-permute-start | bytes 393224 | tf_op jit(solution)/shard_map/ppermute | solution.py:291
  3.6 1.5 collective-permute-start.1
  5.2 0.0 collective-permute-start.2
  5.2 0.0 copy-start
  5.2 0.9 copy-done
  6.1 0.0 copy-start.1
  6.1 0.9 copy-done.1
  7.0 0.0 copy-start.2
  7.0 0.7 copy-done.2
  7.7 0.2 shard_map.58
  7.9 0.0 collective-permute-done.refs_3_
  7.9 3.7 %collective-permute-done.1.refs_4_ = f32[8,4096]{1,0:T(8,128)S(1)} collective-permute-done((f32[8,4096]{1,0:T(8,128)}, f32[8,4096]{1,0:T(8,128)S(1)}, u32[]{:S(2)}, u32[]{:S(2)}) %collective-permute-start.1) | collective-permute-done | bytes 131104 | tf_op jit(solution)/shard_map/ppermute | solution.py:291
  11.6 0.0 collective-permute-done.2.refs_5_
  11.6 13.9 %shard_map.59 = (f32[1024,4096]{1,0:T(8,128)S(1)}, bf16[208,4096]{1,0:T(8,128)(2,1)S(1)}, f32[1,1024]{1,0:T(1,128)S(1)}, f32[1,1024]{1,0:T(1,128)S(1)}) custom-call(bf16[1024,208]{1,0:T(8,128)(2,1)S(1)} %get-tuple-element.14.refs_0_.refs_6_, f32[1,4096]{1,0:T(1,128)S(1)} %get-tuple-element.15.refs_1_.refs_9_, f32[8,4096]{1,0:T(8,128)S(1)} %get-tuple-element.16.refs_2_, ...), custom_call_target="tpu_custom_call" | custom-call | tf_op jit(solution)/shard_map/pallas_call | solution.py:331
  25.6 0.1 collective-permute-start.3
  25.7 1.2 collective-permute-done.3
  26.8 1.6 collective-permute-start.4
  28.5 2.6 collective-permute-start.5
  31.1 0.2 collective-permute-start.6
  31.3 0.0 collective-permute-done.4.refs_1_
  31.3 1.7 collective-permute-done.5.refs_2_
  33.0 3.5 %collective-permute-done.6.refs_3_ = f32[1,1024]{1,0:T(1,128)S(1)} collective-permute-done((f32[1,1024]{1,0:T(1,128)S(1)}, f32[1,1024]{1,0:T(1,128)S(1)}, u32[]{:S(2)}, u32[]{:S(2)}) %collective-permute-start.6) | collective-permute-done | bytes 4128 | tf_op jit(solution)/shard_map/ppermute | solution.py:291
  36.5 48.8 %shard_map.60.refs_0_ = f32[1,4096]{1,0:T(1,128)S(1)} custom-call(f32[1,1024]{1,0:T(1,128)S(1)} %multiply_add_fusion.1.refs_0_, f32[1,1024]{1,0:T(1,128)S(1)} %collective-permute-done.4.refs_1_, f32[1,1024]{1,0:T(1,128)S(1)} %collective-permute-done.5.refs_2_, f32[1,1024]{1,0:T(1,128)S(1)} %collective-permute-done.6.refs_3_, ...), custom_call_target="tpu_custom_call" | custom-call | tf_op jit(solution)/shard_map/pallas_call | solution.py:343
  85.3 1.3 collective-permute-start.7
  86.6 0.8 collective-permute-start.8
  87.4 1.4 collective-permute-start.9
  88.8 0.2 collective-permute-done.7.refs_1_
  89.1 1.2 collective-permute-done.8.refs_2_
  90.3 1.7 collective-permute-done.9.refs_3_
  92.0 66.4 %shard_map.61 = f32[1,1024]{1,0:T(1,128)S(1)} custom-call(f32[1,4096]{1,0:T(1,128)S(1)} %shard_map.60.refs_0_, f32[1,4096]{1,0:T(1,128)S(1)} %collective-permute-done.7.refs_1_, f32[1,4096]{1,0:T(1,128)S(1)} %collective-permute-done.8.refs_2_, f32[1,4096]{1,0:T(1,128)S(1)} %collective-permute-done.9.refs_3_, f32[1,1024]{1,0:T(1,128)S(1)} %get-tuple-element.18.refs_4_, ...), custom_call_target="tpu_custom_call" | custom-call | tf_op jit(solution)/shard_map/pallas_call | solution.py:354
  158.4 0.1 collective-permute-start.10
  158.5 1.2 collective-permute-done.10
  159.7 0.1 collective-permute-start.11
  159.8 0.8 collective-permute-start.12
  160.5 3.6 %collective-permute-start.13 = (f32[1,1024]{1,0:T(1,128)S(1)}, f32[1,1024]{1,0:T(1,128)S(1)}, u32[]{:S(2)}, u32[]{:S(2)}) collective-permute-start(f32[1,1024]{1,0:T(1,128)S(1)} %multiply_add_fusion.refs_0_), channel_id=1, source_target_pairs={{0,6},{1,7},{2,4},{3,5},{4,2},{5,3},{6,0},{7,1},{8,14},{9,15},{10,... | collective-permute-start | bytes 12296 | tf_op jit(solution)/shard_map/ppermute | solution.py:291
  164.1 0.0 collective-permute-done.11.refs_1_
  164.2 0.2 collective-permute-done.12.refs_2_
  164.3 1.6 collective-permute-done.13.refs_3_
  165.9 48.8 %shard_map.62 = (f32[1,4096]{1,0:T(1,128)S(1)}, f32[1,1024]{1,0:T(1,128)S(1)}) custom-call(f32[1,1024]{1,0:T(1,128)S(1)} %multiply_add_fusion.refs_0_, f32[1,1024]{1,0:T(1,128)S(1)} %collective-permute-done.11.refs_1_, f32[1,1024]{1,0:T(1,128)S(1)} %collective-permute-done.12.refs_2_, f32[1,1024]{1,0:T(1,128)S(1)} %collective-permute-done.13.refs_3_, ...), custom_call_target="tpu_custom_call" | custom-call | tf_op jit(solution)/shard_map/pallas_call | solution.py:343
  214.8 1.6 collective-permute-start.14
  216.3 0.5 collective-permute-start.15
  216.9 1.5 collective-permute-start.16
  218.3 0.4 collective-permute-done.14.refs_1_
  218.7 1.3 collective-permute-done.15.refs_2_
  220.1 1.4 collective-permute-done.16.refs_3_
  221.5 66.4 %shard_map.63 = (f32[1,1024]{1,0:T(1,128)S(1)}, f32[1,4096]{1,0:T(1,128)S(1)}) custom-call(f32[1,4096]{1,0:T(1,128)S(1)} %get-tuple-element.22.refs_0_, f32[1,4096]{1,0:T(1,128)S(1)} %collective-permute-done.14.refs_1_, f32[1,4096]{1,0:T(1,128)S(1)} %collective-permute-done.15.refs_2_, f32[1,4096]{1,0:T(1,128)S(1)} %collective-permute-done.16.refs_3_, ...), custom_call_target="tpu_custom_call" | custom-call | tf_op jit(solution)/shard_map/pallas_call | solution.py:364
  287.9 0.1 collective-permute-start.17
  288.0 1.1 collective-permute-done.17
  289.1 0.3 collective-permute-start.18
  289.5 3.8 %collective-permute-start.19 = (f32[1,1024]{1,0:T(1,128)S(1)}, f32[1,1024]{1,0:T(1,128)S(1)}, u32[]{:S(2)}, u32[]{:S(2)}) collective-permute-start(f32[1,1024]{1,0:T(1,128)S(1)} %add.32), channel_id=1, source_target_pairs={{0,4},{1,5},{2,6},{3,7},{4,0},{5,1},{6,2},{7,3},{8,12},{9,13},{10,... | collective-permute-start | bytes 12296 | tf_op jit(solution)/shard_map/ppermute | solution.py:291
  293.3 0.2 collective-permute-start.20
  293.5 0.6 add.31
  294.1 0.6 copy.6
  294.7 0.0 collective-permute-done.18
  294.7 0.1 collective-permute-done.19
  294.9 3.8 %collective-permute-done.20 = f32[1,1024]{1,0:T(1,128)S(1)} collective-permute-done((f32[1,1024]{1,0:T(1,128)S(1)}, f32[1,1024]{1,0:T(1,128)S(1)}, u32[]{:S(2)}, u32[]{:S(2)}) %collective-permute-start.20) | collective-permute-done | bytes 4128 | tf_op jit(solution)/shard_map/ppermute | solution.py:291
  298.7 0.6 add_multiply_fusion
  (5 shorter events, 0.1 us)
Async XLA Ops:
  0.6 7.3 %collective-permute-start = (f32[8,4096]{1,0:T(8,128)}, f32[8,4096]{1,0:T(8,128)S(1)}, u32[]{:S(2)}, u32[]{:S(2)}) collective-permute-start(f32[8,4096]{1,0:T(8,128)} %t_ref.1), channel_id=1, source_target_pairs={{0,8},{8,0},{16,24},{24,16},{1,9},{9,1},{17,25},{25,17},{2,10},{10... | collective-permute-start | bytes 393224 | tf_op jit(solution)/shard_map/ppermute | solution.py:291
  3.6 8.0 %collective-permute-start.1 = (f32[8,4096]{1,0:T(8,128)}, f32[8,4096]{1,0:T(8,128)S(1)}, u32[]{:S(2)}, u32[]{:S(2)}) collective-permute-start(f32[8,4096]{1,0:T(8,128)} %t_ref.1), channel_id=1, source_target_pairs={{0,16},{8,24},{16,0},{24,8},{1,17},{9,25},{17,1},{25,9},{2,18},{10... | collective-permute-start | bytes 393224 | tf_op jit(solution)/shard_map/ppermute | solution.py:291
  5.2 6.5 %collective-permute-start.2 = (f32[8,4096]{1,0:T(8,128)}, f32[8,4096]{1,0:T(8,128)S(1)}, u32[]{:S(2)}, u32[]{:S(2)}) collective-permute-start(f32[8,4096]{1,0:T(8,128)} %t_ref.1), channel_id=1, source_target_pairs={{0,24},{8,16},{16,8},{24,0},{1,25},{9,17},{17,9},{25,1},{2,26},{10... | collective-permute-start | bytes 393224 | tf_op jit(solution)/shard_map/ppermute | solution.py:291
  5.2 0.9 copy-start
  6.1 0.9 copy-start.1
  7.0 0.7 copy-start.2
  25.6 1.2 collective-permute-start.3
  26.8 4.5 %collective-permute-start.4 = (f32[1,1024]{1,0:T(1,128)S(1)}, f32[1,1024]{1,0:T(1,128)S(1)}, u32[]{:S(2)}, u32[]{:S(2)}) collective-permute-start(f32[1,1024]{1,0:T(1,128)S(1)} %multiply_add_fusion.1.refs_0_), channel_id=1, source_target_pairs={{0,2},{1,3},{2,0},{3,1},{4,6},{5,7},{6,4},{7,5},{8,10},{9,11},{10,... | collective-permute-start | bytes 12296 | tf_op jit(solution)/shard_map/ppermute | solution.py:291
  28.5 4.5 %collective-permute-start.5 = (f32[1,1024]{1,0:T(1,128)S(1)}, f32[1,1024]{1,0:T(1,128)S(1)}, u32[]{:S(2)}, u32[]{:S(2)}) collective-permute-start(f32[1,1024]{1,0:T(1,128)S(1)} %multiply_add_fusion.1.refs_0_), channel_id=1, source_target_pairs={{0,4},{1,5},{2,6},{3,7},{4,0},{5,1},{6,2},{7,3},{8,12},{9,13},{10,... | collective-permute-start | bytes 12296 | tf_op jit(solution)/shard_map/ppermute | solution.py:291
  31.1 5.4 %collective-permute-start.6 = (f32[1,1024]{1,0:T(1,128)S(1)}, f32[1,1024]{1,0:T(1,128)S(1)}, u32[]{:S(2)}, u32[]{:S(2)}) collective-permute-start(f32[1,1024]{1,0:T(1,128)S(1)} %multiply_add_fusion.1.refs_0_), channel_id=1, source_target_pairs={{0,6},{1,7},{2,4},{3,5},{4,2},{5,3},{6,0},{7,1},{8,14},{9,15},{10,... | collective-permute-start | bytes 12296 | tf_op jit(solution)/shard_map/ppermute | solution.py:291
  85.3 3.8 %collective-permute-start.7 = (f32[1,4096]{1,0:T(1,128)S(1)}, f32[1,4096]{1,0:T(1,128)S(1)}, u32[]{:S(2)}, u32[]{:S(2)}) collective-permute-start(f32[1,4096]{1,0:T(1,128)S(1)} %shard_map.60.refs_0_), channel_id=1, source_target_pairs={{0,8},{8,0},{16,24},{24,16},{1,9},{9,1},{17,25},{25,17},{2,10},{10... | collective-permute-start | bytes 49160 | tf_op jit(solution)/shard_map/ppermute | solution.py:291
  86.6 3.7 %collective-permute-start.8 = (f32[1,4096]{1,0:T(1,128)S(1)}, f32[1,4096]{1,0:T(1,128)S(1)}, u32[]{:S(2)}, u32[]{:S(2)}) collective-permute-start(f32[1,4096]{1,0:T(1,128)S(1)} %shard_map.60.refs_0_), channel_id=1, source_target_pairs={{0,16},{8,24},{16,0},{24,8},{1,17},{9,25},{17,1},{25,9},{2,18},{10... | collective-permute-start | bytes 49160 | tf_op jit(solution)/shard_map/ppermute | solution.py:291
  87.4 4.6 %collective-permute-start.9 = (f32[1,4096]{1,0:T(1,128)S(1)}, f32[1,4096]{1,0:T(1,128)S(1)}, u32[]{:S(2)}, u32[]{:S(2)}) collective-permute-start(f32[1,4096]{1,0:T(1,128)S(1)} %shard_map.60.refs_0_), channel_id=1, source_target_pairs={{0,24},{8,16},{16,8},{24,0},{1,25},{9,17},{17,9},{25,1},{2,26},{10... | collective-permute-start | bytes 49160 | tf_op jit(solution)/shard_map/ppermute | solution.py:291
  158.4 1.2 collective-permute-start.10
  159.7 4.5 %collective-permute-start.11 = (f32[1,1024]{1,0:T(1,128)S(1)}, f32[1,1024]{1,0:T(1,128)S(1)}, u32[]{:S(2)}, u32[]{:S(2)}) collective-permute-start(f32[1,1024]{1,0:T(1,128)S(1)} %multiply_add_fusion.refs_0_), channel_id=1, source_target_pairs={{0,2},{1,3},{2,0},{3,1},{4,6},{5,7},{6,4},{7,5},{8,10},{9,11},{10,... | collective-permute-start | bytes 12296 | tf_op jit(solution)/shard_map/ppermute | solution.py:291
  159.8 4.6 %collective-permute-start.12 = (f32[1,1024]{1,0:T(1,128)S(1)}, f32[1,1024]{1,0:T(1,128)S(1)}, u32[]{:S(2)}, u32[]{:S(2)}) collective-permute-start(f32[1,1024]{1,0:T(1,128)S(1)} %multiply_add_fusion.refs_0_), channel_id=1, source_target_pairs={{0,4},{1,5},{2,6},{3,7},{4,0},{5,1},{6,2},{7,3},{8,12},{9,13},{10,... | collective-permute-start | bytes 12296 | tf_op jit(solution)/shard_map/ppermute | solution.py:291
  160.5 5.4 %collective-permute-start.13 = (f32[1,1024]{1,0:T(1,128)S(1)}, f32[1,1024]{1,0:T(1,128)S(1)}, u32[]{:S(2)}, u32[]{:S(2)}) collective-permute-start(f32[1,1024]{1,0:T(1,128)S(1)} %multiply_add_fusion.refs_0_), channel_id=1, source_target_pairs={{0,6},{1,7},{2,4},{3,5},{4,2},{5,3},{6,0},{7,1},{8,14},{9,15},{10,... | collective-permute-start | bytes 12296 | tf_op jit(solution)/shard_map/ppermute | solution.py:291
  214.8 4.0 %collective-permute-start.14 = (f32[1,4096]{1,0:T(1,128)S(1)}, f32[1,4096]{1,0:T(1,128)S(1)}, u32[]{:S(2)}, u32[]{:S(2)}) collective-permute-start(f32[1,4096]{1,0:T(1,128)S(1)} %get-tuple-element.22.refs_0_), channel_id=1, source_target_pairs={{0,8},{8,0},{16,24},{24,16},{1,9},{9,1},{17,25},{25,17},{2,10},{10... | collective-permute-start | bytes 49160 | tf_op jit(solution)/shard_map/ppermute | solution.py:291
  216.3 3.7 %collective-permute-start.15 = (f32[1,4096]{1,0:T(1,128)S(1)}, f32[1,4096]{1,0:T(1,128)S(1)}, u32[]{:S(2)}, u32[]{:S(2)}) collective-permute-start(f32[1,4096]{1,0:T(1,128)S(1)} %get-tuple-element.22.refs_0_), channel_id=1, source_target_pairs={{0,16},{8,24},{16,0},{24,8},{1,17},{9,25},{17,1},{25,9},{2,18},{10... | collective-permute-start | bytes 49160 | tf_op jit(solution)/shard_map/ppermute | solution.py:291
  216.9 4.6 %collective-permute-start.16 = (f32[1,4096]{1,0:T(1,128)S(1)}, f32[1,4096]{1,0:T(1,128)S(1)}, u32[]{:S(2)}, u32[]{:S(2)}) collective-permute-start(f32[1,4096]{1,0:T(1,128)S(1)} %get-tuple-element.22.refs_0_), channel_id=1, source_target_pairs={{0,24},{8,16},{16,8},{24,0},{1,25},{9,17},{17,9},{25,1},{2,26},{10... | collective-permute-start | bytes 49160 | tf_op jit(solution)/shard_map/ppermute | solution.py:291
  287.9 1.2 collective-permute-start.17
  289.1 5.6 %collective-permute-start.18 = (f32[1,1024]{1,0:T(1,128)S(1)}, f32[1,1024]{1,0:T(1,128)S(1)}, u32[]{:S(2)}, u32[]{:S(2)}) collective-permute-start(f32[1,1024]{1,0:T(1,128)S(1)} %add.32), channel_id=1, source_target_pairs={{0,2},{1,3},{2,0},{3,1},{4,6},{5,7},{6,4},{7,5},{8,10},{9,11},{10,... | collective-permute-start | bytes 12296 | tf_op jit(solution)/shard_map/ppermute | solution.py:291
  289.5 5.4 %collective-permute-start.19 = (f32[1,1024]{1,0:T(1,128)S(1)}, f32[1,1024]{1,0:T(1,128)S(1)}, u32[]{:S(2)}, u32[]{:S(2)}) collective-permute-start(f32[1,1024]{1,0:T(1,128)S(1)} %add.32), channel_id=1, source_target_pairs={{0,4},{1,5},{2,6},{3,7},{4,0},{5,1},{6,2},{7,3},{8,12},{9,13},{10,... | collective-permute-start | bytes 12296 | tf_op jit(solution)/shard_map/ppermute | solution.py:291
  293.3 5.4 %collective-permute-start.20 = (f32[1,1024]{1,0:T(1,128)S(1)}, f32[1,1024]{1,0:T(1,128)S(1)}, u32[]{:S(2)}, u32[]{:S(2)}) collective-permute-start(f32[1,1024]{1,0:T(1,128)S(1)} %add.32), channel_id=1, source_target_pairs={{0,6},{1,7},{2,4},{3,5},{4,2},{5,3},{6,0},{7,1},{8,14},{9,15},{10,... | collective-permute-start | bytes 12296 | tf_op jit(solution)/shard_map/ppermute | solution.py:291

commit v4 on v3

v4 whole, which is shorter than its diff:
```python
import functools
import math

import jax
import jax.numpy as jnp
from jax import lax
from jax.experimental import pallas as pl
from jax.experimental.pallas import tpu as pltpu
from jax.sharding import PartitionSpec as P

epsilon = 0.05
KAPPA = math.log2(math.e) / epsilon
LANES = 128
ROW_BLOCK = 512
COL_BLOCK = 256
COL_WIDTH = 1024
ROW_HEIGHT = 128

f32 = jnp.float32
bf16 = jnp.bfloat16
VMEM = pl.BlockSpec(memory_space=pltpu.VMEM)
PARAMS = pltpu.CompilerParams(vmem_limit_bytes=16 * 2**20)


HBM = pl.BlockSpec(memory_space=pltpu.HBM)


def vmem(shape, dtype=f32):
    return pltpu.VMEM(shape, dtype)


def pin(x):
    return pltpu.with_memory_space_constraint(x, pltpu.VMEM)


def split(x):
    first = x.astype(bf16)
    rest = x - first.astype(f32)
    second = rest.astype(bf16)
    third = (rest - second.astype(f32)).astype(bf16)
    return first, second, third


def to_lanes(ref, reduce, out_ref):
    for k in range(out_ref.shape[0]):
        part = ref[k * LANES : (k + 1) * LANES, :].T
        out_ref[k : k + 1, :] = reduce(part, axis=0, keepdims=True)


def to_rows(x, out_ref):
    for k in range(x.shape[0]):
        out_ref[k * LANES : (k + 1) * LANES, :] = jnp.broadcast_to(x[k : k + 1, :], (LANES, LANES)).T


def every(*conditions):
    least = [jnp.min(jnp.where(c, 1.0, 0.0), axis=0, keepdims=True) for c in conditions]
    return jnp.min(functools.reduce(jnp.minimum, least)) > 0.5


def total_of(x):
    return jnp.sum(jnp.sum(x, axis=0, keepdims=True), axis=1, keepdims=True)


def lse2(parts):
    top = functools.reduce(jnp.maximum, parts)
    return top + jnp.log2(sum(jnp.exp2(p - top) for p in parts))


def scores(a_ref, b_ref, row, rows, col, cols):
    return jnp.dot(
        a_ref[pl.ds(row, rows), :], b_ref[:, pl.ds(col, cols)], preferred_element_type=f32
    )


def tiles(width):
    return range(0, width, LANES)


def prepare(n_src, src_ref, t_ref, g_ref, g2_ref, a_ref, own_ref, start_ref, start2_ref, square_ref):
    own_ref[...] = t_ref[...]
    start_ref[...] = g_ref[...]
    start2_ref[...] = g2_ref[...]
    dims, rows = src_ref.shape
    square = jnp.sum(src_ref[...] * src_ref[...], axis=0, keepdims=True)
    for k in range(rows // LANES):
        square_ref[k : k + 1, :] = square[:, k * LANES : (k + 1) * LANES]
    if n_src == 4:
        me, each = lax.axis_index("src"), dims // n_src
        points = jnp.concatenate(
            [src_ref[pl.ds(pl.multiple_of((me ^ k) * each, each), each), :] for k in range(n_src)],
            axis=0,
        )
    else:
        points = src_ref[...]
    s1, s2, s3 = (x.astype(f32) for x in split(points * (2.0 * KAPPA)))
    last = (lax.broadcasted_iota(jnp.int32, (16, rows), 0) < 3).astype(f32)
    a_ref[...] = jnp.concatenate([s1, s1, s2, s1, s3, s2, last], axis=0).T.astype(bf16)


def build(n_blocks, *refs):
    a_ref, g_ref = refs[:2]
    blocks = refs[2 : 2 + n_blocks]
    e_ref, b_ref, rho_ref, m_ref, acc_ref, shift_ref = refs[2 + n_blocks :]
    rows, cols = e_ref.shape
    dims = sum(ref.shape[0] for ref in blocks)
    points = jnp.concatenate([ref[...] for ref in blocks], axis=0)
    t1, t2, t3 = split(points)
    for k, part in enumerate((t1, t2, t1, t3, t1, t2)):
        b_ref[k * dims : (k + 1) * dims, :] = part
    offset = KAPPA * (g_ref[...] - jnp.sum(points * points, axis=0, keepdims=True))
    o1, o2, o3 = (x.astype(f32) for x in split(offset))
    fill = jnp.zeros((13, cols), f32)
    b_ref[6 * dims :, :] = jnp.concatenate([o1, o2, o3, fill], axis=0).astype(bf16)

    def block(i, wide):
        row = pl.multiple_of(i * ROW_BLOCK, ROW_BLOCK)
        here = pl.ds(row, ROW_BLOCK)

        def top(col):
            s = scores(a_ref, b_ref, row, ROW_BLOCK, col, COL_BLOCK)
            return s, functools.reduce(jnp.maximum, [s[:, t : t + LANES] for t in tiles(COL_BLOCK)])

        def spread(best):
            return jnp.broadcast_to(jnp.max(best, axis=1, keepdims=True), best.shape)

        if wide:
            best = lax.fori_loop(
                1,
                cols // COL_BLOCK,
                lambda c, best: jnp.maximum(best, top(pl.multiple_of(c * COL_BLOCK, COL_BLOCK))[1]),
                top(0)[1],
            )
            shift_ref[here, :] = spread(best)
        for col in range(0, cols, COL_BLOCK):
            if col == 0 and not wide:
                s, best = top(0)
                shift = spread(best)
                shift_ref[here, :] = shift
            else:
                s = scores(a_ref, b_ref, row, ROW_BLOCK, col, COL_BLOCK)
                shift = shift_ref[here, :]
            acc = acc_ref[here, :] if col else 0.0
            for t in tiles(COL_BLOCK):
                e = jnp.exp2(s[:, t : t + LANES] - shift)
                e_ref[here, col + t : col + t + LANES] = e
                acc = acc + e
            acc_ref[here, :] = acc

    def run(wide):
        lax.fori_loop(0, rows // ROW_BLOCK, lambda i, _: block(i, wide), None)
        to_lanes(acc_ref, jnp.sum, rho_ref)
        to_lanes(shift_ref, jnp.max, m_ref)
        total = rho_ref[...]
        rho_ref[...] = m_ref[...] + jnp.log2(total)
        return total

    total = run(False)
    fine = jnp.max(total) < 2.0**100

    @pl.when(jnp.logical_not(fine))
    def _():
        run(True)


def column_sums(e_ref, u_ref, q_ref):
    rows, cols = e_ref.shape
    for col in range(0, cols, COL_WIDTH):
        acc = [0.0] * (COL_WIDTH // LANES)
        for row in range(0, rows, 8):
            u = u_ref[row : row + 8, :]
            for k, t in enumerate(tiles(COL_WIDTH)):
                acc[k] = acc[k] + e_ref[row : row + 8, col + t : col + t + LANES] * u
        for k, t in enumerate(tiles(COL_WIDTH)):
            at = (col + t) // LANES
            q_ref[at : at + 1, :] = jnp.sum(acc[k], axis=0, keepdims=True)


def row_sums(e_ref, v_ref, acc_ref):
    rows, cols = e_ref.shape
    for row in range(0, rows, ROW_HEIGHT):
        acc = [0.0] * (ROW_HEIGHT // 8)
        for t in tiles(cols):
            v = jnp.broadcast_to(v_ref[t // LANES : t // LANES + 1, :], (8, LANES))
            for k in range(ROW_HEIGHT // 8):
                acc[k] = acc[k] + e_ref[row + 8 * k : row + 8 * k + 8, t : t + LANES] * v
        for k in range(ROW_HEIGHT // 8):
            acc_ref[row + 8 * k : row + 8 * k + 8, :] = acc[k]


def column_pass(n_parts, log_nt, *refs):
    parts = refs[:n_parts]
    m_ref, e_ref, a_ref, b_ref, *rest, u_ref = refs[n_parts:]
    rows, cols = e_ref.shape
    pot = log_nt - lse2([ref[...] for ref in parts])
    copy = None
    if len(rest) == 1:
        (lam_ref,) = rest
    else:
        square_ref, lam_ref, f_ref, out_ref, stage_ref, sem = rest
        f_ref[...] = pot
        stage_ref[...] = square_ref[...] + pot * (1.0 / KAPPA)
        copy = pltpu.make_async_copy(stage_ref, out_ref, sem)
        copy.start()
    power = pot + m_ref[...]
    u = jnp.exp2(power)
    to_rows(u, u_ref)
    column_sums(e_ref, u_ref, lam_ref)
    q = lam_ref[...]
    lam_ref[...] = jnp.log2(q)
    least = jnp.maximum(total_of(u) * 2.0**-106, 2.0**-96)
    fine = every(power > -100.0, (q >= least) & (q < 2.0**120))

    @pl.when(jnp.logical_not(fine))
    def _():
        to_rows(pot, u_ref)

        def block(c, _):
            col = pl.multiple_of(c * LANES, LANES)

            def shifted(i):
                row = pl.multiple_of(i * LANES, LANES)
                return scores(a_ref, b_ref, row, LANES, col, LANES) + u_ref[pl.ds(row, LANES), :]

            top = lax.fori_loop(
                0,
                rows // LANES,
                lambda i, best: jnp.maximum(best, jnp.max(shifted(i), axis=0, keepdims=True)),
                jnp.full((1, LANES), -jnp.inf, f32),
            )
            total = lax.fori_loop(
                0,
                rows // LANES,
                lambda i, acc: acc + jnp.sum(jnp.exp2(shifted(i) - top), axis=0, keepdims=True),
                jnp.zeros((1, LANES), f32),
            )
            lam_ref[pl.ds(c, 1), :] = top + jnp.log2(total)
            return 0

        lax.fori_loop(0, cols // LANES, block, 0)

    if copy is not None:
        copy.wait()


def row_log_sums(change, m_ref, e_ref, a_ref, b_ref, rho_ref, v_ref, acc_ref):
    rows, cols = e_ref.shape
    v = jnp.exp2(change)
    v_ref[...] = v
    row_sums(e_ref, v_ref, acc_ref)
    to_lanes(acc_ref, jnp.sum, rho_ref)
    r = rho_ref[...]
    rho_ref[...] = m_ref[...] + jnp.log2(r)
    least = jnp.maximum(total_of(v) * 2.0**-106, 2.0**-94)
    fine = every(change > -100.0, (r >= least) & (r < 2.0**120))

    @pl.when(jnp.logical_not(fine))
    def _():
        v_ref[...] = change

        def block(i, _):
            row = pl.multiple_of(i * LANES, LANES)

            def shifted(c):
                col = pl.multiple_of(c * LANES, LANES)
                return scores(a_ref, b_ref, row, LANES, col, LANES) + v_ref[pl.ds(c, 1), :]

            top = lax.fori_loop(
                0,
                cols // LANES,
                lambda c, best: jnp.maximum(best, jnp.max(shifted(c), axis=1, keepdims=True)),
                jnp.full((LANES, 1), -jnp.inf, f32),
            )
            total = lax.fori_loop(
                0,
                cols // LANES,
                lambda c, acc: acc + jnp.sum(jnp.exp2(shifted(c) - top), axis=1, keepdims=True),
                jnp.zeros((LANES, 1), f32),
            )
            value = jnp.broadcast_to(top + jnp.log2(total), (LANES, LANES))
            rho_ref[pl.ds(i, 1), :] = jnp.max(value.T, axis=0, keepdims=True)
            return 0

        lax.fori_loop(0, rows // LANES, block, 0)


def row_pass(n_parts, log_ns, *refs):
    parts = refs[:n_parts]
    change = log_ns - lse2([ref[...] for ref in parts])
    row_log_sums(change, *refs[n_parts:])


def marginal_pass(n_parts, log_ns, *refs):
    parts = refs[:n_parts]
    m_ref, e_ref, a_ref, b_ref, f_ref, g_ref, sum_ref, out_ref, rho_ref, v_ref, acc_ref, stage_ref, sem = refs[n_parts:]
    change = log_ns - lse2([ref[...] for ref in parts])
    stage_ref[...] = g_ref[...] + change * (1.0 / KAPPA)
    copy = pltpu.make_async_copy(stage_ref, out_ref, sem)
    copy.start()
    row_log_sums(change, m_ref, e_ref, a_ref, b_ref, rho_ref, v_ref, acc_ref)
    sum_ref[...] = jnp.exp2(f_ref[...] + rho_ref[...])
    copy.wait()


def others(x, axis, size, steps):
    return [lax.ppermute(x, axis, [(i, i ^ k) for i in range(size)]) for k in steps]


def pool_src(x):
    size = lax.axis_size("src")
    if size == 4:
        return [x] + others(x, "src", size, (1, 2, 3))
    every = lax.all_gather(x, "src", axis=0)
    return [every[k] for k in range(size)]


def pool_tgt(x, join):
    size = lax.axis_size("tgt")
    if size == 8:
        x = join([x] + others(x, "tgt", size, (1,)))
        return [x] + others(x, "tgt", size, (3, 5, 7))
    every = lax.all_gather(x, "tgt", axis=0)
    return [every[k] for k in range(size)]


def body(source_points, target_points, g_init):
    dims, rows = source_points.shape
    cols = target_points.shape[1]
    n_src, n_tgt = lax.axis_size("src"), lax.axis_size("tgt")
    log_nt, log_ns = math.log2(cols * n_tgt), math.log2(rows * n_src)
    depth = 6 * dims + 16
    row_shape, col_shape = (rows // LANES, LANES), (cols // LANES, LANES)
    row, col, square = vmem(row_shape), vmem(col_shape), vmem((rows, LANES))

    def call(kernel, outs, scratch, *args):
        specs = [HBM if out.memory_space == pltpu.HBM else VMEM for out in outs]
        return pl.pallas_call(
            kernel,
            out_shape=tuple(outs),
            in_specs=[VMEM] * len(args),
            out_specs=tuple(specs),
            scratch_shapes=scratch,
            compiler_params=PARAMS,
        )(*args)

    a, own, g, g2, squares = call(
        functools.partial(prepare, n_src),
        (vmem((rows, depth), bf16), vmem(target_points.shape), vmem((1, cols)), col, row),
        [],
        source_points,
        target_points,
        g_init.reshape(1, cols),
        g_init.reshape(col_shape),
    )
    if n_src == 4:
        blocks = [own] + others(target_points, "src", n_src, (1, 2, 3))
    else:
        blocks = [lax.all_gather(target_points, "src", axis=0, tiled=True)]
    a = pin(a)
    e, b, rho, m = call(
        functools.partial(build, len(blocks)),
        (vmem((rows, cols)), vmem((depth, cols), bf16), row, row),
        [square, square],
        a,
        pin(g),
        *map(pin, blocks),
    )
    kept = [pin(x) for x in (m, e, a, b)]

    parts = [pin(x) for x in pool_tgt(rho, lse2)]
    (lam,) = call(functools.partial(column_pass, len(parts), log_nt), (col,), [square], *parts, *kept)
    parts = [pin(x) for x in pool_src(lam)]
    (rho,) = call(functools.partial(row_pass, len(parts), log_ns), (row,), [col, square], *parts, *kept)
    parts = [pin(x) for x in pool_tgt(rho, lse2)]
    lam, f, f_pot = call(
        functools.partial(column_pass, len(parts), log_nt),
        (col, row, pltpu.HBM(row_shape, f32)),
        [row, pltpu.SemaphoreType.DMA, square],
        *parts,
        *kept,
        pin(squares),
    )
    parts = [pin(x) for x in pool_src(lam)]
    total, g_pot = call(
        functools.partial(marginal_pass, len(parts), log_ns),
        (row, pltpu.HBM(col_shape, f32)),
        [row, col, square, col, pltpu.SemaphoreType.DMA],
        *parts,
        *kept,
        pin(f),
        pin(g2),
    )
    marginal = sum(pool_tgt(total, sum)) * (1.0 / (cols * n_tgt))
    return f_pot.reshape(rows), g_pot.reshape(cols), marginal.reshape(rows)


def solution(mesh):
    in_specs = (P(None, "src"), P("src", "tgt"), P("tgt"))
    out_specs = (P("src"), P("tgt"), P("src"))
    return jax.shard_map(body, mesh=mesh, in_specs=in_specs, out_specs=out_specs, check_vma=False)
```

time: 300 us -> 512 us (1.71)
  Pallas kernels: 245 us -> 463 us
    pallas_call x6, Pallas kernels: 245 us -> 463 us  [call(): pl.pallas_call(kernel, out_shape=tuple(outs), in_specs=[VMEM] * len(args)...]
where the time goes in v4:
time: 512 us
  Pallas kernels  463 us (90%)
  starting transfers between devices  23.7 us (5%)
  waiting for transfers between devices  20.8 us (4%)
    pallas_call x6, Pallas kernels, call(): pl.pallas_call(kernel, out_shape=tuple(outs), in_specs=[VMEM] * len(args)...  463 us
    ppermute x21, starting transfers between devices, others(): lax.ppermute(x, axis, [(i, i ^ k) for i in range(size)])  23.7 us
    ppermute x21, waiting for transfers between devices, others(): lax.ppermute(x, axis, [(i, i ^ k) for i in range(size)])  20.8 us
  transfers between devices with their start and end apart: 21, of which 16 were waited for; matrix products, arithmetic and copies ran while one was open for 0% of the time, Pallas kernels for 0%

profile of v4, /device:TPU:0, one launch (start us, length us, event | category | flops | bytes accessed | tf_op | source)
XLA Modules:
  0.0 511.8 jit_solution(4154543717289189941)
XLA Ops:
  0.6 3.0 collective-permute-start
  3.6 1.5 collective-permute-start.2
  5.1 0.0 collective-permute-start.1
  5.2 0.0 copy-start
  5.2 0.9 copy-done
  6.1 0.0 copy-start.1
  6.1 0.9 copy-done.1
  7.0 0.0 copy-start.2
  7.0 0.7 copy-done.2
  7.7 0.2 shard_map.58
  7.9 0.0 collective-permute-done.refs_3_
  7.9 3.5 collective-permute-done.2.refs_5_
  11.5 1.4 collective-permute-done.1.refs_4_
  12.8 13.9 %shard_map.59 = (f32[1024,4096]{1,0:T(8,128)S(1)}, bf16[208,4096]{1,0:T(8,128)(2,1)S(1)}, f32[8,128]{1,0:T(8,128)S(1)}, f32[8,128]{1,0:T(8,128)S(1)}) custom-call(bf16[1024,208]{1,0:T(8,128)(2,1)S(1)} %get-tuple-element.17.refs_0_.refs_6_, f32[1,4096]{1,0:T(1,128)S(1)} %get-tuple-element.18.refs_1_, f32[8,4096]{1,0:T(8,128)S(1)} %get-tuple-element.19.refs_2_, ...), custom_call_target="tpu_custom_call" | custom-call | tf_op jit(solution)/shard_map/pallas_call | solution.py:336
  26.8 0.1 collective-permute-start.3
  26.9 1.2 collective-permute-done.3
  28.0 3.4 collective-permute-start.6
  31.4 0.0 collective-permute-start.5
  31.4 0.6 collective-permute-start.4
  32.0 0.9 collective-permute-done.6.refs_3_
  32.9 2.5 collective-permute-done.5.refs_2_
  35.4 0.0 collective-permute-done.4.refs_1_
  35.4 94.9 %shard_map.60.refs_0_ = f32[32,128]{1,0:T(8,128)S(1)} custom-call(f32[8,128]{1,0:T(8,128)S(1)} %multiply_add_fusion.1.refs_0_, f32[8,128]{1,0:T(8,128)S(1)} %collective-permute-done.4.refs_1_, f32[8,128]{1,0:T(8,128)S(1)} %collective-permute-done.5.refs_2_, f32[8,128]{1,0:T(8,128)S(1)} %collective-permute-done.6.refs_3_, ...), custom_call_target="tpu_custom_call" | custom-call | tf_op jit(solution)/shard_map/pallas_call | solution.py:336
  130.3 1.5 collective-permute-start.9
  131.8 1.5 collective-permute-start.8
  133.3 0.5 collective-permute-start.7
  133.8 1.1 collective-permute-done.9.refs_3_
  135.0 0.5 collective-permute-done.8.refs_2_
  135.5 1.5 collective-permute-done.7.refs_1_
  137.0 129.7 %shard_map.61 = f32[8,128]{1,0:T(8,128)S(1)} custom-call(f32[32,128]{1,0:T(8,128)S(1)} %shard_map.60.refs_0_, f32[32,128]{1,0:T(8,128)S(1)} %collective-permute-done.7.refs_1_, f32[32,128]{1,0:T(8,128)S(1)} %collective-permute-done.8.refs_2_, f32[32,128]{1,0:T(8,128)S(1)} %collective-permute-done.9.refs_3_, f32[8,128]{1,0:T(8,128)S(1)} %get-tuple-element.21.refs_4_, ...), custom_call_target="tpu_custom_call" | custom-call | tf_op jit(solution)/shard_map/pallas_call | solution.py:336
  266.8 0.1 collective-permute-start.10
  266.8 1.2 collective-permute-done.10
  268.0 1.3 collective-permute-start.13
  269.3 0.6 collective-permute-start.12
  269.9 2.1 collective-permute-start.11
  271.9 0.9 collective-permute-done.13.refs_3_
  272.9 0.4 collective-permute-done.12.refs_2_
  273.3 0.0 collective-permute-done.11.refs_1_
  273.3 94.9 %shard_map.62 = (f32[32,128]{1,0:T(8,128)S(1)}, f32[8,128]{1,0:T(8,128)S(1)}, f32[8,128]{1,0:T(8,128)}) custom-call(f32[8,128]{1,0:T(8,128)S(1)} %multiply_add_fusion.refs_0_, f32[8,128]{1,0:T(8,128)S(1)} %collective-permute-done.11.refs_1_, f32[8,128]{1,0:T(8,128)S(1)} %collective-permute-done.12.refs_2_, f32[8,128]{1,0:T(8,128)S(1)} %collective-permute-done.13.refs_3_, ...), custom_call_target="tpu_custom_call" | custom-call | tf_op jit(solution)/shard_map/pallas_call | solution.py:336
  368.2 0.5 collective-permute-start.16
  368.8 1.5 collective-permute-start.15
  370.3 1.5 collective-permute-start.14
  371.8 1.1 collective-permute-done.16.refs_3_
  372.9 0.0 collective-permute-done.15.refs_2_
  372.9 1.1 collective-permute-done.14.refs_1_
  374.0 129.8 %shard_map.63 = (f32[8,128]{1,0:T(8,128)S(1)}, f32[32,128]{1,0:T(8,128)}) custom-call(f32[32,128]{1,0:T(8,128)S(1)} %get-tuple-element.26.refs_0_, f32[32,128]{1,0:T(8,128)S(1)} %collective-permute-done.14.refs_1_, f32[32,128]{1,0:T(8,128)S(1)} %collective-permute-done.15.refs_2_, f32[32,128]{1,0:T(8,128)S(1)} %collective-permute-done.16.refs_3_, ...), custom_call_target="tpu_custom_call" | custom-call | tf_op jit(solution)/shard_map/pallas_call | solution.py:336
  503.8 0.1 collective-permute-start.17
  503.9 1.2 collective-permute-done.17
  505.1 2.2 collective-permute-start.20
  507.2 0.9 collective-permute-start.19
  508.1 0.8 collective-permute-start.18
  508.9 0.9 collective-permute-done.20
  509.9 1.3 collective-permute-done.19
  511.2 0.0 collective-permute-done.18
  511.2 0.6 multiply_bitcast_fusion
  (3 shorter events, 0.0 us)
Async XLA Ops:
  0.6 7.3 %collective-permute-start = (f32[8,4096]{1,0:T(8,128)}, f32[8,4096]{1,0:T(8,128)S(1)}, u32[]{:S(2)}, u32[]{:S(2)}) collective-permute-start(f32[8,4096]{1,0:T(8,128)} %t_ref.1), channel_id=1, source_target_pairs={{0,8},{8,0},{16,24},{24,16},{1,9},{9,1},{17,25},{25,17},{2,10},{10... | collective-permute-start | bytes 393224 | tf_op jit(solution)/shard_map/ppermute | solution.py:305
  3.6 7.8 %collective-permute-start.2 = (f32[8,4096]{1,0:T(8,128)}, f32[8,4096]{1,0:T(8,128)S(1)}, u32[]{:S(2)}, u32[]{:S(2)}) collective-permute-start(f32[8,4096]{1,0:T(8,128)} %t_ref.1), channel_id=1, source_target_pairs={{0,24},{8,16},{16,8},{24,0},{1,25},{9,17},{17,9},{25,1},{2,26},{10... | collective-permute-start | bytes 393224 | tf_op jit(solution)/shard_map/ppermute | solution.py:305
  5.1 7.7 %collective-permute-start.1 = (f32[8,4096]{1,0:T(8,128)}, f32[8,4096]{1,0:T(8,128)S(1)}, u32[]{:S(2)}, u32[]{:S(2)}) collective-permute-start(f32[8,4096]{1,0:T(8,128)} %t_ref.1), channel_id=1, source_target_pairs={{0,16},{8,24},{16,0},{24,8},{1,17},{9,25},{17,1},{25,9},{2,18},{10... | collective-permute-start | bytes 393224 | tf_op jit(solution)/shard_map/ppermute | solution.py:305
  5.2 0.9 copy-start
  6.1 0.9 copy-start.1
  7.0 0.7 copy-start.2
  26.8 1.2 collective-permute-start.3
  28.0 4.9 collective-permute-start.6
  31.4 3.9 collective-permute-start.5
  31.4 3.9 collective-permute-start.4
  130.3 4.7 collective-permute-start.9
  131.8 3.7 collective-permute-start.8
  133.3 3.7 collective-permute-start.7
  266.8 1.2 collective-permute-start.10
  268.0 4.9 collective-permute-start.13
  269.3 4.0 collective-permute-start.12
  269.9 3.4 collective-permute-start.11
  368.2 4.7 collective-permute-start.16
  368.8 4.2 collective-permute-start.15
  370.3 3.7 collective-permute-start.14
  503.8 1.2 collective-permute-start.17
  505.1 4.8 collective-permute-start.20
  507.2 3.9 collective-permute-start.19
  508.1 3.1 collective-permute-start.18

commit v5 on v4

v5 whole, which is shorter than its diff:
```python
import functools
import math

import jax
import jax.numpy as jnp
from jax import lax
from jax.experimental import pallas as pl
from jax.experimental.pallas import tpu as pltpu
from jax.sharding import PartitionSpec as P

epsilon = 0.05
KAPPA = math.log2(math.e) / epsilon
LANES = 128
ROW_BLOCK = 512
COL_BLOCK = 256
COL_WIDTH = 1024
ROW_HEIGHT = 128

f32 = jnp.float32
bf16 = jnp.bfloat16
VMEM = pl.BlockSpec(memory_space=pltpu.VMEM)
PARAMS = pltpu.CompilerParams(vmem_limit_bytes=16 * 2**20)


HBM = pl.BlockSpec(memory_space=pltpu.HBM)


def vmem(shape, dtype=f32):
    return pltpu.VMEM(shape, dtype)


def pin(x, space=pltpu.VMEM):
    return pltpu.with_memory_space_constraint(x, space)


def split(x):
    first = x.astype(bf16)
    rest = x - first.astype(f32)
    second = rest.astype(bf16)
    third = (rest - second.astype(f32)).astype(bf16)
    return first, second, third


def to_lanes(ref, reduce, out_ref):
    for k in range(out_ref.shape[0]):
        part = ref[k * LANES : (k + 1) * LANES, :].T
        out_ref[k : k + 1, :] = reduce(part, axis=0, keepdims=True)


def to_rows(x, out_ref):
    for k in range(x.shape[0]):
        out_ref[k * LANES : (k + 1) * LANES, :] = jnp.broadcast_to(x[k : k + 1, :], (LANES, LANES)).T


def every(*conditions):
    least = [jnp.min(jnp.where(c, 1.0, 0.0), axis=0, keepdims=True) for c in conditions]
    return jnp.min(functools.reduce(jnp.minimum, least)) > 0.5


def total_of(x):
    return jnp.sum(jnp.sum(x, axis=0, keepdims=True), axis=1, keepdims=True)


def lse2(parts):
    top = functools.reduce(jnp.maximum, parts)
    return top + jnp.log2(sum(jnp.exp2(p - top) for p in parts))


def scores(a_ref, b_ref, row, rows, col, cols):
    return jnp.dot(
        a_ref[pl.ds(row, rows), :], b_ref[:, pl.ds(col, cols)], preferred_element_type=f32
    )


def tiles(width):
    return range(0, width, LANES)


def prepare(n_src, src_ref, t_ref, g_ref, g2_ref, a_ref, square_ref, start_ref, start2_ref, *rest):
    *targets, points_ref, sems = rest
    pairs = [(src_ref, points_ref), (g_ref, start_ref), (g2_ref, start2_ref)]
    if targets:
        own_ref, *halves = targets
        pairs.append((t_ref, own_ref))
        width = halves[0].shape[1]
        pairs += [(t_ref.at[:, pl.ds(k * width, width)], half) for k, half in enumerate(halves)]
    copies = [pltpu.make_async_copy(x, y, sems.at[k]) for k, (x, y) in enumerate(pairs)]
    for copy in copies:
        copy.start()
    for copy in copies:
        copy.wait()
    dims, rows = points_ref.shape
    points = points_ref[...]
    square = jnp.sum(points * points, axis=0, keepdims=True)
    for k in range(rows // LANES):
        square_ref[k : k + 1, :] = square[:, k * LANES : (k + 1) * LANES]
    if n_src == 4:
        me, each = lax.axis_index("src"), dims // n_src
        points = jnp.concatenate(
            [points_ref[pl.ds(pl.multiple_of((me ^ k) * each, each), each), :] for k in range(n_src)],
            axis=0,
        )
    s1, s2, s3 = (x.astype(f32) for x in split(points * (2.0 * KAPPA)))
    last = (lax.broadcasted_iota(jnp.int32, (16, rows), 0) < 3).astype(f32)
    a_ref[...] = jnp.concatenate([s1, s1, s2, s1, s3, s2, last], axis=0).T.astype(bf16)


def fill_right(half, g_ref, blocks, b_ref):
    cols = b_ref.shape[1]
    here = slice(half * cols, (half + 1) * cols)
    points = jnp.concatenate([ref[...] if ref.shape[1] == cols else ref[:, here] for ref in blocks], axis=0)
    dims = points.shape[0]
    t1, t2, t3 = split(points)
    for k, part in enumerate((t1, t2, t1, t3, t1, t2)):
        b_ref[k * dims : (k + 1) * dims, :] = part
    offset = KAPPA * (g_ref[:, here] - jnp.sum(points * points, axis=0, keepdims=True))
    o1, o2, o3 = (x.astype(f32) for x in split(offset))
    fill = jnp.zeros((13, cols), f32)
    b_ref[6 * dims :, :] = jnp.concatenate([o1, o2, o3, fill], axis=0).astype(bf16)


def row_top(a_ref, b_ref, row, col):
    s = scores(a_ref, b_ref, row, ROW_BLOCK, col, COL_BLOCK)
    return s, functools.reduce(jnp.maximum, [s[:, t : t + LANES] for t in tiles(COL_BLOCK)])


def spread(best):
    return jnp.broadcast_to(jnp.max(best, axis=1, keepdims=True), best.shape)


def fill_half(first, a_ref, b_ref, e_ref, shift_ref, start_ref, acc_ref):
    rows, cols = e_ref.shape

    def block(i, _):
        row = pl.multiple_of(i * ROW_BLOCK, ROW_BLOCK)
        here = pl.ds(row, ROW_BLOCK)
        for col in range(0, cols, COL_BLOCK):
            if first and col == 0:
                s, best = row_top(a_ref, b_ref, row, col)
                shift = spread(best)
                shift_ref[here, :] = shift
            else:
                s = scores(a_ref, b_ref, row, ROW_BLOCK, col, COL_BLOCK)
                shift = shift_ref[here, :]
            if col:
                acc = acc_ref[here, :]
            else:
                acc = start_ref[here, :] if start_ref is not None else 0.0
            for t in tiles(COL_BLOCK):
                e = jnp.exp2(s[:, t : t + LANES] - shift)
                e_ref[here, col + t : col + t + LANES] = e
                acc = acc + e
            acc_ref[here, :] = acc

    lax.fori_loop(0, rows // ROW_BLOCK, block, None)


def build_first(n_blocks, *refs):
    a_ref, g_ref = refs[:2]
    blocks = refs[2 : 2 + n_blocks]
    e_ref, b_ref, shift_ref, acc_ref = refs[2 + n_blocks :]
    fill_right(0, g_ref, blocks, b_ref)
    fill_half(True, a_ref, b_ref, e_ref, shift_ref, None, acc_ref)


def build_second(n_blocks, *refs):
    a_ref, g_ref = refs[:2]
    blocks = refs[2 : 2 + n_blocks]
    _, b0_ref, shift_ref, start_ref = refs[2 + n_blocks : 6 + n_blocks]
    e0_ref, e_ref, b_ref, rho_ref, m_ref, acc_ref, exact_ref = refs[6 + n_blocks :]
    fill_right(1, g_ref, blocks, b_ref)
    fill_half(False, a_ref, b_ref, e_ref, shift_ref, start_ref, acc_ref)

    def finish(shift_ref):
        to_lanes(acc_ref, jnp.sum, rho_ref)
        to_lanes(shift_ref, jnp.max, m_ref)
        total = rho_ref[...]
        rho_ref[...] = m_ref[...] + jnp.log2(total)
        return total

    fine = every(finish(shift_ref) < 2.0**100)

    @pl.when(jnp.logical_not(fine))
    def _():
        def block(i, _):
            row = pl.multiple_of(i * ROW_BLOCK, ROW_BLOCK)
            best = jnp.full((ROW_BLOCK, LANES), -jnp.inf, f32)
            for part in (b0_ref, b_ref):
                best = lax.fori_loop(
                    0,
                    part.shape[1] // COL_BLOCK,
                    lambda c, best: jnp.maximum(
                        best, row_top(a_ref, part, row, pl.multiple_of(c * COL_BLOCK, COL_BLOCK))[1]
                    ),
                    best,
                )
            exact_ref[pl.ds(row, ROW_BLOCK), :] = spread(best)

        lax.fori_loop(0, e_ref.shape[0] // ROW_BLOCK, block, None)
        fill_half(False, a_ref, b0_ref, e0_ref, exact_ref, None, acc_ref)
        fill_half(False, a_ref, b_ref, e_ref, exact_ref, acc_ref, acc_ref)
        finish(exact_ref)


def column_sums(e_refs, u_ref, q_ref):
    at = 0
    for e_ref in e_refs:
        rows, cols = e_ref.shape
        for col in range(0, cols, COL_WIDTH):
            acc = [0.0] * (COL_WIDTH // LANES)
            for row in range(0, rows, 8):
                u = u_ref[row : row + 8, :]
                for k, t in enumerate(tiles(COL_WIDTH)):
                    acc[k] = acc[k] + e_ref[row : row + 8, col + t : col + t + LANES] * u
            for part in acc:
                q_ref[at : at + 1, :] = jnp.sum(part, axis=0, keepdims=True)
                at += 1


def row_sums(e_refs, v_ref, acc_ref):
    for row in range(0, acc_ref.shape[0], ROW_HEIGHT):
        acc = [0.0] * (ROW_HEIGHT // 8)
        at = 0
        for e_ref in e_refs:
            for t in tiles(e_ref.shape[1]):
                v = jnp.broadcast_to(v_ref[at : at + 1, :], (8, LANES))
                at += 1
                for k in range(ROW_HEIGHT // 8):
                    acc[k] = acc[k] + e_ref[row + 8 * k : row + 8 * k + 8, t : t + LANES] * v
        for k in range(ROW_HEIGHT // 8):
            acc_ref[row + 8 * k : row + 8 * k + 8, :] = acc[k]


def column_pass(n_parts, log_nt, *refs):
    parts = refs[:n_parts]
    m_ref, a_ref, e0_ref, e1_ref, b0_ref, b1_ref, lam_ref, *f_ref, u_ref = refs[n_parts:]
    rows = a_ref.shape[0]
    pot = log_nt - lse2([ref[...] for ref in parts])
    for ref in f_ref:
        ref[...] = pot
    power = pot + m_ref[...]
    u = jnp.exp2(power)
    to_rows(u, u_ref)
    column_sums((e0_ref, e1_ref), u_ref, lam_ref)
    q = lam_ref[...]
    lam_ref[...] = jnp.log2(q)
    least = jnp.maximum(total_of(u) * 2.0**-106, 2.0**-96)
    fine = every(power > -100.0, (q >= least) & (q < 2.0**120))

    @pl.when(jnp.logical_not(fine))
    def _():
        to_rows(pot, u_ref)
        first = 0
        for b_ref in (b0_ref, b1_ref):

            def block(c, _):
                col = pl.multiple_of(c * LANES, LANES)

                def shifted(i):
                    row = pl.multiple_of(i * LANES, LANES)
                    return scores(a_ref, b_ref, row, LANES, col, LANES) + u_ref[pl.ds(row, LANES), :]

                top = lax.fori_loop(
                    0,
                    rows // LANES,
                    lambda i, best: jnp.maximum(best, jnp.max(shifted(i), axis=0, keepdims=True)),
                    jnp.full((1, LANES), -jnp.inf, f32),
                )
                total = lax.fori_loop(
                    0,
                    rows // LANES,
                    lambda i, acc: acc + jnp.sum(jnp.exp2(shifted(i) - top), axis=0, keepdims=True),
                    jnp.zeros((1, LANES), f32),
                )
                lam_ref[pl.ds(first + c, 1), :] = top + jnp.log2(total)

            lax.fori_loop(0, b_ref.shape[1] // LANES, block, None)
            first += b_ref.shape[1] // LANES


def row_log_sums(change, m_ref, a_ref, e0_ref, e1_ref, b0_ref, b1_ref, rho_ref, v_ref, acc_ref):
    v = jnp.exp2(change)
    v_ref[...] = v
    row_sums((e0_ref, e1_ref), v_ref, acc_ref)
    to_lanes(acc_ref, jnp.sum, rho_ref)
    r = rho_ref[...]
    rho_ref[...] = m_ref[...] + jnp.log2(r)
    least = jnp.maximum(total_of(v) * 2.0**-106, 2.0**-94)
    fine = every(change > -100.0, (r >= least) & (r < 2.0**120))

    @pl.when(jnp.logical_not(fine))
    def _():
        v_ref[...] = change

        def block(i, _):
            row = pl.multiple_of(i * LANES, LANES)

            def over_columns(step, value):
                first = 0
                for b_ref in (b0_ref, b1_ref):

                    def body(c, value):
                        col = pl.multiple_of(c * LANES, LANES)
                        s = scores(a_ref, b_ref, row, LANES, col, LANES) + v_ref[pl.ds(first + c, 1), :]
                        return step(value, s)

                    value = lax.fori_loop(0, b_ref.shape[1] // LANES, body, value)
                    first += b_ref.shape[1] // LANES
                return value

            top = over_columns(
                lambda best, s: jnp.maximum(best, jnp.max(s, axis=1, keepdims=True)),
                jnp.full((LANES, 1), -jnp.inf, f32),
            )
            total = over_columns(
                lambda acc, s: acc + jnp.sum(jnp.exp2(s - top), axis=1, keepdims=True),
                jnp.zeros((LANES, 1), f32),
            )
            value = jnp.broadcast_to(top + jnp.log2(total), (LANES, LANES))
            rho_ref[pl.ds(i, 1), :] = jnp.max(value.T, axis=0, keepdims=True)

        lax.fori_loop(0, a_ref.shape[0] // LANES, block, None)


def row_pass(n_parts, log_ns, *refs):
    parts = refs[:n_parts]
    change = log_ns - lse2([ref[...] for ref in parts])
    row_log_sums(change, *refs[n_parts:])


def marginal_pass(n_parts, log_ns, *refs):
    parts = refs[:n_parts]
    *kept, f_ref, g_ref, _, sum_ref, new_ref, rho_ref, v_ref, acc_ref = refs[n_parts:]
    change = log_ns - lse2([ref[...] for ref in parts])
    new_ref[...] = g_ref[...] + change * (1.0 / KAPPA)
    row_log_sums(change, *kept, rho_ref, v_ref, acc_ref)
    sum_ref[...] = jnp.exp2(f_ref[...] + rho_ref[...])


def others(x, axis, size, steps):
    return [lax.ppermute(x, axis, [(i, i ^ k) for i in range(size)]) for k in steps]


def pool_src(x):
    size = lax.axis_size("src")
    if size == 4:
        return [x] + others(x, "src", size, (1, 2, 3))
    every = lax.all_gather(x, "src", axis=0)
    return [every[k] for k in range(size)]


def pool_tgt(x, join):
    size = lax.axis_size("tgt")
    if size == 8:
        x = join([x] + others(x, "tgt", size, (1,)))
        return [x] + others(x, "tgt", size, (3, 5, 7))
    every = lax.all_gather(x, "tgt", axis=0)
    return [every[k] for k in range(size)]


def body(source_points, target_points, g_init):
    dims, rows = source_points.shape
    cols = target_points.shape[1]
    half = cols // 2
    n_src, n_tgt = lax.axis_size("src"), lax.axis_size("tgt")
    log_nt, log_ns = math.log2(cols * n_tgt), math.log2(rows * n_src)
    depth = 6 * dims + 16
    row_shape, col_shape = (rows // LANES, LANES), (cols // LANES, LANES)
    row, col, square = vmem(row_shape), vmem(col_shape), vmem((rows, LANES))
    e_half, b_half = vmem((rows, half)), vmem((depth, half), bf16)

    def call(kernel, outs, scratch, *args, in_hbm=(), aliases={}):
        return pl.pallas_call(
            kernel,
            out_shape=tuple(outs),
            in_specs=[HBM if k in in_hbm else VMEM for k in range(len(args))],
            out_specs=(VMEM,) * len(outs),
            scratch_shapes=scratch,
            input_output_aliases=aliases,
            compiler_params=PARAMS,
        )(*args)

    split_gather = n_src == 4
    targets = (vmem(target_points.shape),) + (vmem((target_points.shape[0], half)),) * 2
    a, squares, g, g2, *own = call(
        functools.partial(prepare, n_src),
        (vmem((rows, depth), bf16), row, vmem((1, cols)), col) + (targets if split_gather else ()),
        [vmem(source_points.shape), pltpu.SemaphoreType.DMA((6,))],
        *(
            pin(x, pltpu.HBM)
            for x in (source_points, target_points, g_init.reshape(1, cols), g_init.reshape(col_shape))
        ),
        in_hbm=(0, 1, 2, 3),
    )
    if split_gather:
        far, near = others(target_points, "src", n_src, (3, 2))
        first, second = (others(pin(x), "src", n_src, (1,))[0] for x in own[1:])
        blocks = [[own[0], x, near, far] for x in (first, second)]
    else:
        blocks = [[lax.all_gather(target_points, "src", axis=0, tiled=True)]] * 2
    blocks = [[pin(x) for x in part] for part in blocks]
    a, g = pin(a), pin(g)
    e0, b0, shift, acc = call(
        functools.partial(build_first, len(blocks[0])),
        (e_half, b_half, square, square),
        [],
        a,
        g,
        *blocks[0],
    )
    b0 = pin(b0)
    e0, e1, b1, rho, m = call(
        functools.partial(build_second, len(blocks[1])),
        (e_half, e_half, b_half, row, row),
        [square, square],
        a,
        g,
        *blocks[1],
        pin(e0),
        b0,
        pin(shift),
        pin(acc),
        aliases={2 + len(blocks[1]): 0},
    )
    kept = [pin(m), a, pin(e0), pin(e1), b0, pin(b1)]

    parts = [pin(x) for x in pool_tgt(rho, lse2)]
    (lam,) = call(functools.partial(column_pass, len(parts), log_nt), (col,), [square], *parts, *kept)
    parts = [pin(x) for x in pool_src(lam)]
    (rho,) = call(functools.partial(row_pass, len(parts), log_ns), (row,), [col, square], *parts, *kept)
    parts = [pin(x) for x in pool_tgt(rho, lse2)]
    lam, f = call(functools.partial(column_pass, len(parts), log_nt), (col, row), [square], *parts, *kept)
    parts = [pin(x) for x in pool_src(lam)]
    f_pot = squares + f * (1.0 / KAPPA)
    args = parts + kept + [pin(f), pin(g2), f_pot]
    total, g_pot = call(
        functools.partial(marginal_pass, len(parts), log_ns),
        (row, col),
        [row, col, square],
        *args,
        in_hbm=(len(args) - 1,),
    )
    marginal = sum(pool_tgt(total, sum)) * (1.0 / (cols * n_tgt))
    return f_pot.reshape(rows), g_pot.reshape(cols), marginal.reshape(rows)


def solution(mesh):
    in_specs = (P(None, "src"), P("src", "tgt"), P("tgt"))
    out_specs = (P("src"), P("tgt"), P("src"))
    return jax.shard_map(body, mesh=mesh, in_specs=in_specs, out_specs=out_specs, check_vma=False)
```

time: 512 us -> 511 us (level)
    ppermute x21 -> x22, waiting for transfers between devices: 20.8 us -> 17.9 us  [others(): lax.ppermute(x, axis, [(i, i ^ k) for i in range(size)])]
    ppermute x21 -> x22, starting transfers between devices: 23.7 us -> 25.9 us  [others(): lax.ppermute(x, axis, [(i, i ^ k) for i in range(size)])]
    pallas_call x6 -> x7, Pallas kernels: 463 us -> 465 us  [call(): pl.pallas_call(kernel, out_shape=tuple(outs), in_specs=[HBM if k in in_hb...]
  transfers between devices with their start and end apart: 21 -> 22, of which waited for: 16 -> 17; matrix products, arithmetic and copies ran while one was open for 0% -> 0% of each run, Pallas kernels for 0% -> 1%
where the time goes in v5:
time: 511 us
  Pallas kernels  465 us (91%)
  starting transfers between devices  25.9 us (5%)
  waiting for transfers between devices  17.9 us (4%)
    pallas_call x7, Pallas kernels, call(): pl.pallas_call(kernel, out_shape=tuple(outs), in_specs=[HBM if k in in_hb...  465 us
    ppermute x22, starting transfers between devices, others(): lax.ppermute(x, axis, [(i, i ^ k) for i in range(size)])  25.9 us
    ppermute x22, waiting for transfers between devices, others(): lax.ppermute(x, axis, [(i, i ^ k) for i in range(size)])  17.9 us
  transfers between devices with their start and end apart: 22, of which 17 were waited for; matrix products, arithmetic and copies ran while one was open for 0% of the time, Pallas kernels for 1%

profile of v5, /device:TPU:0, one launch (start us, length us, event | category | flops | bytes accessed | tf_op | source)
XLA Modules:
  0.0 510.8 jit_solution(1581770465513729069)
XLA Ops:
  0.6 4.0 collective-permute-start.2
  4.6 0.5 collective-permute-start.1
  5.1 1.3 shard_map.58
  6.4 0.2 collective-permute-start.3
  6.6 1.9 collective-permute-start
  8.5 2.2 collective-permute-done.3.refs_3_
  10.7 0.0 collective-permute-done.2.refs_5_
  10.7 0.4 collective-permute-done.1.refs_4_
  11.1 1.8 shard_map.59
  12.9 0.0 collective-permute-done.refs_3_
  12.9 13.2 %shard_map.60 = (f32[1024,2048]{1,0:T(8,128)S(1)}, f32[1024,2048]{1,0:T(8,128)S(1)}, bf16[208,2048]{1,0:T(8,128)(2,1)S(1)}, f32[8,128]{1,0:T(8,128)S(1)}, f32[8,128]{1,0:T(8,128)S(1)}) custom-call(bf16[1024,208]{1,0:T(8,128)(2,1)S(1)} %get-tuple-element.24.refs_0_.refs_5_, f32[1,4096]{1,0:T(1,128)S(1)} %get-tuple-element.25.refs_1_, ...), custom_call_target="tpu_custom_call", output_to_operand_aliasing={{0}: (6, {})} | custom-call | tf_op jit(solution)/shard_map/pallas_call | solution.py:373
  26.1 0.1 collective-permute-start.4
  26.2 1.2 collective-permute-done.4
  27.4 3.6 collective-permute-start.7
  31.0 0.0 collective-permute-start.6
  31.0 0.6 collective-permute-start.5
  31.6 0.7 collective-permute-done.7.refs_3_
  32.3 2.6 collective-permute-done.6.refs_2_
  34.9 0.0 collective-permute-done.5.refs_1_
  35.0 94.9 %shard_map.61.refs_0_ = f32[32,128]{1,0:T(8,128)S(1)} custom-call(f32[8,128]{1,0:T(8,128)S(1)} %multiply_add_fusion.2.refs_0_, f32[8,128]{1,0:T(8,128)S(1)} %collective-permute-done.5.refs_1_, f32[8,128]{1,0:T(8,128)S(1)} %collective-permute-done.6.refs_2_, f32[8,128]{1,0:T(8,128)S(1)} %collective-permute-done.7.refs_3_, ...), custom_call_target="tpu_custom_call" | custom-call | tf_op jit(solution)/shard_map/pallas_call | solution.py:373
  129.8 1.8 collective-permute-start.10
  131.7 1.2 collective-permute-start.9
  132.9 0.5 collective-permute-start.8
  133.4 1.3 collective-permute-done.10.refs_3_
  134.7 0.7 collective-permute-done.9.refs_2_
  135.4 1.2 collective-permute-done.8.refs_1_
  136.6 129.4 %shard_map.62 = f32[8,128]{1,0:T(8,128)S(1)} custom-call(f32[32,128]{1,0:T(8,128)S(1)} %shard_map.61.refs_0_, f32[32,128]{1,0:T(8,128)S(1)} %collective-permute-done.8.refs_1_, f32[32,128]{1,0:T(8,128)S(1)} %collective-permute-done.9.refs_2_, f32[32,128]{1,0:T(8,128)S(1)} %collective-permute-done.10.refs_3_, f32[8,128]{1,0:T(8,128)S(1)} %get-tuple-element.34.refs_4_, ...), custom_call_target="tpu_custom_call" | custom-call | tf_op jit(solution)/shard_map/pallas_call | solution.py:373
  266.1 0.1 collective-permute-start.11
  266.1 1.2 collective-permute-done.11
  267.3 1.3 collective-permute-start.14
  268.6 0.5 collective-permute-start.13
  269.2 2.1 collective-permute-start.12
  271.2 0.9 collective-permute-done.14.refs_3_
  272.2 0.4 collective-permute-done.13.refs_2_
  272.6 0.0 collective-permute-done.12.refs_1_
  272.6 94.9 %shard_map.63 = (f32[32,128]{1,0:T(8,128)S(1)}, f32[8,128]{1,0:T(8,128)S(1)}) custom-call(f32[8,128]{1,0:T(8,128)S(1)} %multiply_add_fusion.1.refs_0_, f32[8,128]{1,0:T(8,128)S(1)} %collective-permute-done.12.refs_1_, f32[8,128]{1,0:T(8,128)S(1)} %collective-permute-done.13.refs_2_, f32[8,128]{1,0:T(8,128)S(1)} %collective-permute-done.14.refs_3_, ...), custom_call_target="tpu_custom_call" | custom-call | tf_op jit(solution)/shard_map/pallas_call | solution.py:373
  367.5 1.6 collective-permute-start.17
  369.1 0.5 collective-permute-start.16
  369.6 1.5 collective-permute-start.15
  371.1 0.0 copy-start
  371.1 1.1 collective-permute-done.17.refs_3_
  372.2 0.6 collective-permute-done.16.refs_2_
  372.8 0.5 collective-permute-done.15.refs_1_
  373.3 129.5 %shard_map.64 = (f32[8,128]{1,0:T(8,128)S(1)}, f32[32,128]{1,0:T(8,128)S(1)}) custom-call(f32[32,128]{1,0:T(8,128)S(1)} %get-tuple-element.39.refs_0_, f32[32,128]{1,0:T(8,128)S(1)} %collective-permute-done.15.refs_1_, f32[32,128]{1,0:T(8,128)S(1)} %collective-permute-done.16.refs_2_, f32[32,128]{1,0:T(8,128)S(1)} %collective-permute-done.17.refs_3_, ...), custom_call_target="tpu_custom_call" | custom-call | tf_op jit(solution)/shard_map/pallas_call | solution.py:373
  502.8 0.0 copy-done
  502.8 0.1 collective-permute-start.18
  502.9 1.2 collective-permute-done.18
  504.1 2.2 collective-permute-start.21
  506.2 0.9 collective-permute-start.20
  507.1 0.8 collective-permute-start.19
  507.9 0.6 copy.8
  508.5 0.3 collective-permute-done.21
  508.9 1.3 collective-permute-done.20
  510.1 0.0 collective-permute-done.19
  510.2 0.6 multiply_bitcast_fusion
  (4 shorter events, 0.0 us)
Async XLA Ops:
  0.6 10.1 %collective-permute-start.2 = (f32[8,4096]{1,0:T(8,128)}, f32[8,4096]{1,0:T(8,128)S(1)}, u32[]{:S(2)}, u32[]{:S(2)}) collective-permute-start(f32[8,4096]{1,0:T(8,128)} %t_ref.1), channel_id=1, source_target_pairs={{0,24},{8,16},{16,8},{24,0},{1,25},{9,17},{17,9},{25,1},{2,26},{10... | collective-permute-start | bytes 393224 | tf_op jit(solution)/shard_map/ppermute | solution.py:341
  4.6 6.5 %collective-permute-start.1 = (f32[8,4096]{1,0:T(8,128)}, f32[8,4096]{1,0:T(8,128)S(1)}, u32[]{:S(2)}, u32[]{:S(2)}) collective-permute-start(f32[8,4096]{1,0:T(8,128)} %t_ref.1), channel_id=1, source_target_pairs={{0,16},{8,24},{16,0},{24,8},{1,17},{9,25},{17,1},{25,9},{2,18},{10... | collective-permute-start | bytes 393224 | tf_op jit(solution)/shard_map/ppermute | solution.py:341
  6.4 4.3 collective-permute-start.3
  6.6 6.3 %collective-permute-start = (f32[8,2048]{1,0:T(8,128)S(1)}, f32[8,2048]{1,0:T(8,128)S(1)}, u32[]{:S(2)}, u32[]{:S(2)}) collective-permute-start(f32[8,2048]{1,0:T(8,128)S(1)} %get-tuple-element.27), channel_id=1, source_target_pairs={{0,8},{8,0},{16,24},{24,16},{1,9},{9,1},{17,25},{25,17},{2,10},{10... | collective-permute-start | bytes 196616 | tf_op jit(solution)/shard_map/ppermute | solution.py:341
  26.1 1.2 collective-permute-start.4
  27.4 5.0 collective-permute-start.7
  31.0 3.9 collective-permute-start.6
  31.0 3.9 collective-permute-start.5
  129.8 4.8 collective-permute-start.10
  131.7 3.7 collective-permute-start.9
  132.9 3.7 collective-permute-start.8
  266.1 1.2 collective-permute-start.11
  267.3 4.9 collective-permute-start.14
  268.6 4.0 collective-permute-start.13
  269.2 3.4 collective-permute-start.12
  367.5 4.7 collective-permute-start.17
  369.1 3.7 collective-permute-start.16
  369.6 3.7 collective-permute-start.15
  371.1 131.7 %copy-start = (f32[8,128]{1,0:T(8,128)}, f32[8,128]{1,0:T(8,128)S(1)}, u32[]{:S(2)}) copy-start(f32[8,128]{1,0:T(8,128)S(1)} %multiply_add_fusion.refs_12_) | copy-start | bytes 12292
  502.8 1.2 collective-permute-start.18
  504.1 4.8 collective-permute-start.21
  506.2 3.9 collective-permute-start.20
  507.1 3.1 collective-permute-start.19

commit v6 on v5

--- a/solution.py
+++ b/solution.py
@@ -393,9 +393,9 @@
         in_hbm=(0, 1, 2, 3),
     )
     if split_gather:
-        far, near = others(target_points, "src", n_src, (3, 2))
-        first, second = (others(pin(x), "src", n_src, (1,))[0] for x in own[1:])
-        blocks = [[own[0], x, near, far] for x in (first, second)]
+        near = others(target_points, "src", n_src, (1, 2))
+        far = [others(pin(x), "src", n_src, (3,))[0] for x in own[1:]]
+        blocks = [[own[0], *near, x] for x in far]
     else:
         blocks = [[lax.all_gather(target_points, "src", axis=0, tiled=True)]] * 2
     blocks = [[pin(x) for x in part] for part in blocks]

time: 511 us -> 511 us (level)
  transfers between devices with their start and end apart: 22 -> 22, of which waited for: 17 -> 16; matrix products, arithmetic and copies ran while one was open for 0% -> 0% of each run, Pallas kernels for 1% -> 1%
where the time goes in v6:
time: 511 us
  Pallas kernels  465 us (91%)
  starting transfers between devices  26.7 us (5%)
  waiting for transfers between devices  17.5 us (3%)
    pallas_call x7, Pallas kernels, call(): pl.pallas_call(kernel, out_shape=tuple(outs), in_specs=[HBM if k in in_hb...  465 us
    ppermute x22, starting transfers between devices, others(): lax.ppermute(x, axis, [(i, i ^ k) for i in range(size)])  26.7 us
    ppermute x22, waiting for transfers between devices, others(): lax.ppermute(x, axis, [(i, i ^ k) for i in range(size)])  17.5 us
  transfers between devices with their start and end apart: 22, of which 16 were waited for; matrix products, arithmetic and copies ran while one was open for 0% of the time, Pallas kernels for 1%

profile of v6, /device:TPU:0, one launch (start us, length us, event | category | flops | bytes accessed | tf_op | source)
XLA Modules:
  0.0 511.2 jit_solution(967803664659007449)
XLA Ops:
  0.6 3.0 collective-permute-start.1
  3.7 1.5 collective-permute-start
  5.2 1.3 shard_map.58
  6.5 0.1 collective-permute-start.3
  6.6 2.9 collective-permute-start.2
  9.5 2.2 collective-permute-done.3.refs_5_
  11.7 0.0 collective-permute-done.1.refs_4_
  11.7 0.0 collective-permute-done.refs_3_
  11.7 1.8 shard_map.59
  13.5 0.0 collective-permute-done.2.refs_5_
  13.5 13.2 %shard_map.60 = (f32[1024,2048]{1,0:T(8,128)S(1)}, f32[1024,2048]{1,0:T(8,128)S(1)}, bf16[208,2048]{1,0:T(8,128)(2,1)S(1)}, f32[8,128]{1,0:T(8,128)S(1)}, f32[8,128]{1,0:T(8,128)S(1)}) custom-call(bf16[1024,208]{1,0:T(8,128)(2,1)S(1)} %get-tuple-element.24.refs_0_.refs_5_, f32[1,4096]{1,0:T(1,128)S(1)} %get-tuple-element.25.refs_1_, ...), custom_call_target="tpu_custom_call", output_to_operand_aliasing={{0}: (6, {})} | custom-call | tf_op jit(solution)/shard_map/pallas_call | solution.py:373
  26.7 0.1 collective-permute-start.4
  26.8 1.2 collective-permute-done.4
  28.0 3.4 collective-permute-start.7
  31.4 0.0 collective-permute-start.6
  31.4 0.6 collective-permute-start.5
  32.0 0.9 collective-permute-done.7.refs_3_
  32.9 2.5 collective-permute-done.6.refs_2_
  35.4 0.0 collective-permute-done.5.refs_1_
  35.4 94.9 %shard_map.61.refs_0_ = f32[32,128]{1,0:T(8,128)S(1)} custom-call(f32[8,128]{1,0:T(8,128)S(1)} %multiply_add_fusion.2.refs_0_, f32[8,128]{1,0:T(8,128)S(1)} %collective-permute-done.5.refs_1_, f32[8,128]{1,0:T(8,128)S(1)} %collective-permute-done.6.refs_2_, f32[8,128]{1,0:T(8,128)S(1)} %collective-permute-done.7.refs_3_, ...), custom_call_target="tpu_custom_call" | custom-call | tf_op jit(solution)/shard_map/pallas_call | solution.py:373
  130.3 1.6 collective-permute-start.10
  131.9 0.6 collective-permute-start.9
  132.5 1.3 collective-permute-start.8
  133.8 1.1 collective-permute-done.10.refs_3_
  135.0 0.7 collective-permute-done.9.refs_2_
  135.6 0.6 collective-permute-done.8.refs_1_
  136.2 129.4 %shard_map.62 = f32[8,128]{1,0:T(8,128)S(1)} custom-call(f32[32,128]{1,0:T(8,128)S(1)} %shard_map.61.refs_0_, f32[32,128]{1,0:T(8,128)S(1)} %collective-permute-done.8.refs_1_, f32[32,128]{1,0:T(8,128)S(1)} %collective-permute-done.9.refs_2_, f32[32,128]{1,0:T(8,128)S(1)} %collective-permute-done.10.refs_3_, f32[8,128]{1,0:T(8,128)S(1)} %get-tuple-element.34.refs_4_, ...), custom_call_target="tpu_custom_call" | custom-call | tf_op jit(solution)/shard_map/pallas_call | solution.py:373
  265.7 0.1 collective-permute-start.11
  265.8 1.2 collective-permute-done.11
  266.9 1.3 collective-permute-start.14
  268.3 0.5 collective-permute-start.13
  268.8 2.1 collective-permute-start.12
  270.9 0.9 collective-permute-done.14.refs_3_
  271.8 0.4 collective-permute-done.13.refs_2_
  272.3 0.0 collective-permute-done.12.refs_1_
  272.3 94.9 %shard_map.63 = (f32[32,128]{1,0:T(8,128)S(1)}, f32[8,128]{1,0:T(8,128)S(1)}) custom-call(f32[8,128]{1,0:T(8,128)S(1)} %multiply_add_fusion.1.refs_0_, f32[8,128]{1,0:T(8,128)S(1)} %collective-permute-done.12.refs_1_, f32[8,128]{1,0:T(8,128)S(1)} %collective-permute-done.13.refs_2_, f32[8,128]{1,0:T(8,128)S(1)} %collective-permute-done.14.refs_3_, ...), custom_call_target="tpu_custom_call" | custom-call | tf_op jit(solution)/shard_map/pallas_call | solution.py:373
  367.1 1.5 collective-permute-start.17
  368.7 1.3 collective-permute-start.16
  370.0 0.7 collective-permute-start.15
  370.7 0.0 copy-start
  370.7 1.1 collective-permute-done.17.refs_3_
  371.8 0.6 collective-permute-done.16.refs_2_
  372.4 1.3 collective-permute-done.15.refs_1_
  373.7 129.5 %shard_map.64 = (f32[8,128]{1,0:T(8,128)S(1)}, f32[32,128]{1,0:T(8,128)S(1)}) custom-call(f32[32,128]{1,0:T(8,128)S(1)} %get-tuple-element.39.refs_0_, f32[32,128]{1,0:T(8,128)S(1)} %collective-permute-done.15.refs_1_, f32[32,128]{1,0:T(8,128)S(1)} %collective-permute-done.16.refs_2_, f32[32,128]{1,0:T(8,128)S(1)} %collective-permute-done.17.refs_3_, ...), custom_call_target="tpu_custom_call" | custom-call | tf_op jit(solution)/shard_map/pallas_call | solution.py:373
  503.2 0.0 copy-done
  503.2 0.1 collective-permute-start.18
  503.3 1.2 collective-permute-done.18
  504.5 2.2 collective-permute-start.21
  506.6 0.9 collective-permute-start.20
  507.5 0.8 collective-permute-start.19
  508.3 0.6 copy.8
  508.9 0.3 collective-permute-done.21
  509.3 1.3 collective-permute-done.20
  510.5 0.0 collective-permute-done.19
  510.6 0.6 multiply_bitcast_fusion
  (4 shorter events, 0.0 us)
Async XLA Ops:
  0.6 11.1 %collective-permute-start.1 = (f32[8,4096]{1,0:T(8,128)}, f32[8,4096]{1,0:T(8,128)S(1)}, u32[]{:S(2)}, u32[]{:S(2)}) collective-permute-start(f32[8,4096]{1,0:T(8,128)} %t_ref.1), channel_id=1, source_target_pairs={{0,16},{8,24},{16,0},{24,8},{1,17},{9,25},{17,1},{25,9},{2,18},{10... | collective-permute-start | bytes 393224 | tf_op jit(solution)/shard_map/ppermute | solution.py:341
  3.7 8.0 %collective-permute-start = (f32[8,4096]{1,0:T(8,128)}, f32[8,4096]{1,0:T(8,128)S(1)}, u32[]{:S(2)}, u32[]{:S(2)}) collective-permute-start(f32[8,4096]{1,0:T(8,128)} %t_ref.1), channel_id=1, source_target_pairs={{0,8},{8,0},{16,24},{24,16},{1,9},{9,1},{17,25},{25,17},{2,10},{10... | collective-permute-start | bytes 393224 | tf_op jit(solution)/shard_map/ppermute | solution.py:341
  6.5 5.2 %collective-permute-start.3 = (f32[8,2048]{1,0:T(8,128)S(1)}, f32[8,2048]{1,0:T(8,128)S(1)}, u32[]{:S(2)}, u32[]{:S(2)}) collective-permute-start(f32[8,2048]{1,0:T(8,128)S(1)} %get-tuple-element.28), channel_id=1, source_target_pairs={{0,24},{8,16},{16,8},{24,0},{1,25},{9,17},{17,9},{25,1},{2,26},{10... | collective-permute-start | bytes 196616 | tf_op jit(solution)/shard_map/ppermute | solution.py:341
  6.6 6.9 %collective-permute-start.2 = (f32[8,2048]{1,0:T(8,128)S(1)}, f32[8,2048]{1,0:T(8,128)S(1)}, u32[]{:S(2)}, u32[]{:S(2)}) collective-permute-start(f32[8,2048]{1,0:T(8,128)S(1)} %get-tuple-element.27), channel_id=1, source_target_pairs={{0,24},{8,16},{16,8},{24,0},{1,25},{9,17},{17,9},{25,1},{2,26},{10... | collective-permute-start | bytes 196616 | tf_op jit(solution)/shard_map/ppermute | solution.py:341
  26.7 1.2 collective-permute-start.4
  28.0 4.9 collective-permute-start.7
  31.4 3.9 collective-permute-start.6
  31.4 3.9 collective-permute-start.5
  130.3 4.7 collective-permute-start.10
  131.9 3.7 collective-permute-start.9
  132.5 3.7 collective-permute-start.8
  265.7 1.2 collective-permute-start.11
  266.9 4.9 collective-permute-start.14
  268.3 4.0 collective-permute-start.13
  268.8 3.4 collective-permute-start.12
  367.1 4.7 collective-permute-start.17
  368.7 3.7 collective-permute-start.16
  370.0 3.7 collective-permute-start.15
  370.7 132.5 %copy-start = (f32[8,128]{1,0:T(8,128)}, f32[8,128]{1,0:T(8,128)S(1)}, u32[]{:S(2)}) copy-start(f32[8,128]{1,0:T(8,128)S(1)} %multiply_add_fusion.refs_12_) | copy-start | bytes 12292
  503.2 1.2 collective-permute-start.18
  504.5 4.8 collective-permute-start.21
  506.6 3.9 collective-permute-start.20
  507.5 3.1 collective-permute-start.19

commit v7 on v5

--- a/solution.py
+++ b/solution.py
@@ -14,7 +14,6 @@
 ROW_BLOCK = 512
 COL_BLOCK = 256
 COL_WIDTH = 1024
-ROW_HEIGHT = 128
 
 f32 = jnp.float32
 bf16 = jnp.bfloat16
@@ -168,17 +167,17 @@
     blocks = refs[2 : 2 + n_blocks]
     _, b0_ref, shift_ref, start_ref = refs[2 + n_blocks : 6 + n_blocks]
     e0_ref, e_ref, b_ref, rho_ref, m_ref, acc_ref, exact_ref = refs[6 + n_blocks :]
+    to_lanes(shift_ref, jnp.max, m_ref)
     fill_right(1, g_ref, blocks, b_ref)
     fill_half(False, a_ref, b_ref, e_ref, shift_ref, start_ref, acc_ref)
 
-    def finish(shift_ref):
+    def finish():
         to_lanes(acc_ref, jnp.sum, rho_ref)
-        to_lanes(shift_ref, jnp.max, m_ref)
         total = rho_ref[...]
         rho_ref[...] = m_ref[...] + jnp.log2(total)
         return total
 
-    fine = every(finish(shift_ref) < 2.0**100)
+    fine = every(finish() < 2.0**100)
 
     @pl.when(jnp.logical_not(fine))
     def _():
@@ -199,7 +198,8 @@
         lax.fori_loop(0, e_ref.shape[0] // ROW_BLOCK, block, None)
         fill_half(False, a_ref, b0_ref, e0_ref, exact_ref, None, acc_ref)
         fill_half(False, a_ref, b_ref, e_ref, exact_ref, acc_ref, acc_ref)
-        finish(exact_ref)
+        to_lanes(exact_ref, jnp.max, m_ref)
+        finish()
 
 
 def column_sums(e_refs, u_ref, q_ref):
@@ -217,18 +217,18 @@
                 at += 1
 
 
-def row_sums(e_refs, v_ref, acc_ref):
-    for row in range(0, acc_ref.shape[0], ROW_HEIGHT):
-        acc = [0.0] * (ROW_HEIGHT // 8)
+def row_sums(e_refs, v_ref, out_ref):
+    for k in range(out_ref.shape[0]):
+        acc = [0.0] * (LANES // 8)
         at = 0
         for e_ref in e_refs:
             for t in tiles(e_ref.shape[1]):
                 v = jnp.broadcast_to(v_ref[at : at + 1, :], (8, LANES))
                 at += 1
-                for k in range(ROW_HEIGHT // 8):
-                    acc[k] = acc[k] + e_ref[row + 8 * k : row + 8 * k + 8, t : t + LANES] * v
-        for k in range(ROW_HEIGHT // 8):
-            acc_ref[row + 8 * k : row + 8 * k + 8, :] = acc[k]
+                for n in range(LANES // 8):
+                    row = k * LANES + 8 * n
+                    acc[n] = acc[n] + e_ref[row : row + 8, t : t + LANES] * v
+        out_ref[k : k + 1, :] = jnp.sum(jnp.concatenate(acc, axis=0).T, axis=0, keepdims=True)
 
 
 def column_pass(n_parts, log_nt, *refs):
@@ -240,11 +240,11 @@
         ref[...] = pot
     power = pot + m_ref[...]
     u = jnp.exp2(power)
+    least = jnp.maximum(total_of(u) * 2.0**-106, 2.0**-96)
     to_rows(u, u_ref)
     column_sums((e0_ref, e1_ref), u_ref, lam_ref)
     q = lam_ref[...]
     lam_ref[...] = jnp.log2(q)
-    least = jnp.maximum(total_of(u) * 2.0**-106, 2.0**-96)
     fine = every(power > -100.0, (q >= least) & (q < 2.0**120))
 
     @pl.when(jnp.logical_not(fine))
@@ -278,14 +278,13 @@
             first += b_ref.shape[1] // LANES
 
 
-def row_log_sums(change, m_ref, a_ref, e0_ref, e1_ref, b0_ref, b1_ref, rho_ref, v_ref, acc_ref):
+def row_log_sums(change, m_ref, a_ref, e0_ref, e1_ref, b0_ref, b1_ref, rho_ref, v_ref):
     v = jnp.exp2(change)
     v_ref[...] = v
-    row_sums((e0_ref, e1_ref), v_ref, acc_ref)
-    to_lanes(acc_ref, jnp.sum, rho_ref)
+    least = jnp.maximum(total_of(v) * 2.0**-106, 2.0**-94)
+    row_sums((e0_ref, e1_ref), v_ref, rho_ref)
     r = rho_ref[...]
     rho_ref[...] = m_ref[...] + jnp.log2(r)
-    least = jnp.maximum(total_of(v) * 2.0**-106, 2.0**-94)
     fine = every(change > -100.0, (r >= least) & (r < 2.0**120))
 
     @pl.when(jnp.logical_not(fine))
@@ -330,10 +329,10 @@
 
 def marginal_pass(n_parts, log_ns, *refs):
     parts = refs[:n_parts]
-    *kept, f_ref, g_ref, _, sum_ref, new_ref, rho_ref, v_ref, acc_ref = refs[n_parts:]
+    *kept, f_ref, g_ref, _, sum_ref, new_ref, rho_ref, v_ref = refs[n_parts:]
     change = log_ns - lse2([ref[...] for ref in parts])
     new_ref[...] = g_ref[...] + change * (1.0 / KAPPA)
-    row_log_sums(change, *kept, rho_ref, v_ref, acc_ref)
+    row_log_sums(change, *kept, rho_ref, v_ref)
     sum_ref[...] = jnp.exp2(f_ref[...] + rho_ref[...])
 
 
@@ -427,7 +426,7 @@
     parts = [pin(x) for x in pool_tgt(rho, lse2)]
     (lam,) = call(functools.partial(column_pass, len(parts), log_nt), (col,), [square], *parts, *kept)
     parts = [pin(x) for x in pool_src(lam)]
-    (rho,) = call(functools.partial(row_pass, len(parts), log_ns), (row,), [col, square], *parts, *kept)
+    (rho,) = call(functools.partial(row_pass, len(parts), log_ns), (row,), [col], *parts, *kept)
     parts = [pin(x) for x in pool_tgt(rho, lse2)]
     lam, f = call(functools.partial(column_pass, len(parts), log_nt), (col, row), [square], *parts, *kept)
     parts = [pin(x) for x in pool_src(lam)]
@@ -436,7 +435,7 @@
     total, g_pot = call(
         functools.partial(marginal_pass, len(parts), log_ns),
         (row, col),
-        [row, col, square],
+        [row, col],
         *args,
         in_hbm=(len(args) - 1,),
     )

time: 511 us -> 511 us (level)
  no operation moved by 1% of the time
where the time goes in v7:
time: 511 us
  Pallas kernels  465 us (91%)
  starting transfers between devices  25.9 us (5%)
  waiting for transfers between devices  17.9 us (4%)
    pallas_call x7, Pallas kernels, call(): pl.pallas_call(kernel, out_shape=tuple(outs), in_specs=[HBM if k in in_hb...  465 us
    ppermute x22, starting transfers between devices, others(): lax.ppermute(x, axis, [(i, i ^ k) for i in range(size)])  25.9 us
    ppermute x22, waiting for transfers between devices, others(): lax.ppermute(x, axis, [(i, i ^ k) for i in range(size)])  17.9 us
  transfers between devices with their start and end apart: 22, of which 17 were waited for; matrix products, arithmetic and copies ran while one was open for 0% of the time, Pallas kernels for 1%

profile of v7, /device:TPU:0, one launch (start us, length us, event | category | flops | bytes accessed | tf_op | source)
XLA Modules:
  0.0 510.8 jit_solution(16020539568011433812)
XLA Ops:
  0.6 4.0 collective-permute-start.2
  4.6 0.5 collective-permute-start.1
  5.1 1.3 shard_map.58
  6.4 0.2 collective-permute-start.3
  6.6 1.9 collective-permute-start
  8.5 2.2 collective-permute-done.3.refs_3_
  10.7 0.0 collective-permute-done.2.refs_5_
  10.7 0.4 collective-permute-done.1.refs_4_
  11.1 1.8 shard_map.59
  12.9 0.0 collective-permute-done.refs_3_
  12.9 13.3 %shard_map.60 = (f32[1024,2048]{1,0:T(8,128)S(1)}, f32[1024,2048]{1,0:T(8,128)S(1)}, bf16[208,2048]{1,0:T(8,128)(2,1)S(1)}, f32[8,128]{1,0:T(8,128)S(1)}, f32[8,128]{1,0:T(8,128)S(1)}) custom-call(bf16[1024,208]{1,0:T(8,128)(2,1)S(1)} %get-tuple-element.24.refs_0_.refs_5_, f32[1,4096]{1,0:T(1,128)S(1)} %get-tuple-element.25.refs_1_, ...), custom_call_target="tpu_custom_call", output_to_operand_aliasing={{0}: (6, {})} | custom-call | tf_op jit(solution)/shard_map/pallas_call | solution.py:372
  26.2 0.1 collective-permute-start.4
  26.3 1.2 collective-permute-done.4
  27.5 3.6 collective-permute-start.7
  31.1 0.0 collective-permute-start.6
  31.1 0.6 collective-permute-start.5
  31.7 0.7 collective-permute-done.7.refs_3_
  32.4 2.6 collective-permute-done.6.refs_2_
  35.0 0.0 collective-permute-done.5.refs_1_
  35.0 94.9 %shard_map.61.refs_0_ = f32[32,128]{1,0:T(8,128)S(1)} custom-call(f32[8,128]{1,0:T(8,128)S(1)} %multiply_add_fusion.2.refs_0_, f32[8,128]{1,0:T(8,128)S(1)} %collective-permute-done.5.refs_1_, f32[8,128]{1,0:T(8,128)S(1)} %collective-permute-done.6.refs_2_, f32[8,128]{1,0:T(8,128)S(1)} %collective-permute-done.7.refs_3_, ...), custom_call_target="tpu_custom_call" | custom-call | tf_op jit(solution)/shard_map/pallas_call | solution.py:372
  129.9 1.8 collective-permute-start.10
  131.7 1.2 collective-permute-start.9
  132.9 0.5 collective-permute-start.8
  133.5 1.3 collective-permute-done.10.refs_3_
  134.7 0.7 collective-permute-done.9.refs_2_
  135.5 1.2 collective-permute-done.8.refs_1_
  136.7 129.4 %shard_map.62 = f32[8,128]{1,0:T(8,128)S(1)} custom-call(f32[32,128]{1,0:T(8,128)S(1)} %shard_map.61.refs_0_, f32[32,128]{1,0:T(8,128)S(1)} %collective-permute-done.8.refs_1_, f32[32,128]{1,0:T(8,128)S(1)} %collective-permute-done.9.refs_2_, f32[32,128]{1,0:T(8,128)S(1)} %collective-permute-done.10.refs_3_, f32[8,128]{1,0:T(8,128)S(1)} %get-tuple-element.34.refs_4_, ...), custom_call_target="tpu_custom_call" | custom-call | tf_op jit(solution)/shard_map/pallas_call | solution.py:372
  266.1 0.1 collective-permute-start.11
  266.2 1.2 collective-permute-done.11
  267.3 1.3 collective-permute-start.14
  268.7 0.5 collective-permute-start.13
  269.2 2.1 collective-permute-start.12
  271.3 0.9 collective-permute-done.14.refs_3_
  272.2 0.4 collective-permute-done.13.refs_2_
  272.7 0.0 collective-permute-done.12.refs_1_
  272.7 94.9 %shard_map.63 = (f32[32,128]{1,0:T(8,128)S(1)}, f32[8,128]{1,0:T(8,128)S(1)}) custom-call(f32[8,128]{1,0:T(8,128)S(1)} %multiply_add_fusion.1.refs_0_, f32[8,128]{1,0:T(8,128)S(1)} %collective-permute-done.12.refs_1_, f32[8,128]{1,0:T(8,128)S(1)} %collective-permute-done.13.refs_2_, f32[8,128]{1,0:T(8,128)S(1)} %collective-permute-done.14.refs_3_, ...), custom_call_target="tpu_custom_call" | custom-call | tf_op jit(solution)/shard_map/pallas_call | solution.py:372
  367.5 1.6 collective-permute-start.17
  369.1 0.5 collective-permute-start.16
  369.6 1.5 collective-permute-start.15
  371.1 0.0 copy-start
  371.1 1.1 collective-permute-done.17.refs_3_
  372.3 0.6 collective-permute-done.16.refs_2_
  372.8 0.5 collective-permute-done.15.refs_1_
  373.4 129.5 %shard_map.64 = (f32[8,128]{1,0:T(8,128)S(1)}, f32[32,128]{1,0:T(8,128)S(1)}) custom-call(f32[32,128]{1,0:T(8,128)S(1)} %get-tuple-element.39.refs_0_, f32[32,128]{1,0:T(8,128)S(1)} %collective-permute-done.15.refs_1_, f32[32,128]{1,0:T(8,128)S(1)} %collective-permute-done.16.refs_2_, f32[32,128]{1,0:T(8,128)S(1)} %collective-permute-done.17.refs_3_, ...), custom_call_target="tpu_custom_call" | custom-call | tf_op jit(solution)/shard_map/pallas_call | solution.py:372
  502.8 0.0 copy-done
  502.8 0.1 collective-permute-start.18
  502.9 1.2 collective-permute-done.18
  504.1 2.2 collective-permute-start.21
  506.2 0.9 collective-permute-start.20
  507.1 0.8 collective-permute-start.19
  507.9 0.6 copy.8
  508.5 0.3 collective-permute-done.21
  508.9 1.3 collective-permute-done.20
  510.1 0.0 collective-permute-done.19
  510.2 0.6 multiply_bitcast_fusion
  (4 shorter events, 0.0 us)
Async XLA Ops:
  0.6 10.1 %collective-permute-start.2 = (f32[8,4096]{1,0:T(8,128)}, f32[8,4096]{1,0:T(8,128)S(1)}, u32[]{:S(2)}, u32[]{:S(2)}) collective-permute-start(f32[8,4096]{1,0:T(8,128)} %t_ref.1), channel_id=1, source_target_pairs={{0,24},{8,16},{16,8},{24,0},{1,25},{9,17},{17,9},{25,1},{2,26},{10... | collective-permute-start | bytes 393224 | tf_op jit(solution)/shard_map/ppermute | solution.py:340
  4.6 6.5 %collective-permute-start.1 = (f32[8,4096]{1,0:T(8,128)}, f32[8,4096]{1,0:T(8,128)S(1)}, u32[]{:S(2)}, u32[]{:S(2)}) collective-permute-start(f32[8,4096]{1,0:T(8,128)} %t_ref.1), channel_id=1, source_target_pairs={{0,16},{8,24},{16,0},{24,8},{1,17},{9,25},{17,1},{25,9},{2,18},{10... | collective-permute-start | bytes 393224 | tf_op jit(solution)/shard_map/ppermute | solution.py:340
  6.4 4.3 collective-permute-start.3
  6.6 6.3 %collective-permute-start = (f32[8,2048]{1,0:T(8,128)S(1)}, f32[8,2048]{1,0:T(8,128)S(1)}, u32[]{:S(2)}, u32[]{:S(2)}) collective-permute-start(f32[8,2048]{1,0:T(8,128)S(1)} %get-tuple-element.27), channel_id=1, source_target_pairs={{0,8},{8,0},{16,24},{24,16},{1,9},{9,1},{17,25},{25,17},{2,10},{10... | collective-permute-start | bytes 196616 | tf_op jit(solution)/shard_map/ppermute | solution.py:340
  26.2 1.2 collective-permute-start.4
  27.5 5.0 collective-permute-start.7
  31.1 3.9 collective-permute-start.6
  31.1 3.9 collective-permute-start.5
  129.9 4.8 collective-permute-start.10
  131.7 3.7 collective-permute-start.9
  132.9 3.7 collective-permute-start.8
  266.1 1.2 collective-permute-start.11
  267.3 4.9 collective-permute-start.14
  268.7 4.0 collective-permute-start.13
  269.2 3.4 collective-permute-start.12
  367.5 4.7 collective-permute-start.17
  369.1 3.7 collective-permute-start.16
  369.6 3.7 collective-permute-start.15
  371.1 131.7 %copy-start = (f32[8,128]{1,0:T(8,128)}, f32[8,128]{1,0:T(8,128)S(1)}, u32[]{:S(2)}) copy-start(f32[8,128]{1,0:T(8,128)S(1)} %multiply_add_fusion.refs_12_) | copy-start | bytes 12292
  502.8 1.2 collective-permute-start.18
  504.1 4.8 collective-permute-start.21
  506.2 3.9 collective-permute-start.20
  507.1 3.1 collective-permute-start.19

commit v8 on v7

--- a/solution.py
+++ b/solution.py
@@ -392,7 +392,7 @@
         in_hbm=(0, 1, 2, 3),
     )
     if split_gather:
-        far, near = others(target_points, "src", n_src, (3, 2))
+        near, far = others(target_points, "src", n_src, (2, 3))
         first, second = (others(pin(x), "src", n_src, (1,))[0] for x in own[1:])
         blocks = [[own[0], x, near, far] for x in (first, second)]
     else:

time: 511 us -> 511 us (level)
  no operation moved by 1% of the time
where the time goes in v8:
time: 511 us
  Pallas kernels  465 us (91%)
  starting transfers between devices  25.9 us (5%)
  waiting for transfers between devices  17.9 us (4%)
    pallas_call x7, Pallas kernels, call(): pl.pallas_call(kernel, out_shape=tuple(outs), in_specs=[HBM if k in in_hb...  465 us
    ppermute x22, starting transfers between devices, others(): lax.ppermute(x, axis, [(i, i ^ k) for i in range(size)])  25.9 us
    ppermute x22, waiting for transfers between devices, others(): lax.ppermute(x, axis, [(i, i ^ k) for i in range(size)])  17.9 us
  transfers between devices with their start and end apart: 22, of which 17 were waited for; matrix products, arithmetic and copies ran while one was open for 0% of the time, Pallas kernels for 1%

profile of v8, /device:TPU:0, one launch (start us, length us, event | category | flops | bytes accessed | tf_op | source)
XLA Modules:
  0.0 510.8 jit_solution(16020539568011433812)
XLA Ops:
  0.6 4.0 collective-permute-start.2
  4.6 0.5 collective-permute-start.1
  5.1 1.3 shard_map.58
  6.4 0.2 collective-permute-start.3
  6.6 1.9 collective-permute-start
  8.5 2.2 collective-permute-done.3.refs_3_
  10.7 0.0 collective-permute-done.2.refs_5_
  10.7 0.4 collective-permute-done.1.refs_4_
  11.1 1.8 shard_map.59
  12.9 0.0 collective-permute-done.refs_3_
  12.9 13.3 %shard_map.60 = (f32[1024,2048]{1,0:T(8,128)S(1)}, f32[1024,2048]{1,0:T(8,128)S(1)}, bf16[208,2048]{1,0:T(8,128)(2,1)S(1)}, f32[8,128]{1,0:T(8,128)S(1)}, f32[8,128]{1,0:T(8,128)S(1)}) custom-call(bf16[1024,208]{1,0:T(8,128)(2,1)S(1)} %get-tuple-element.24.refs_0_.refs_5_, f32[1,4096]{1,0:T(1,128)S(1)} %get-tuple-element.25.refs_1_, ...), custom_call_target="tpu_custom_call", output_to_operand_aliasing={{0}: (6, {})} | custom-call | tf_op jit(solution)/shard_map/pallas_call | solution.py:372
  26.2 0.1 collective-permute-start.4
  26.3 1.2 collective-permute-done.4
  27.5 3.6 collective-permute-start.7
  31.1 0.0 collective-permute-start.6
  31.1 0.6 collective-permute-start.5
  31.7 0.7 collective-permute-done.7.refs_3_
  32.4 2.6 collective-permute-done.6.refs_2_
  35.0 0.0 collective-permute-done.5.refs_1_
  35.0 94.9 %shard_map.61.refs_0_ = f32[32,128]{1,0:T(8,128)S(1)} custom-call(f32[8,128]{1,0:T(8,128)S(1)} %multiply_add_fusion.2.refs_0_, f32[8,128]{1,0:T(8,128)S(1)} %collective-permute-done.5.refs_1_, f32[8,128]{1,0:T(8,128)S(1)} %collective-permute-done.6.refs_2_, f32[8,128]{1,0:T(8,128)S(1)} %collective-permute-done.7.refs_3_, ...), custom_call_target="tpu_custom_call" | custom-call | tf_op jit(solution)/shard_map/pallas_call | solution.py:372
  129.9 1.8 collective-permute-start.10
  131.7 1.2 collective-permute-start.9
  132.9 0.5 collective-permute-start.8
  133.5 1.3 collective-permute-done.10.refs_3_
  134.7 0.7 collective-permute-done.9.refs_2_
  135.5 1.2 collective-permute-done.8.refs_1_
  136.7 129.4 %shard_map.62 = f32[8,128]{1,0:T(8,128)S(1)} custom-call(f32[32,128]{1,0:T(8,128)S(1)} %shard_map.61.refs_0_, f32[32,128]{1,0:T(8,128)S(1)} %collective-permute-done.8.refs_1_, f32[32,128]{1,0:T(8,128)S(1)} %collective-permute-done.9.refs_2_, f32[32,128]{1,0:T(8,128)S(1)} %collective-permute-done.10.refs_3_, f32[8,128]{1,0:T(8,128)S(1)} %get-tuple-element.34.refs_4_, ...), custom_call_target="tpu_custom_call" | custom-call | tf_op jit(solution)/shard_map/pallas_call | solution.py:372
  266.1 0.1 collective-permute-start.11
  266.2 1.2 collective-permute-done.11
  267.3 1.3 collective-permute-start.14
  268.7 0.5 collective-permute-start.13
  269.2 2.1 collective-permute-start.12
  271.3 0.9 collective-permute-done.14.refs_3_
  272.2 0.4 collective-permute-done.13.refs_2_
  272.7 0.0 collective-permute-done.12.refs_1_
  272.7 94.9 %shard_map.63 = (f32[32,128]{1,0:T(8,128)S(1)}, f32[8,128]{1,0:T(8,128)S(1)}) custom-call(f32[8,128]{1,0:T(8,128)S(1)} %multiply_add_fusion.1.refs_0_, f32[8,128]{1,0:T(8,128)S(1)} %collective-permute-done.12.refs_1_, f32[8,128]{1,0:T(8,128)S(1)} %collective-permute-done.13.refs_2_, f32[8,128]{1,0:T(8,128)S(1)} %collective-permute-done.14.refs_3_, ...), custom_call_target="tpu_custom_call" | custom-call | tf_op jit(solution)/shard_map/pallas_call | solution.py:372
  367.5 1.6 collective-permute-start.17
  369.1 0.5 collective-permute-start.16
  369.6 1.5 collective-permute-start.15
  371.1 0.0 copy-start
  371.1 1.1 collective-permute-done.17.refs_3_
  372.3 0.6 collective-permute-done.16.refs_2_
  372.8 0.5 collective-permute-done.15.refs_1_
  373.4 129.5 %shard_map.64 = (f32[8,128]{1,0:T(8,128)S(1)}, f32[32,128]{1,0:T(8,128)S(1)}) custom-call(f32[32,128]{1,0:T(8,128)S(1)} %get-tuple-element.39.refs_0_, f32[32,128]{1,0:T(8,128)S(1)} %collective-permute-done.15.refs_1_, f32[32,128]{1,0:T(8,128)S(1)} %collective-permute-done.16.refs_2_, f32[32,128]{1,0:T(8,128)S(1)} %collective-permute-done.17.refs_3_, ...), custom_call_target="tpu_custom_call" | custom-call | tf_op jit(solution)/shard_map/pallas_call | solution.py:372
  502.8 0.0 copy-done
  502.8 0.1 collective-permute-start.18
  502.9 1.2 collective-permute-done.18
  504.1 2.2 collective-permute-start.21
  506.2 0.9 collective-permute-start.20
  507.1 0.8 collective-permute-start.19
  507.9 0.6 copy.8
  508.5 0.3 collective-permute-done.21
  508.9 1.3 collective-permute-done.20
  510.1 0.0 collective-permute-done.19
  510.2 0.6 multiply_bitcast_fusion
  (4 shorter events, 0.0 us)
Async XLA Ops:
  0.6 10.1 %collective-permute-start.2 = (f32[8,4096]{1,0:T(8,128)}, f32[8,4096]{1,0:T(8,128)S(1)}, u32[]{:S(2)}, u32[]{:S(2)}) collective-permute-start(f32[8,4096]{1,0:T(8,128)} %t_ref.1), channel_id=1, source_target_pairs={{0,24},{8,16},{16,8},{24,0},{1,25},{9,17},{17,9},{25,1},{2,26},{10... | collective-permute-start | bytes 393224 | tf_op jit(solution)/shard_map/ppermute | solution.py:340
  4.6 6.5 %collective-permute-start.1 = (f32[8,4096]{1,0:T(8,128)}, f32[8,4096]{1,0:T(8,128)S(1)}, u32[]{:S(2)}, u32[]{:S(2)}) collective-permute-start(f32[8,4096]{1,0:T(8,128)} %t_ref.1), channel_id=1, source_target_pairs={{0,16},{8,24},{16,0},{24,8},{1,17},{9,25},{17,1},{25,9},{2,18},{10... | collective-permute-start | bytes 393224 | tf_op jit(solution)/shard_map/ppermute | solution.py:340
  6.4 4.3 collective-permute-start.3
  6.6 6.3 %collective-permute-start = (f32[8,2048]{1,0:T(8,128)S(1)}, f32[8,2048]{1,0:T(8,128)S(1)}, u32[]{:S(2)}, u32[]{:S(2)}) collective-permute-start(f32[8,2048]{1,0:T(8,128)S(1)} %get-tuple-element.27), channel_id=1, source_target_pairs={{0,8},{8,0},{16,24},{24,16},{1,9},{9,1},{17,25},{25,17},{2,10},{10... | collective-permute-start | bytes 196616 | tf_op jit(solution)/shard_map/ppermute | solution.py:340
  26.2 1.2 collective-permute-start.4
  27.5 5.0 collective-permute-start.7
  31.1 3.9 collective-permute-start.6
  31.1 3.9 collective-permute-start.5
  129.9 4.8 collective-permute-start.10
  131.7 3.7 collective-permute-start.9
  132.9 3.7 collective-permute-start.8
  266.1 1.2 collective-permute-start.11
  267.3 4.9 collective-permute-start.14
  268.7 4.0 collective-permute-start.13
  269.2 3.4 collective-permute-start.12
  367.5 4.7 collective-permute-start.17
  369.1 3.7 collective-permute-start.16
  369.6 3.7 collective-permute-start.15
  371.1 131.7 %copy-start = (f32[8,128]{1,0:T(8,128)}, f32[8,128]{1,0:T(8,128)S(1)}, u32[]{:S(2)}) copy-start(f32[8,128]{1,0:T(8,128)S(1)} %multiply_add_fusion.refs_12_) | copy-start | bytes 12292
  502.8 1.2 collective-permute-start.18
  504.1 4.8 collective-permute-start.21
  506.2 3.9 collective-permute-start.20
  507.1 3.1 collective-permute-start.19
